TPU v7x, 32 devices: a whole 2x2x4 slice. The times are simulated.
32 devices in a mesh: row: 8 (over z, x), col: 4 (over y, core).
Axes of the slice: x: 2, y: 2, z: 4, core: 2. Of those that a mesh axis runs over, the one named last changes fastest.
Arguments:
- amplitudes: bfloat16 [8192, 768], P(('row', 'col')), may hold values from -6 to 6
- integrals: bfloat16 [8192, 768], P(('row', 'col')), may hold values from -0.21875 to 0.21875
- block_mask: int32 [64, 64], P('row'), may hold values from 0 to 1, as said below
- occ_energy: float32 [8], replicated, may hold values from -1.5 to -0.5
- vir_energy: float32 [1024], replicated, may hold values from 0.1 to 1.5
Outputs:
- update: bfloat16 [8, 4, 32, 128, 128], P('row', 'col')
Inputs may be any that keep to these rules, and one draw needn't show every extreme that they name: block_mask is symmetric; among the 2 x 2 blocks (a, b) with the same a // 2 and b // 2 at most one is present, and for every a // 2 one block with b // 2 = a // 2 and b = a is present; for every cell (r, c) at most 32 of its blocks are present, with exactly 32 in some cell.
All inputs are finite; a program needn't handle non-finite values.
Results may differ from a plain program's by a relative error of at most 0.0049.
Values may be sent and summed in bfloat16 or wider, within the bound.
No kernel may reach another device: no remote copies, remote signals or barrier semaphores. Data moves between devices by JAX's collectives and lax.ppermute only.
A program may use at most 64 MiB of HBM per device.

v0:
```python
import functools

import jax
import jax.numpy as jnp
import numpy as np
from jax import lax
from jax.experimental import pallas as pl
from jax.experimental.pallas import tpu as pltpu
from jax.sharding import PartitionSpec as P

BLOCK = 128
SHARD_BLOCKS = 2
TILES = 192


def ring_order(count):
    short = 1
    while short * short * 4 <= count:
        short *= 2
    if count % short or (count // short) % 2 or short == 1:
        return list(range(count))
    tall = count // short
    walk = [z * short for z in range(tall)]
    for at, z in enumerate(reversed(range(tall))):
        xs = range(1, short) if at % 2 == 0 else reversed(range(1, short))
        walk += [z * short + x for x in xs]
    return walk


def table_kernel(ncol, nrow, split, where, source, mask, tab):
    cells = ncol * nrow
    row_at, col_at = where[0], where[1]
    for s in range(nrow):
        tab[3 * cells + s] = source[row_at * nrow + s]
    tab[3 * cells + nrow] = row_at
    tab[3 * cells + nrow + 1] = col_at

    def clear(at, carry):
        tab[at] = -1
        tab[cells + at] = 0
        tab[2 * cells + at] = 0
        return carry

    lax.fori_loop(0, cells, clear, 0)

    def rows(u, count):
        def cols(i, count):
            for trail in range(split):
                hit = mask[u, (i * ncol + col_at) * split + trail] > 0

                @pl.when(hit)
                def _():
                    at = lax.div(u, split) * nrow + i
                    tab[at] = count
                    tab[cells + at] = lax.rem(u, split)
                    tab[2 * cells + at] = trail

                count = count + hit.astype(jnp.int32)
            return count

        return lax.fori_loop(0, nrow, cols, count)

    lax.fori_loop(0, ncol * split, rows, jnp.int32(0))


def slot_table(where, source, mask, ncol, nrow, split):
    smem = pl.BlockSpec(memory_space=pltpu.SMEM)
    return pl.pallas_call(
        functools.partial(table_kernel, ncol, nrow, split),
        in_specs=[smem, smem, smem],
        out_specs=smem,
        out_shape=jax.ShapeDtypeStruct((3 * ncol * nrow + nrow + 2,), jnp.int32),
        name="slots",
    )(where, source, mask)


def step_kernel(hops, spots, ncol, nrow, split, tab, occ, vir, *refs):
    kept = 1 + max(n for at in spots.values() for n, _ in at)
    row_shards = refs[:kept]
    refs = refs[kept:]
    count = len(hops)
    rows = split * BLOCK
    amp_b, int_b = refs[:count], refs[count : 2 * count]
    _, out, tiles, sem = refs[2 * count :]
    cells = ncol * nrow
    row_at, col_at = tab[3 * cells + nrow], tab[3 * cells + nrow + 1]
    groups = vir.shape[0]
    nt = (((1,), (1,)), ((), ()))

    def half(index):
        return pl.ds(pl.multiple_of(index * BLOCK, BLOCK), BLOCK)

    def gap(block):
        return vir[pl.ds(lax.rem(block, groups), 1), :] - occ[lax.div(block, groups)]

    stores = []
    for n, s in enumerate(hops):
        i = tab[3 * cells + s]
        for m in range(ncol):
            j = jnp.bitwise_xor(col_at, m)
            at = j * nrow + i
            lead, trail = tab[cells + at], tab[2 * cells + at]
            a, b = half(lead), half(trail)
            amp_a, int_a = (row_shards[n_at].at[pl.ds(q * rows, rows)] for n_at, q in spots[m])
            direct = lax.dot_general(amp_a[a, :], int_b[n][b, :], nt, preferred_element_type=jnp.float32)
            mirror = lax.dot_general(int_a[a, :], amp_b[n][b, :], nt, preferred_element_type=jnp.float32)
            gap_a = gap((row_at * ncol + j) * split + lead)
            gap_b = gap((i * ncol + col_at) * split + trail)
            denom = jnp.broadcast_to(gap_a, (BLOCK, BLOCK)).T + gap_b
            total = direct.astype(jnp.bfloat16).astype(jnp.float32) + mirror.astype(jnp.bfloat16).astype(jnp.float32)
            tiles[n, m] = (total / denom).astype(jnp.bfloat16)
            slot = tab[at]
            stores.append((slot, pltpu.make_async_copy(tiles.at[n, m], out.at[jnp.maximum(slot, 0)], sem.at[n, m])))
    for slot, store in stores:
        pl.when(slot >= 0)(store.start)
    for slot, store in stores:
        pl.when(slot >= 0)(store.wait)


def step(hops, spots, tab, occ, vir, row_shards, amp_b, int_b, out, ncol, nrow, split):
    rows, width = amp_b[0].shape
    count = len(hops)
    smem = pl.BlockSpec(memory_space=pltpu.SMEM)
    vmem = pl.BlockSpec(memory_space=pltpu.VMEM)
    hbm = pl.BlockSpec(memory_space=pl.ANY)
    shard_count = len(row_shards) + 2 * count
    return pl.pallas_call(
        functools.partial(step_kernel, hops, spots, ncol, nrow, split),
        in_specs=[smem, smem, vmem] + [vmem] * shard_count + [hbm],
        out_specs=hbm,
        scratch_shapes=[
            pltpu.VMEM((count, ncol, BLOCK, BLOCK), jnp.bfloat16),
            pltpu.SemaphoreType.DMA((count, ncol)),
        ],
        out_shape=jax.ShapeDtypeStruct(out.shape, out.dtype),
        input_output_aliases={3 + shard_count: 0},
        compiler_params=pltpu.CompilerParams(vmem_limit_bytes=4 * (ncol + count) * rows * width + (4 << 20)),
        cost_estimate=pl.CostEstimate(
            flops=4 * count * ncol * BLOCK * BLOCK * width,
            bytes_accessed=4 * count * (ncol * BLOCK + rows) * width,
            transcendentals=0,
        ),
        name="blocks",
    )(tab, occ, vir, *row_shards, *amp_b, *int_b, out)


def gather_cols(amplitudes, integrals, ncol, held):
    arrays, spots = [amplitudes, integrals], {0: ((0, 0), (1, 0))}
    rows = amplitudes.shape[0]
    bit = ncol // 2
    while bit:
        pairs = [(c, c ^ bit) for c in range(ncol)]
        if len(arrays) == 2:
            spots[bit] = ((2, 0), (3, 0))
            arrays.append(lax.ppermute(amplitudes, "col", pairs))
            arrays.append(lax.ppermute(after(integrals, arrays[2]), "col", pairs))
        else:
            starts = np.cumsum([0] + [array.shape[0] // rows for array in arrays])
            moved = {m ^ bit: tuple((len(arrays), int(starts[n]) + q) for n, q in at) for m, at in spots.items()}
            spots.update(moved)
            arrays.append(lax.ppermute(after(jnp.concatenate(arrays), held), "col", pairs))
        bit //= 2
    return arrays, spots


def after(x, gate):
    return x if gate is None else lax.optimization_barrier((x, gate))[0]


def shards(amplitudes, integrals, block_mask, occ_energy, vir_energy):
    nrow = lax.axis_size("row")
    ncol = lax.axis_size("col")
    split = SHARD_BLOCKS
    limit = min(TILES, nrow * ncol)
    where = jnp.stack([lax.axis_index("row"), lax.axis_index("col")]).astype(jnp.int32)
    order = ring_order(nrow)
    spot = {row: at for at, row in enumerate(order)}
    source = np.array([order[(spot[row] - s) % nrow] for row in range(nrow) for s in range(nrow)], np.int32)
    ahead = [(order[p], order[(p + 1) % nrow]) for p in range(nrow)]
    behind = [(b, a) for a, b in ahead]
    tab = slot_table(where, source, block_mask, ncol, nrow, split)
    vir = vir_energy.reshape(-1, BLOCK)
    out = jnp.zeros((limit, BLOCK, BLOCK), jnp.bfloat16)

    def update(hops, amp_b, int_b, out):
        return step(hops, spots, tab, occ_energy, vir, row_shards, amp_b, int_b, out, ncol, nrow, split)

    far = nrow // 2
    amp_up = amp_down = amplitudes
    int_up = int_down = integrals
    outs = {}
    for s in range(1, far + 1):
        last = (amp_up, amp_down, int_up, int_down)
        gate = outs[s - 3] if s >= 4 else None
        amp_up = lax.ppermute(after(amp_up, gate), "row", ahead)
        int_down = lax.ppermute(after(int_down, gate), "row", behind)
        if s < nrow - s:
            int_up = lax.ppermute(after(int_up, gate), "row", ahead)
            amp_down = lax.ppermute(after(amp_down, gate), "row", behind)
        if s == min(2, far):
            row_shards, spots = gather_cols(amplitudes, integrals, ncol, (amp_up, int_down, int_up, amp_down))
            out = update((0,), (amplitudes,), (integrals,), out)
        if s >= 2:
            out = update((s - 1, nrow - s + 1), last[:2], last[2:], out)
            outs[s - 1] = out
    if far == nrow - far:
        out = update((far,), (amp_up,), (int_down,), out)
    else:
        out = update((far, nrow - far), (amp_up, amp_down), (int_up, int_down), out)
    return out[None, None]


def solution(mesh):
    in_specs = (P(("row", "col"), None), P(("row", "col"), None), P("row", None), P(), P())
    out_specs = P("row", "col", None, None, None)
    return jax.shard_map(shards, mesh=mesh, in_specs=in_specs, out_specs=out_specs, check_vma=False)
```

profile of v0, /device:TPU:0, one launch (start us, length us, event | category | flops | bytes accessed | tf_op | source)
XLA Modules:
  0.0 71.5 jit_solution(10027542084099088358)
XLA Ops:
  0.0 0.0 copy-start
  0.0 0.0 copy-start.1
  0.0 3.0 %collective-permute-start = (bf16[256,768]{1,0:T(8,128)(2,1)}, bf16[256,768]{1,0:T(8,128)(2,1)S(1)}, u32[]{:S(2)}, u32[]{:S(2)}) collective-permute-start(bf16[256,768]{1,0:T(8,128)(2,1)} %refs_0_.9), channel_id=1, source_target_pairs={{0,2},{1,3},{2,0},{3,1},{4,6},{5,7},{6,4},{7,5},{8,10},{9,11},{10,... | collective-permute-start | bytes 1179656 | tf_op jit(solution)/shard_map/ppermute | solution.py:155
  3.1 1.6 %collective-permute-start.2 = (bf16[256,768]{1,0:T(8,128)(2,1)}, bf16[256,768]{1,0:T(8,128)(2,1)S(1)}, u32[]{:S(2)}, u32[]{:S(2)}) collective-permute-start(bf16[256,768]{1,0:T(8,128)(2,1)} %refs_0_.9), channel_id=1, source_target_pairs={{0,8},{8,16},{16,24},{24,28},{28,20},{20,12},{12,4},{4,0},{1,9},{9... | collective-permute-start | bytes 1179656 | tf_op jit(solution)/shard_map/ppermute | solution.py:195
  4.6 0.4 collective-permute-start.4
  5.1 1.6 %collective-permute-start.6 = (bf16[256,768]{1,0:T(8,128)(2,1)}, bf16[256,768]{1,0:T(8,128)(2,1)S(1)}, u32[]{:S(2)}, u32[]{:S(2)}) collective-permute-start(bf16[256,768]{1,0:T(8,128)(2,1)} %refs_1_.9), channel_id=1, source_target_pairs={{0,8},{8,16},{16,24},{24,28},{28,20},{20,12},{12,4},{4,0},{1,9},{9... | collective-permute-start | bytes 1179656 | tf_op jit(solution)/shard_map/ppermute | solution.py:198
  6.7 0.4 collective-permute-start.8
  7.1 5.3 %collective-permute-done.refs_2_ = bf16[256,768]{1,0:T(8,128)(2,1)S(1)} collective-permute-done((bf16[256,768]{1,0:T(8,128)(2,1)}, bf16[256,768]{1,0:T(8,128)(2,1)S(1)}, u32[]{:S(2)}, u32[]{:S(2)}) %collective-permute-start) | collective-permute-done | bytes 393248 | tf_op jit(solution)/shard_map/ppermute | solution.py:155
  12.4 1.7 %collective-permute-start.1 = (bf16[256,768]{1,0:T(8,128)(2,1)}, bf16[256,768]{1,0:T(8,128)(2,1)S(1)}, u32[]{:S(2)}, u32[]{:S(2)}) collective-permute-start(bf16[256,768]{1,0:T(8,128)(2,1)} %refs_1_.9), channel_id=1, source_target_pairs={{0,2},{1,3},{2,0},{3,1},{4,6},{5,7},{6,4},{7,5},{8,10},{9,11},{10,... | collective-permute-start | bytes 1179656 | tf_op jit(solution)/shard_map/ppermute | solution.py:156
  14.1 1.2 %collective-permute-done.2.refs_5_ = bf16[256,768]{1,0:T(8,128)(2,1)S(1)} collective-permute-done((bf16[256,768]{1,0:T(8,128)(2,1)}, bf16[256,768]{1,0:T(8,128)(2,1)S(1)}, u32[]{:S(2)}, u32[]{:S(2)}) %collective-permute-start.2) | collective-permute-done | bytes 393248 | tf_op jit(solution)/shard_map/ppermute | solution.py:195
  15.3 1.6 %collective-permute-start.3 = (bf16[256,768]{1,0:T(8,128)(2,1)S(1)}, bf16[256,768]{1,0:T(8,128)(2,1)}, u32[]{:S(2)}, u32[]{:S(2)}) collective-permute-start(bf16[256,768]{1,0:T(8,128)(2,1)S(1)} %collective-permute-done.2.refs_5_), channel_id=1, source_target_pairs={{0,8},{8,16},{16,24},{24,28},{28,20},{20,12},{12,4},{4,0},{1,9},{9... | collective-permute-start | bytes 1179656 | tf_op jit(solution)/shard_map/ppermute | solution.py:195
  16.9 0.0 collective-permute-done.4.refs_8_
  16.9 0.4 collective-permute-start.5
  17.3 6.4 %collective-permute-done.6.refs_7_ = bf16[256,768]{1,0:T(8,128)(2,1)S(1)} collective-permute-done((bf16[256,768]{1,0:T(8,128)(2,1)}, bf16[256,768]{1,0:T(8,128)(2,1)S(1)}, u32[]{:S(2)}, u32[]{:S(2)}) %collective-permute-start.6) | collective-permute-done | bytes 393248 | tf_op jit(solution)/shard_map/ppermute | solution.py:198
  23.7 1.6 %collective-permute-start.7 = (bf16[256,768]{1,0:T(8,128)(2,1)S(1)}, bf16[256,768]{1,0:T(8,128)(2,1)S(1)}, u32[]{:S(2)}, u32[]{:S(2)}) collective-permute-start(bf16[256,768]{1,0:T(8,128)(2,1)S(1)} %collective-permute-done.6.refs_7_), channel_id=1, source_target_pairs={{0,8},{8,16},{16,24},{24,28},{28,20},{20,12},{12,4},{4,0},{1,9},{9... | collective-permute-start | bytes 1179656 | tf_op jit(solution)/shard_map/ppermute | solution.py:198
  25.3 0.0 collective-permute-done.8.refs_6_
  25.3 0.4 collective-permute-start.9
  25.8 0.0 collective-permute-done.1.refs_3_
  25.8 2.4 %pad_maximum_fusion = bf16[1024,768]{1,0:T(8,128)(2,1)} fusion(bf16[256,768]{1,0:T(8,128)(2,1)S(1)} %collective-permute-done.1.refs_3_, bf16[256,768]{1,0:T(8,128)(2,1)S(1)} %collective-permute-done.refs_2_, bf16[256,768]{1,0:T(8,128)(2,1)} %refs_1_.9, bf16[256,768]{1,0:T(8,128)(2,1)} %refs_0_.9), kind=kLoop, calls=%fused_computation | loop fusion | flops 6291456 | bytes 3145728 | tf_op jit(solution)/shard_map/concatenate | solution.py:161
  28.2 0.0 copy-done.2
  28.2 0.0 copy-done.4
  28.2 0.0 copy-done.6
  28.2 4.1 %collective-permute-done.3.refs_5_ = bf16[256,768]{1,0:T(8,128)(2,1)} collective-permute-done((bf16[256,768]{1,0:T(8,128)(2,1)S(1)}, bf16[256,768]{1,0:T(8,128)(2,1)}, u32[]{:S(2)}, u32[]{:S(2)}) %collective-permute-start.3) | collective-permute-done | bytes 393248 | tf_op jit(solution)/shard_map/ppermute | solution.py:195
  32.3 1.6 %collective-permute-done.5.refs_8_ = bf16[256,768]{1,0:T(8,128)(2,1)} collective-permute-done((bf16[256,768]{1,0:T(8,128)(2,1)S(1)}, bf16[256,768]{1,0:T(8,128)(2,1)}, u32[]{:S(2)}, u32[]{:S(2)}) %collective-permute-start.5) | collective-permute-done | bytes 393248 | tf_op jit(solution)/shard_map/ppermute | solution.py:196
  33.9 5.3 %collective-permute-done.7.refs_7_ = bf16[256,768]{1,0:T(8,128)(2,1)S(1)} collective-permute-done((bf16[256,768]{1,0:T(8,128)(2,1)S(1)}, bf16[256,768]{1,0:T(8,128)(2,1)S(1)}, u32[]{:S(2)}, u32[]{:S(2)}) %collective-permute-start.7) | collective-permute-done | bytes 393248 | tf_op jit(solution)/shard_map/ppermute | solution.py:198
  39.1 1.3 %collective-permute-done.9.refs_6_ = bf16[256,768]{1,0:T(8,128)(2,1)S(1)} collective-permute-done((bf16[256,768]{1,0:T(8,128)(2,1)S(1)}, bf16[256,768]{1,0:T(8,128)(2,1)S(1)}, u32[]{:S(2)}, u32[]{:S(2)}) %collective-permute-start.9) | collective-permute-done | bytes 393248 | tf_op jit(solution)/shard_map/ppermute | solution.py:199
  40.4 0.0 copy-done.8
  40.4 0.0 collective-permute-start.10
  40.4 0.7 %copy-done.10 = bf16[256,768]{1,0:T(8,128)(2,1)} copy-done((bf16[256,768]{1,0:T(8,128)(2,1)}, bf16[256,768]{1,0:T(8,128)(2,1)S(1)}, u32[]{:S(2)}) %copy-start.10) | copy-done | bytes 393240
  41.2 0.9 %collective-permute-start.13 = (bf16[256,768]{1,0:T(8,128)(2,1)}, bf16[256,768]{1,0:T(8,128)(2,1)}, u32[]{:S(2)}, u32[]{:S(2)}) collective-permute-start(bf16[256,768]{1,0:T(8,128)(2,1)} %collective-permute-done.5.refs_8_), channel_id=1, source_target_pairs={{8,0},{16,8},{24,16},{28,24},{20,28},{12,20},{4,12},{0,4},{9,1},{1... | collective-permute-start | bytes 1179656 | tf_op jit(solution)/shard_map/ppermute | solution.py:196
  42.1 1.1 %collective-permute-start.11 = (bf16[256,768]{1,0:T(8,128)(2,1)}, bf16[256,768]{1,0:T(8,128)(2,1)}, u32[]{:S(2)}, u32[]{:S(2)}) collective-permute-start(bf16[256,768]{1,0:T(8,128)(2,1)} %collective-permute-done.3.refs_5_), channel_id=1, source_target_pairs={{0,8},{8,16},{16,24},{24,28},{28,20},{20,12},{12,4},{4,0},{1,9},{9... | collective-permute-start | bytes 1179656 | tf_op jit(solution)/shard_map/ppermute | solution.py:195
  43.2 0.7 pad_add_fusion.where
  43.8 2.6 %slots.1.tab = s32[106]{0:T(128)} custom-call(s32[2]{0:T(128)} %pad_add_fusion.where, s32[64]{0:T(128)} %constant.13.clone.source, s32[8,64]{1,0:T(8,128)} %mask.1), custom_call_target="tpu_custom_call" | custom-call | tf_op jit(solution)/shard_map/slots/pallas_call | solution.py:68
  46.5 1.0 %collective-permute-start.15 = (bf16[256,768]{1,0:T(8,128)(2,1)}, bf16[256,768]{1,0:T(8,128)(2,1)S(1)}, u32[]{:S(2)}, u32[]{:S(2)}) collective-permute-start(bf16[256,768]{1,0:T(8,128)(2,1)} %copy-done.10), channel_id=1, source_target_pairs={{8,0},{16,8},{24,16},{28,24},{20,28},{12,20},{4,12},{0,4},{9,1},{1... | collective-permute-start | bytes 1179656 | tf_op jit(solution)/shard_map/ppermute | solution.py:199
  47.5 1.1 %collective-permute-start.16 = (bf16[256,768]{1,0:T(8,128)(2,1)}, bf16[256,768]{1,0:T(8,128)(2,1)S(1)}, u32[]{:S(2)}, u32[]{:S(2)}) collective-permute-start(bf16[256,768]{1,0:T(8,128)(2,1)} %copy-done.8), channel_id=1, source_target_pairs={{0,8},{8,16},{16,24},{24,28},{28,20},{20,12},{12,4},{4,0},{1,9},{9... | collective-permute-start | bytes 1179656 | tf_op jit(solution)/shard_map/ppermute | solution.py:198
  48.6 0.0 collective-permute-done.10.refs_4_
  48.6 1.2 %broadcast_in_dim.6.refs_7_ = bf16[32,128,128]{2,1,0:T(8,128)(2,1)} broadcast(bf16[]{:T(256)} %constant.12.clone.1), dimensions={} | broadcast | bytes 1048578 | tf_op jit(solution)/shard_map/broadcast_in_dim | solution.py:183
  49.8 0.0 copy-done
  49.8 0.0 copy-done.1
  49.8 0.0 copy-done.12
  49.8 0.0 copy-done.15
  49.8 0.0 copy-start.13
  49.8 0.6 copy-done.13
  50.4 1.8 %blocks.5.refs_9_ = bf16[32,128,128]{2,1,0:T(8,128)(2,1)} custom-call(s32[106]{0:T(128)S(1)} %copy-done.13, f32[8]{0:T(128)S(1)} %copy-done.15, f32[8,128]{1,0:T(8,128)S(1)} %bitcast.4, bf16[256,768]{1,0:T(8,128)(2,1)S(1)} %copy-done, bf16[256,768]{1,0:T(8,128)(2,1)S(1)} %copy-done.1, ...), custom_call_target="tpu_custom_call", output_to_operand_aliasing={{}: (10, {})} | custom-call | flops 201326592 | bytes 2359296 | tf_op jit(solution)/shard_map/blocks/pallas_call | solution.py:127
  52.2 0.0 copy-done.3
  52.2 0.0 copy-done.5
  52.3 0.0 copy-done.7
  52.3 0.0 copy-done.14
  52.3 0.0 copy-start.9
  52.3 0.0 copy-start.11
  52.3 2.3 %blocks.6.refs_9_ = bf16[32,128,128]{2,1,0:T(8,128)(2,1)} custom-call(s32[106]{0:T(128)S(1)} %copy-done.14, f32[8]{0:T(128)S(1)} %copy-done.15, f32[8,128]{1,0:T(8,128)S(1)} %bitcast.5, bf16[256,768]{1,0:T(8,128)(2,1)S(1)} %copy-done, bf16[256,768]{1,0:T(8,128)(2,1)S(1)} %copy-done.1, ...), custom_call_target="tpu_custom_call", output_to_operand_aliasing={{}: (12, {})} | custom-call | flops 402653184 | bytes 4718592 | tf_op jit(solution)/shard_map/blocks/pallas_call | solution.py:127
  54.6 0.0 collective-permute-done.13.refs_8_
  54.6 0.0 collective-permute-done.11.refs_5_
  54.6 1.4 %collective-permute-start.14 = (bf16[256,768]{1,0:T(8,128)(2,1)}, bf16[256,768]{1,0:T(8,128)(2,1)S(1)}, u32[]{:S(2)}, u32[]{:S(2)}) collective-permute-start(bf16[256,768]{1,0:T(8,128)(2,1)} %collective-permute-done.13.refs_8_), channel_id=1, source_target_pairs={{8,0},{16,8},{24,16},{28,24},{20,28},{12,20},{4,12},{0,4},{9,1},{1... | collective-permute-start | bytes 1179656 | tf_op jit(solution)/shard_map/ppermute | solution.py:196
  56.0 0.7 collective-permute-start.12
  56.7 0.0 copy-done.9
  56.7 0.0 copy-done.11
  56.7 2.9 %blocks.7.refs_9_ = bf16[32,128,128]{2,1,0:T(8,128)(2,1)} custom-call(s32[106]{0:T(128)S(1)} %copy-done.14, f32[8]{0:T(128)S(1)} %copy-done.15, f32[8,128]{1,0:T(8,128)S(1)} %bitcast.6, bf16[256,768]{1,0:T(8,128)(2,1)S(1)} %copy-done, bf16[256,768]{1,0:T(8,128)(2,1)S(1)} %copy-done.1, ...), custom_call_target="tpu_custom_call", output_to_operand_aliasing={{}: (12, {})} | custom-call | flops 402653184 | bytes 4718592 | tf_op jit(solution)/shard_map/blocks/pallas_call | solution.py:127
  59.6 2.2 %collective-permute-done.15.refs_6_ = bf16[256,768]{1,0:T(8,128)(2,1)S(1)} collective-permute-done((bf16[256,768]{1,0:T(8,128)(2,1)}, bf16[256,768]{1,0:T(8,128)(2,1)S(1)}, u32[]{:S(2)}, u32[]{:S(2)}) %collective-permute-start.15) | collective-permute-done | bytes 393248 | tf_op jit(solution)/shard_map/ppermute | solution.py:199
  61.8 1.0 %collective-permute-done.16.refs_7_ = bf16[256,768]{1,0:T(8,128)(2,1)S(1)} collective-permute-done((bf16[256,768]{1,0:T(8,128)(2,1)}, bf16[256,768]{1,0:T(8,128)(2,1)S(1)}, u32[]{:S(2)}, u32[]{:S(2)}) %collective-permute-start.16) | collective-permute-done | bytes 393248 | tf_op jit(solution)/shard_map/ppermute | solution.py:198
  62.8 2.9 %blocks.8.refs_7_ = bf16[32,128,128]{2,1,0:T(8,128)(2,1)} custom-call(s32[106]{0:T(128)S(1)} %copy-done.14, f32[8]{0:T(128)S(1)} %copy-done.15, f32[8,128]{1,0:T(8,128)S(1)} %bitcast.7, bf16[256,768]{1,0:T(8,128)(2,1)S(1)} %copy-done, bf16[256,768]{1,0:T(8,128)(2,1)S(1)} %copy-done.1, ...), custom_call_target="tpu_custom_call", output_to_operand_aliasing={{}: (12, {})} | custom-call | flops 402653184 | bytes 4718592 | tf_op jit(solution)/shard_map/blocks/pallas_call | solution.py:127
  65.7 3.3 %collective-permute-done.14.refs_6_ = bf16[256,768]{1,0:T(8,128)(2,1)S(1)} collective-permute-done((bf16[256,768]{1,0:T(8,128)(2,1)}, bf16[256,768]{1,0:T(8,128)(2,1)S(1)}, u32[]{:S(2)}, u32[]{:S(2)}) %collective-permute-start.14) | collective-permute-done | bytes 393248 | tf_op jit(solution)/shard_map/ppermute | solution.py:196
  69.0 0.7 collective-permute-done.12.refs_5_
  69.7 1.8 %blocks.9 = bf16[32,128,128]{2,1,0:T(8,128)(2,1)} custom-call(s32[106]{0:T(128)S(1)} %copy-done.14, f32[8]{0:T(128)S(1)} %copy-done.15, f32[8,128]{1,0:T(8,128)S(1)} %bitcast.8, bf16[256,768]{1,0:T(8,128)(2,1)S(1)} %copy-done, bf16[256,768]{1,0:T(8,128)(2,1)S(1)} %copy-done.1, ...), custom_call_target="tpu_custom_call", output_to_operand_aliasing={{}: (10, {})} | custom-call | flops 201326592 | bytes 2359296 | tf_op jit(solution)/shard_map/blocks/pallas_call | solution.py:127
  (11 shorter events, 0.0 us)
Async XLA Ops:
  0.0 49.8 %copy-start = (bf16[256,768]{1,0:T(8,128)(2,1)S(1)}, bf16[256,768]{1,0:T(8,128)(2,1)}, u32[]{:S(2)}) copy-start(bf16[256,768]{1,0:T(8,128)(2,1)} %refs_0_.9) | copy-start | bytes 1179652
  0.0 49.8 %copy-start.1 = (bf16[256,768]{1,0:T(8,128)(2,1)S(1)}, bf16[256,768]{1,0:T(8,128)(2,1)}, u32[]{:S(2)}) copy-start(bf16[256,768]{1,0:T(8,128)(2,1)} %refs_1_.9) | copy-start | bytes 1179652
  0.0 49.8 %copy-start.12 = (f32[1024]{0:T(1024)S(1)}, f32[1024]{0:T(1024)}, u32[]{:S(2)}) copy-start(f32[1024]{0:T(1024)} %param.10) | copy-start | bytes 12292
  0.0 49.8 %copy-start.15 = (f32[8]{0:T(128)S(1)}, f32[8]{0:T(128)}, u32[]{:S(2)}) copy-start(f32[8]{0:T(128)} %occ.9) | copy-start | bytes 100
  0.0 12.4 %collective-permute-start = (bf16[256,768]{1,0:T(8,128)(2,1)}, bf16[256,768]{1,0:T(8,128)(2,1)S(1)}, u32[]{:S(2)}, u32[]{:S(2)}) collective-permute-start(bf16[256,768]{1,0:T(8,128)(2,1)} %refs_0_.9), channel_id=1, source_target_pairs={{0,2},{1,3},{2,0},{3,1},{4,6},{5,7},{6,4},{7,5},{8,10},{9,11},{10,... | collective-permute-start | bytes 1179656 | tf_op jit(solution)/shard_map/ppermute | solution.py:155
  3.1 12.2 %collective-permute-start.2 = (bf16[256,768]{1,0:T(8,128)(2,1)}, bf16[256,768]{1,0:T(8,128)(2,1)S(1)}, u32[]{:S(2)}, u32[]{:S(2)}) collective-permute-start(bf16[256,768]{1,0:T(8,128)(2,1)} %refs_0_.9), channel_id=1, source_target_pairs={{0,8},{8,16},{16,24},{24,28},{28,20},{20,12},{12,4},{4,0},{1,9},{9... | collective-permute-start | bytes 1179656 | tf_op jit(solution)/shard_map/ppermute | solution.py:195
  4.6 12.3 %collective-permute-start.4 = (bf16[256,768]{1,0:T(8,128)(2,1)}, bf16[256,768]{1,0:T(8,128)(2,1)S(1)}, u32[]{:S(2)}, u32[]{:S(2)}) collective-permute-start(bf16[256,768]{1,0:T(8,128)(2,1)} %refs_1_.9), channel_id=1, source_target_pairs={{8,0},{16,8},{24,16},{28,24},{20,28},{12,20},{4,12},{0,4},{9,1},{1... | collective-permute-start | bytes 1179656 | tf_op jit(solution)/shard_map/ppermute | solution.py:196
  5.1 18.6 %collective-permute-start.6 = (bf16[256,768]{1,0:T(8,128)(2,1)}, bf16[256,768]{1,0:T(8,128)(2,1)S(1)}, u32[]{:S(2)}, u32[]{:S(2)}) collective-permute-start(bf16[256,768]{1,0:T(8,128)(2,1)} %refs_1_.9), channel_id=1, source_target_pairs={{0,8},{8,16},{16,24},{24,28},{28,20},{20,12},{12,4},{4,0},{1,9},{9... | collective-permute-start | bytes 1179656 | tf_op jit(solution)/shard_map/ppermute | solution.py:198
  6.7 18.7 %collective-permute-start.8 = (bf16[256,768]{1,0:T(8,128)(2,1)}, bf16[256,768]{1,0:T(8,128)(2,1)S(1)}, u32[]{:S(2)}, u32[]{:S(2)}) collective-permute-start(bf16[256,768]{1,0:T(8,128)(2,1)} %refs_0_.9), channel_id=1, source_target_pairs={{8,0},{16,8},{24,16},{28,24},{20,28},{12,20},{4,12},{0,4},{9,1},{1... | collective-permute-start | bytes 1179656 | tf_op jit(solution)/shard_map/ppermute | solution.py:199
  12.4 13.4 %collective-permute-start.1 = (bf16[256,768]{1,0:T(8,128)(2,1)}, bf16[256,768]{1,0:T(8,128)(2,1)S(1)}, u32[]{:S(2)}, u32[]{:S(2)}) collective-permute-start(bf16[256,768]{1,0:T(8,128)(2,1)} %refs_1_.9), channel_id=1, source_target_pairs={{0,2},{1,3},{2,0},{3,1},{4,6},{5,7},{6,4},{7,5},{8,10},{9,11},{10,... | collective-permute-start | bytes 1179656 | tf_op jit(solution)/shard_map/ppermute | solution.py:156
  15.3 17.0 %collective-permute-start.3 = (bf16[256,768]{1,0:T(8,128)(2,1)S(1)}, bf16[256,768]{1,0:T(8,128)(2,1)}, u32[]{:S(2)}, u32[]{:S(2)}) collective-permute-start(bf16[256,768]{1,0:T(8,128)(2,1)S(1)} %collective-permute-done.2.refs_5_), channel_id=1, source_target_pairs={{0,8},{8,16},{16,24},{24,28},{28,20},{20,12},{12,4},{4,0},{1,9},{9... | collective-permute-start | bytes 1179656 | tf_op jit(solution)/shard_map/ppermute | solution.py:195
  16.9 11.3 %copy-start.2 = (bf16[256,768]{1,0:T(8,128)(2,1)}, bf16[256,768]{1,0:T(8,128)(2,1)S(1)}, u32[]{:S(2)}) copy-start(bf16[256,768]{1,0:T(8,128)(2,1)S(1)} %collective-permute-done.4.refs_8_) | copy-start | bytes 1179652
  16.9 17.0 %collective-permute-start.5 = (bf16[256,768]{1,0:T(8,128)(2,1)S(1)}, bf16[256,768]{1,0:T(8,128)(2,1)}, u32[]{:S(2)}, u32[]{:S(2)}) collective-permute-start(bf16[256,768]{1,0:T(8,128)(2,1)S(1)} %collective-permute-done.4.refs_8_), channel_id=1, source_target_pairs={{8,0},{16,8},{24,16},{28,24},{20,28},{12,20},{4,12},{0,4},{9,1},{1... | collective-permute-start | bytes 1179656 | tf_op jit(solution)/shard_map/ppermute | solution.py:196
  23.7 4.5 %copy-start.4 = (bf16[256,768]{1,0:T(8,128)(2,1)}, bf16[256,768]{1,0:T(8,128)(2,1)S(1)}, u32[]{:S(2)}) copy-start(bf16[256,768]{1,0:T(8,128)(2,1)S(1)} %collective-permute-done.6.refs_7_) | copy-start | bytes 1179652
  23.7 15.4 %collective-permute-start.7 = (bf16[256,768]{1,0:T(8,128)(2,1)S(1)}, bf16[256,768]{1,0:T(8,128)(2,1)S(1)}, u32[]{:S(2)}, u32[]{:S(2)}) collective-permute-start(bf16[256,768]{1,0:T(8,128)(2,1)S(1)} %collective-permute-done.6.refs_7_), channel_id=1, source_target_pairs={{0,8},{8,16},{16,24},{24,28},{28,20},{20,12},{12,4},{4,0},{1,9},{9... | collective-permute-start | bytes 1179656 | tf_op jit(solution)/shard_map/ppermute | solution.py:198
  25.3 2.9 %copy-start.6 = (bf16[256,768]{1,0:T(8,128)(2,1)}, bf16[256,768]{1,0:T(8,128)(2,1)S(1)}, u32[]{:S(2)}) copy-start(bf16[256,768]{1,0:T(8,128)(2,1)S(1)} %collective-permute-done.8.refs_6_) | copy-start | bytes 1179652
  25.3 15.1 %collective-permute-start.9 = (bf16[256,768]{1,0:T(8,128)(2,1)S(1)}, bf16[256,768]{1,0:T(8,128)(2,1)S(1)}, u32[]{:S(2)}, u32[]{:S(2)}) collective-permute-start(bf16[256,768]{1,0:T(8,128)(2,1)S(1)} %collective-permute-done.8.refs_6_), channel_id=1, source_target_pairs={{8,0},{16,8},{24,16},{28,24},{20,28},{12,20},{4,12},{0,4},{9,1},{1... | collective-permute-start | bytes 1179656 | tf_op jit(solution)/shard_map/ppermute | solution.py:199
  39.1 1.3 %copy-start.8 = (bf16[256,768]{1,0:T(8,128)(2,1)}, bf16[256,768]{1,0:T(8,128)(2,1)S(1)}, u32[]{:S(2)}) copy-start(bf16[256,768]{1,0:T(8,128)(2,1)S(1)} %collective-permute-done.7.refs_7_) | copy-start | bytes 1179652
  40.4 0.7 %copy-start.10 = (bf16[256,768]{1,0:T(8,128)(2,1)}, bf16[256,768]{1,0:T(8,128)(2,1)S(1)}, u32[]{:S(2)}) copy-start(bf16[256,768]{1,0:T(8,128)(2,1)S(1)} %collective-permute-done.9.refs_6_) | copy-start | bytes 1179652
  40.4 8.2 %collective-permute-start.10 = (bf16[1024,768]{1,0:T(8,128)(2,1)}, bf16[1024,768]{1,0:T(8,128)(2,1)S(1)}, u32[]{:S(2)}, u32[]{:S(2)}) collective-permute-start(bf16[1024,768]{1,0:T(8,128)(2,1)} %pad_maximum_fusion), channel_id=1, source_target_pairs={{0,1},{1,0},{2,3},{3,2},{4,5},{5,4},{6,7},{7,6},{8,9},{9,8},{10,11... | collective-permute-start | bytes 4718600 | tf_op jit(solution)/shard_map/ppermute | solution.py:161
  41.2 13.4 %collective-permute-start.13 = (bf16[256,768]{1,0:T(8,128)(2,1)}, bf16[256,768]{1,0:T(8,128)(2,1)}, u32[]{:S(2)}, u32[]{:S(2)}) collective-permute-start(bf16[256,768]{1,0:T(8,128)(2,1)} %collective-permute-done.5.refs_8_), channel_id=1, source_target_pairs={{8,0},{16,8},{24,16},{28,24},{20,28},{12,20},{4,12},{0,4},{9,1},{1... | collective-permute-start | bytes 1179656 | tf_op jit(solution)/shard_map/ppermute | solution.py:196
  42.1 12.5 %collective-permute-start.11 = (bf16[256,768]{1,0:T(8,128)(2,1)}, bf16[256,768]{1,0:T(8,128)(2,1)}, u32[]{:S(2)}, u32[]{:S(2)}) collective-permute-start(bf16[256,768]{1,0:T(8,128)(2,1)} %collective-permute-done.3.refs_5_), channel_id=1, source_target_pairs={{0,8},{8,16},{16,24},{24,28},{28,20},{20,12},{12,4},{4,0},{1,9},{9... | collective-permute-start | bytes 1179656 | tf_op jit(solution)/shard_map/ppermute | solution.py:195
  46.5 15.3 %collective-permute-start.15 = (bf16[256,768]{1,0:T(8,128)(2,1)}, bf16[256,768]{1,0:T(8,128)(2,1)S(1)}, u32[]{:S(2)}, u32[]{:S(2)}) collective-permute-start(bf16[256,768]{1,0:T(8,128)(2,1)} %copy-done.10), channel_id=1, source_target_pairs={{8,0},{16,8},{24,16},{28,24},{20,28},{12,20},{4,12},{0,4},{9,1},{1... | collective-permute-start | bytes 1179656 | tf_op jit(solution)/shard_map/ppermute | solution.py:199
  47.5 15.3 %collective-permute-start.16 = (bf16[256,768]{1,0:T(8,128)(2,1)}, bf16[256,768]{1,0:T(8,128)(2,1)S(1)}, u32[]{:S(2)}, u32[]{:S(2)}) collective-permute-start(bf16[256,768]{1,0:T(8,128)(2,1)} %copy-done.8), channel_id=1, source_target_pairs={{0,8},{8,16},{16,24},{24,28},{28,20},{20,12},{12,4},{4,0},{1,9},{9... | collective-permute-start | bytes 1179656 | tf_op jit(solution)/shard_map/ppermute | solution.py:198
  49.8 0.6 copy-start.13
  50.4 1.8 %copy-start.3 = (bf16[256,768]{1,0:T(8,128)(2,1)S(1)}, bf16[256,768]{1,0:T(8,128)(2,1)}, u32[]{:S(2)}) copy-start(bf16[256,768]{1,0:T(8,128)(2,1)} %copy-done.2) | copy-start | bytes 1179652
  50.4 1.8 %copy-start.5 = (bf16[256,768]{1,0:T(8,128)(2,1)S(1)}, bf16[256,768]{1,0:T(8,128)(2,1)}, u32[]{:S(2)}) copy-start(bf16[256,768]{1,0:T(8,128)(2,1)} %copy-done.4) | copy-start | bytes 1179652
  50.4 1.9 %copy-start.7 = (bf16[256,768]{1,0:T(8,128)(2,1)S(1)}, bf16[256,768]{1,0:T(8,128)(2,1)}, u32[]{:S(2)}) copy-start(bf16[256,768]{1,0:T(8,128)(2,1)} %copy-done.6) | copy-start | bytes 1179652
  50.4 1.9 %copy-start.14 = (s32[106]{0:T(128)S(1)}, s32[106]{0:T(128)}, u32[]{:S(2)}) copy-start(s32[106]{0:T(128)} %slots.1.tab) | copy-start | bytes 1276
  52.3 4.4 %copy-start.9 = (bf16[256,768]{1,0:T(8,128)(2,1)S(1)}, bf16[256,768]{1,0:T(8,128)(2,1)}, u32[]{:S(2)}) copy-start(bf16[256,768]{1,0:T(8,128)(2,1)} %copy-done.8) | copy-start | bytes 1179652
  52.3 4.4 %copy-start.11 = (bf16[256,768]{1,0:T(8,128)(2,1)S(1)}, bf16[256,768]{1,0:T(8,128)(2,1)}, u32[]{:S(2)}) copy-start(bf16[256,768]{1,0:T(8,128)(2,1)} %copy-done.10) | copy-start | bytes 1179652
  54.6 14.4 %collective-permute-start.14 = (bf16[256,768]{1,0:T(8,128)(2,1)}, bf16[256,768]{1,0:T(8,128)(2,1)S(1)}, u32[]{:S(2)}, u32[]{:S(2)}) collective-permute-start(bf16[256,768]{1,0:T(8,128)(2,1)} %collective-permute-done.13.refs_8_), channel_id=1, source_target_pairs={{8,0},{16,8},{24,16},{28,24},{20,28},{12,20},{4,12},{0,4},{9,1},{1... | collective-permute-start | bytes 1179656 | tf_op jit(solution)/shard_map/ppermute | solution.py:196
  56.0 13.6 %collective-permute-start.12 = (bf16[256,768]{1,0:T(8,128)(2,1)}, bf16[256,768]{1,0:T(8,128)(2,1)S(1)}, u32[]{:S(2)}, u32[]{:S(2)}) collective-permute-start(bf16[256,768]{1,0:T(8,128)(2,1)} %collective-permute-done.11.refs_5_), channel_id=1, source_target_pairs={{0,8},{8,16},{16,24},{24,28},{28,20},{20,12},{12,4},{4,0},{1,9},{9... | collective-permute-start | bytes 1179656 | tf_op jit(solution)/shard_map/ppermute | solution.py:195
where the time goes:
time: 71.7 us; the launch traced here: 71.5 us
  waiting for transfers between devices  32.3 us (45%)
  starting transfers between devices  19.1 us (27%)
  Pallas kernels  14.4 us (20%)
  other arithmetic  3.07 us (4%)
  local copies, waits for them, and re-layouts  2.59 us (4%)
    ppermute x3, waiting for transfers between devices, shards(): int_up = lax.ppermute(after(int_up, gate), 'row', ahead)  12.6 us
    pallas_call x5, Pallas kernels, step(): pl.pallas_call(functools.partial(step_kernel, hops, spots, ncol, nrow, sp...  11.7 us
    ppermute x4, waiting for transfers between devices, shards(): amp_up = lax.ppermute(after(amp_up, gate), 'row', ahead)  5.91 us
    ppermute x1, waiting for transfers between devices, gather_cols(): arrays.append(lax.ppermute(amplitudes, 'col', pairs))  5.27 us
    ppermute x4, waiting for transfers between devices, shards(): int_down = lax.ppermute(after(int_down, gate), 'row', behind)  4.95 us
    ppermute x4, starting transfers between devices, shards(): amp_up = lax.ppermute(after(amp_up, gate), 'row', ahead)  4.89 us
    ppermute x3, starting transfers between devices, shards(): int_up = lax.ppermute(after(int_up, gate), 'row', ahead)  4.24 us
    ppermute x3, waiting for transfers between devices, shards(): amp_down = lax.ppermute(after(amp_down, gate), 'row', behind)  3.51 us
  transfers between devices with their start and end apart: 17, of which 11 were waited for; matrix products, arithmetic and copies ran while one was open for 6% of the time, Pallas kernels for 18%

commit v1 on v0

--- a/solution.py
+++ b/solution.py
@@ -188,21 +188,20 @@
     far = nrow // 2
     amp_up = amp_down = amplitudes
     int_up = int_down = integrals
-    outs = {}
     for s in range(1, far + 1):
         last = (amp_up, amp_down, int_up, int_down)
-        gate = outs[s - 3] if s >= 4 else None
-        amp_up = lax.ppermute(after(amp_up, gate), "row", ahead)
-        int_down = lax.ppermute(after(int_down, gate), "row", behind)
+        amp_up = lax.ppermute(amp_up, "row", ahead)
+        int_down = lax.ppermute(int_down, "row", behind)
         if s < nrow - s:
-            int_up = lax.ppermute(after(int_up, gate), "row", ahead)
-            amp_down = lax.ppermute(after(amp_down, gate), "row", behind)
-        if s == min(2, far):
-            row_shards, spots = gather_cols(amplitudes, integrals, ncol, (amp_up, int_down, int_up, amp_down))
+            int_up = lax.ppermute(int_up, "row", ahead)
+            amp_down = lax.ppermute(amp_down, "row", behind)
+        if s == min(3, far):
+            row_shards, spots = gather_cols(amplitudes, integrals, ncol, (amp_up, int_down, *last))
             out = update((0,), (amplitudes,), (integrals,), out)
-        if s >= 2:
+            out = update((1, nrow - 1), before[:2], before[2:], out)
+        if s >= 3:
             out = update((s - 1, nrow - s + 1), last[:2], last[2:], out)
-            outs[s - 1] = out
+        before = last
     if far == nrow - far:
         out = update((far,), (amp_up,), (int_down,), out)
     else:

time: 71.7 us -> 70.6 us (0.985)
  waiting for transfers between devices: 32.3 us -> 29.6 us
  Pallas kernels: 14.4 us -> 15.2 us
    ppermute x1, waiting for transfers between devices: 5.27 us -> 0.01 us  [gather_cols(): arrays.append(lax.ppermute(amplitudes, 'col', pairs))]
    ppermute x14, waiting for transfers between devices: 27 us -> 29.6 us  [the longest x4 18.5 us: shards(): amp_up = lax.ppermute(amp_up, 'row', ahead)]
    ppermute x14, starting transfers between devices: 14.3 us -> 15.6 us  [the longest x4 8.95 us: shards(): amp_up = lax.ppermute(amp_up, 'row', ahead)]
    ppermute x1, starting transfers between devices: 3.04 us -> 1.97 us  [gather_cols(): arrays.append(lax.ppermute(amplitudes, 'col', pairs))]
    pallas_call x5, Pallas kernels: 11.7 us -> 12.6 us  [step(): pl.pallas_call(functools.partial(step_kernel, hops, spots, ncol, nrow, sp...]
  transfers between devices with their start and end apart: 17 -> 17, of which waited for: 11 -> 8; matrix products, arithmetic and copies ran while one was open for 6% -> 6% of each run, Pallas kernels for 18% -> 18%
where the time goes in v1:
time: 70.6 us; the launch traced here: 70.4 us
  waiting for transfers between devices  29.6 us (42%)
  starting transfers between devices  19.5 us (28%)
  Pallas kernels  15.2 us (22%)
  other arithmetic  3.17 us (4%)
  local copies, waits for them, and re-layouts  2.69 us (4%)
    ppermute x4, waiting for transfers between devices, shards(): amp_up = lax.ppermute(amp_up, 'row', ahead)  18.5 us
    pallas_call x5, Pallas kernels, step(): pl.pallas_call(functools.partial(step_kernel, hops, spots, ncol, nrow, sp...  12.6 us
    ppermute x4, starting transfers between devices, shards(): amp_up = lax.ppermute(amp_up, 'row', ahead)  8.95 us
    ppermute x3, waiting for transfers between devices, shards(): int_up = lax.ppermute(int_up, 'row', ahead)  7.26 us
    ppermute x3, starting transfers between devices, shards(): int_up = lax.ppermute(int_up, 'row', ahead)  5.46 us
    pallas_call x1, Pallas kernels, slot_table(): pl.pallas_call(functools.partial(table_kernel, ncol, nrow, split), in_spe...  2.64 us
    concatenate x1, other arithmetic, gather_cols(): jnp.concatenate(arrays)  2.55 us
    ppermute x3, waiting for transfers between devices, shards(): amp_down = lax.ppermute(amp_down, 'row', behind)  2.22 us
  transfers between devices with their start and end apart: 17, of which 8 were waited for; matrix products, arithmetic and copies ran while one was open for 6% of the time, Pallas kernels for 18%

profile of v1, /device:TPU:0, one launch (start us, length us, event | category | flops | bytes accessed | tf_op | source)
XLA Modules:
  0.0 70.4 jit_solution(16562263301449024648)
XLA Ops:
  0.0 0.0 copy-start
  0.0 0.0 copy-start.1
  0.0 3.1 %collective-permute-start.2 = (bf16[256,768]{1,0:T(8,128)(2,1)}, bf16[256,768]{1,0:T(8,128)(2,1)S(1)}, u32[]{:S(2)}, u32[]{:S(2)}) collective-permute-start(bf16[256,768]{1,0:T(8,128)(2,1)} %refs_0_.9), channel_id=1, source_target_pairs={{0,8},{8,16},{16,24},{24,28},{28,20},{20,12},{12,4},{4,0},{1,9},{9... | collective-permute-start | bytes 1179656 | tf_op jit(solution)/shard_map/ppermute | solution.py:193
  3.1 0.0 collective-permute-start.5
  3.1 2.0 %collective-permute-start = (bf16[256,768]{1,0:T(8,128)(2,1)}, bf16[256,768]{1,0:T(8,128)(2,1)S(1)}, u32[]{:S(2)}, u32[]{:S(2)}) collective-permute-start(bf16[256,768]{1,0:T(8,128)(2,1)} %refs_0_.9), channel_id=1, source_target_pairs={{0,2},{1,3},{2,0},{3,1},{4,6},{5,7},{6,4},{7,5},{8,10},{9,11},{10,... | collective-permute-start | bytes 1179656 | tf_op jit(solution)/shard_map/ppermute | solution.py:155
  5.1 1.6 %collective-permute-start.10 = (bf16[256,768]{1,0:T(8,128)(2,1)}, bf16[256,768]{1,0:T(8,128)(2,1)S(1)}, u32[]{:S(2)}, u32[]{:S(2)}) collective-permute-start(bf16[256,768]{1,0:T(8,128)(2,1)} %refs_1_.9), channel_id=1, source_target_pairs={{0,8},{8,16},{16,24},{24,28},{28,20},{20,12},{12,4},{4,0},{1,9},{9... | collective-permute-start | bytes 1179656 | tf_op jit(solution)/shard_map/ppermute | solution.py:196
  6.6 0.4 collective-permute-start.8
  7.1 6.1 %collective-permute-done.2.refs_5_ = bf16[256,768]{1,0:T(8,128)(2,1)S(1)} collective-permute-done((bf16[256,768]{1,0:T(8,128)(2,1)}, bf16[256,768]{1,0:T(8,128)(2,1)S(1)}, u32[]{:S(2)}, u32[]{:S(2)}) %collective-permute-start.2) | collective-permute-done | bytes 393248 | tf_op jit(solution)/shard_map/ppermute | solution.py:193
  13.2 2.1 %collective-permute-start.3 = (bf16[256,768]{1,0:T(8,128)(2,1)S(1)}, bf16[256,768]{1,0:T(8,128)(2,1)S(1)}, u32[]{:S(2)}, u32[]{:S(2)}) collective-permute-start(bf16[256,768]{1,0:T(8,128)(2,1)S(1)} %collective-permute-done.2.refs_5_), channel_id=1, source_target_pairs={{0,8},{8,16},{16,24},{24,28},{28,20},{20,12},{12,4},{4,0},{1,9},{9... | collective-permute-start | bytes 1179656 | tf_op jit(solution)/shard_map/ppermute | solution.py:193
  15.3 0.0 collective-permute-done.5.refs_8_
  15.3 0.0 collective-permute-start.6
  15.4 0.8 %copy-done.2 = bf16[256,768]{1,0:T(8,128)(2,1)} copy-done((bf16[256,768]{1,0:T(8,128)(2,1)}, bf16[256,768]{1,0:T(8,128)(2,1)S(1)}, u32[]{:S(2)}) %copy-start.2) | copy-done | bytes 393240
  16.1 0.0 collective-permute-done.refs_2_
  16.1 2.0 %collective-permute-start.1 = (bf16[256,768]{1,0:T(8,128)(2,1)}, bf16[256,768]{1,0:T(8,128)(2,1)S(1)}, u32[]{:S(2)}, u32[]{:S(2)}) collective-permute-start(bf16[256,768]{1,0:T(8,128)(2,1)} %refs_1_.9), channel_id=1, source_target_pairs={{0,2},{1,3},{2,0},{3,1},{4,6},{5,7},{6,4},{7,5},{8,10},{9,11},{10,... | collective-permute-start | bytes 1179656 | tf_op jit(solution)/shard_map/ppermute | solution.py:156
  18.1 3.5 %collective-permute-done.10.refs_7_ = bf16[256,768]{1,0:T(8,128)(2,1)S(1)} collective-permute-done((bf16[256,768]{1,0:T(8,128)(2,1)}, bf16[256,768]{1,0:T(8,128)(2,1)S(1)}, u32[]{:S(2)}, u32[]{:S(2)}) %collective-permute-start.10) | collective-permute-done | bytes 393248 | tf_op jit(solution)/shard_map/ppermute | solution.py:196
  21.6 2.1 %collective-permute-start.11 = (bf16[256,768]{1,0:T(8,128)(2,1)S(1)}, bf16[256,768]{1,0:T(8,128)(2,1)}, u32[]{:S(2)}, u32[]{:S(2)}) collective-permute-start(bf16[256,768]{1,0:T(8,128)(2,1)S(1)} %collective-permute-done.10.refs_7_), channel_id=1, source_target_pairs={{0,8},{8,16},{16,24},{24,28},{28,20},{20,12},{12,4},{4,0},{1,9},{9... | collective-permute-start | bytes 1179656 | tf_op jit(solution)/shard_map/ppermute | solution.py:196
  23.7 0.0 collective-permute-done.8.refs_6_
  23.8 0.0 collective-permute-start.9
  23.8 6.2 %collective-permute-done.3.refs_5_ = bf16[256,768]{1,0:T(8,128)(2,1)S(1)} collective-permute-done((bf16[256,768]{1,0:T(8,128)(2,1)S(1)}, bf16[256,768]{1,0:T(8,128)(2,1)S(1)}, u32[]{:S(2)}, u32[]{:S(2)}) %collective-permute-start.3) | collective-permute-done | bytes 393248 | tf_op jit(solution)/shard_map/ppermute | solution.py:193
  30.0 2.1 %collective-permute-start.4 = (bf16[256,768]{1,0:T(8,128)(2,1)S(1)}, bf16[256,768]{1,0:T(8,128)(2,1)}, u32[]{:S(2)}, u32[]{:S(2)}) collective-permute-start(bf16[256,768]{1,0:T(8,128)(2,1)S(1)} %collective-permute-done.3.refs_5_), channel_id=1, source_target_pairs={{0,8},{8,16},{16,24},{24,28},{28,20},{20,12},{12,4},{4,0},{1,9},{9... | collective-permute-start | bytes 1179656 | tf_op jit(solution)/shard_map/ppermute | solution.py:193
  32.2 0.0 collective-permute-done.6.refs_8_
  32.2 0.0 collective-permute-start.7
  32.2 0.0 collective-permute-done.1.refs_3_
  32.2 2.5 %pad_maximum_fusion = bf16[1024,768]{1,0:T(8,128)(2,1)} fusion(bf16[256,768]{1,0:T(8,128)(2,1)S(1)} %collective-permute-done.1.refs_3_, bf16[256,768]{1,0:T(8,128)(2,1)S(1)} %collective-permute-done.refs_2_, bf16[256,768]{1,0:T(8,128)(2,1)} %refs_1_.9, bf16[256,768]{1,0:T(8,128)(2,1)} %refs_0_.9), kind=kLoop, calls=%fused_computation | loop fusion | flops 6291456 | bytes 3145728 | tf_op jit(solution)/shard_map/concatenate | solution.py:161
  34.8 0.0 copy-done.4
  34.8 0.0 copy-done.6
  34.8 0.0 copy-done.8
  34.8 0.0 copy-done.10
  34.8 3.8 %collective-permute-done.11.refs_7_ = bf16[256,768]{1,0:T(8,128)(2,1)} collective-permute-done((bf16[256,768]{1,0:T(8,128)(2,1)S(1)}, bf16[256,768]{1,0:T(8,128)(2,1)}, u32[]{:S(2)}, u32[]{:S(2)}) %collective-permute-start.11) | collective-permute-done | bytes 393248 | tf_op jit(solution)/shard_map/ppermute | solution.py:196
  38.5 2.2 %collective-permute-done.9.refs_6_ = bf16[256,768]{1,0:T(8,128)(2,1)} collective-permute-done((bf16[256,768]{1,0:T(8,128)(2,1)S(1)}, bf16[256,768]{1,0:T(8,128)(2,1)}, u32[]{:S(2)}, u32[]{:S(2)}) %collective-permute-start.9) | collective-permute-done | bytes 393248 | tf_op jit(solution)/shard_map/ppermute | solution.py:197
  40.7 5.4 %collective-permute-done.4.refs_5_ = bf16[256,768]{1,0:T(8,128)(2,1)} collective-permute-done((bf16[256,768]{1,0:T(8,128)(2,1)S(1)}, bf16[256,768]{1,0:T(8,128)(2,1)}, u32[]{:S(2)}, u32[]{:S(2)}) %collective-permute-start.4) | collective-permute-done | bytes 393248 | tf_op jit(solution)/shard_map/ppermute | solution.py:193
  46.1 1.5 %collective-permute-done.7.refs_8_ = bf16[256,768]{1,0:T(8,128)(2,1)} collective-permute-done((bf16[256,768]{1,0:T(8,128)(2,1)S(1)}, bf16[256,768]{1,0:T(8,128)(2,1)}, u32[]{:S(2)}, u32[]{:S(2)}) %collective-permute-start.7) | collective-permute-done | bytes 393248 | tf_op jit(solution)/shard_map/ppermute | solution.py:194
  47.7 0.0 collective-permute-start.12
  47.7 0.3 collective-permute-start.15
  48.0 1.7 %collective-permute-start.16 = (bf16[256,768]{1,0:T(8,128)(2,1)}, bf16[256,768]{1,0:T(8,128)(2,1)}, u32[]{:S(2)}, u32[]{:S(2)}) collective-permute-start(bf16[256,768]{1,0:T(8,128)(2,1)} %collective-permute-done.11.refs_7_), channel_id=1, source_target_pairs={{0,8},{8,16},{16,24},{24,28},{28,20},{20,12},{12,4},{4,0},{1,9},{9... | collective-permute-start | bytes 1179656 | tf_op jit(solution)/shard_map/ppermute | solution.py:196
  49.7 1.6 %collective-permute-start.13 = (bf16[256,768]{1,0:T(8,128)(2,1)}, bf16[256,768]{1,0:T(8,128)(2,1)}, u32[]{:S(2)}, u32[]{:S(2)}) collective-permute-start(bf16[256,768]{1,0:T(8,128)(2,1)} %collective-permute-done.4.refs_5_), channel_id=1, source_target_pairs={{0,8},{8,16},{16,24},{24,28},{28,20},{20,12},{12,4},{4,0},{1,9},{9... | collective-permute-start | bytes 1179656 | tf_op jit(solution)/shard_map/ppermute | solution.py:193
  51.3 0.4 collective-permute-start.14
  51.8 0.6 pad_add_fusion.where
  52.4 2.6 %slots.1.tab = s32[106]{0:T(128)} custom-call(s32[2]{0:T(128)} %pad_add_fusion.where, s32[64]{0:T(128)} %constant.13.clone.source, s32[8,64]{1,0:T(8,128)} %mask.1), custom_call_target="tpu_custom_call" | custom-call | tf_op jit(solution)/shard_map/slots/pallas_call | solution.py:68
  55.0 0.0 collective-permute-done.12.refs_4_
  55.0 1.2 %broadcast_in_dim.6.refs_7_ = bf16[32,128,128]{2,1,0:T(8,128)(2,1)} broadcast(bf16[]{:T(256)} %constant.12.clone.1), dimensions={} | broadcast | bytes 1048578 | tf_op jit(solution)/shard_map/broadcast_in_dim | solution.py:183
  56.2 0.0 copy-done
  56.2 0.0 copy-done.1
  56.2 0.0 copy-done.12
  56.2 0.0 copy-done.15
  56.3 0.0 copy-start.13
  56.3 0.7 copy-done.13
  56.9 1.8 %blocks.5.refs_9_ = bf16[32,128,128]{2,1,0:T(8,128)(2,1)} custom-call(s32[106]{0:T(128)S(1)} %copy-done.13, f32[8]{0:T(128)S(1)} %copy-done.15, f32[8,128]{1,0:T(8,128)S(1)} %bitcast.4, bf16[256,768]{1,0:T(8,128)(2,1)S(1)} %copy-done, bf16[256,768]{1,0:T(8,128)(2,1)S(1)} %copy-done.1, ...), custom_call_target="tpu_custom_call", output_to_operand_aliasing={{}: (10, {})} | custom-call | flops 201326592 | bytes 2359296 | tf_op jit(solution)/shard_map/blocks/pallas_call | solution.py:127
  58.8 0.0 copy-done.3
  58.8 0.0 copy-done.5
  58.8 0.0 copy-done.7
  58.8 0.0 copy-done.14
  58.8 0.0 copy-start.9
  58.8 0.0 copy-start.11
  58.8 2.3 %blocks.6.refs_9_ = bf16[32,128,128]{2,1,0:T(8,128)(2,1)} custom-call(s32[106]{0:T(128)S(1)} %copy-done.14, f32[8]{0:T(128)S(1)} %copy-done.15, f32[8,128]{1,0:T(8,128)S(1)} %bitcast.5, bf16[256,768]{1,0:T(8,128)(2,1)S(1)} %copy-done, bf16[256,768]{1,0:T(8,128)(2,1)S(1)} %copy-done.1, ...), custom_call_target="tpu_custom_call", output_to_operand_aliasing={{}: (12, {})} | custom-call | flops 402653184 | bytes 4718592 | tf_op jit(solution)/shard_map/blocks/pallas_call | solution.py:127
  61.1 0.0 copy-done.9
  61.2 0.0 copy-done.11
  61.2 2.9 %blocks.7.refs_9_ = bf16[32,128,128]{2,1,0:T(8,128)(2,1)} custom-call(s32[106]{0:T(128)S(1)} %copy-done.14, f32[8]{0:T(128)S(1)} %copy-done.15, f32[8,128]{1,0:T(8,128)S(1)} %bitcast.6, bf16[256,768]{1,0:T(8,128)(2,1)S(1)} %copy-done, bf16[256,768]{1,0:T(8,128)(2,1)S(1)} %copy-done.1, ...), custom_call_target="tpu_custom_call", output_to_operand_aliasing={{}: (12, {})} | custom-call | flops 402653184 | bytes 4718592 | tf_op jit(solution)/shard_map/blocks/pallas_call | solution.py:127
  64.1 0.0 collective-permute-done.15.refs_6_
  64.1 0.0 collective-permute-done.16.refs_7_
  64.1 3.1 %blocks.8.refs_7_ = bf16[32,128,128]{2,1,0:T(8,128)(2,1)} custom-call(s32[106]{0:T(128)S(1)} %copy-done.14, f32[8]{0:T(128)S(1)} %copy-done.15, f32[8,128]{1,0:T(8,128)S(1)} %bitcast.7, bf16[256,768]{1,0:T(8,128)(2,1)S(1)} %copy-done, bf16[256,768]{1,0:T(8,128)(2,1)S(1)} %copy-done.1, ...), custom_call_target="tpu_custom_call", output_to_operand_aliasing={{}: (12, {})} | custom-call | flops 402653184 | bytes 4718592 | tf_op jit(solution)/shard_map/blocks/pallas_call | solution.py:127
  67.2 0.7 %collective-permute-done.13.refs_5_ = bf16[256,768]{1,0:T(8,128)(2,1)} collective-permute-done((bf16[256,768]{1,0:T(8,128)(2,1)}, bf16[256,768]{1,0:T(8,128)(2,1)}, u32[]{:S(2)}, u32[]{:S(2)}) %collective-permute-start.13) | collective-permute-done | bytes 393248 | tf_op jit(solution)/shard_map/ppermute | solution.py:193
  68.0 0.0 collective-permute-done.14.refs_6_
  68.0 2.4 %blocks.9 = bf16[32,128,128]{2,1,0:T(8,128)(2,1)} custom-call(s32[106]{0:T(128)S(1)} %copy-done.14, f32[8]{0:T(128)S(1)} %copy-done.15, f32[8,128]{1,0:T(8,128)S(1)} %bitcast.8, bf16[256,768]{1,0:T(8,128)(2,1)S(1)} %copy-done, bf16[256,768]{1,0:T(8,128)(2,1)S(1)} %copy-done.1, ...), custom_call_target="tpu_custom_call", output_to_operand_aliasing={{}: (10, {})} | custom-call | flops 201326592 | bytes 2359296 | tf_op jit(solution)/shard_map/blocks/pallas_call | solution.py:127
  (11 shorter events, 0.0 us)
Async XLA Ops:
  0.0 56.2 %copy-start = (bf16[256,768]{1,0:T(8,128)(2,1)S(1)}, bf16[256,768]{1,0:T(8,128)(2,1)}, u32[]{:S(2)}) copy-start(bf16[256,768]{1,0:T(8,128)(2,1)} %refs_0_.9) | copy-start | bytes 1179652
  0.0 56.2 %copy-start.1 = (bf16[256,768]{1,0:T(8,128)(2,1)S(1)}, bf16[256,768]{1,0:T(8,128)(2,1)}, u32[]{:S(2)}) copy-start(bf16[256,768]{1,0:T(8,128)(2,1)} %refs_1_.9) | copy-start | bytes 1179652
  0.0 56.2 %copy-start.12 = (f32[1024]{0:T(1024)S(1)}, f32[1024]{0:T(1024)}, u32[]{:S(2)}) copy-start(f32[1024]{0:T(1024)} %param.10) | copy-start | bytes 12292
  0.0 56.2 %copy-start.15 = (f32[8]{0:T(128)S(1)}, f32[8]{0:T(128)}, u32[]{:S(2)}) copy-start(f32[8]{0:T(128)} %occ.9) | copy-start | bytes 100
  0.0 13.2 %collective-permute-start.2 = (bf16[256,768]{1,0:T(8,128)(2,1)}, bf16[256,768]{1,0:T(8,128)(2,1)S(1)}, u32[]{:S(2)}, u32[]{:S(2)}) collective-permute-start(bf16[256,768]{1,0:T(8,128)(2,1)} %refs_0_.9), channel_id=1, source_target_pairs={{0,8},{8,16},{16,24},{24,28},{28,20},{20,12},{12,4},{4,0},{1,9},{9... | collective-permute-start | bytes 1179656 | tf_op jit(solution)/shard_map/ppermute | solution.py:193
  3.1 12.2 %collective-permute-start.5 = (bf16[256,768]{1,0:T(8,128)(2,1)}, bf16[256,768]{1,0:T(8,128)(2,1)S(1)}, u32[]{:S(2)}, u32[]{:S(2)}) collective-permute-start(bf16[256,768]{1,0:T(8,128)(2,1)} %refs_1_.9), channel_id=1, source_target_pairs={{8,0},{16,8},{24,16},{28,24},{20,28},{12,20},{4,12},{0,4},{9,1},{1... | collective-permute-start | bytes 1179656 | tf_op jit(solution)/shard_map/ppermute | solution.py:194
  3.1 13.0 %collective-permute-start = (bf16[256,768]{1,0:T(8,128)(2,1)}, bf16[256,768]{1,0:T(8,128)(2,1)S(1)}, u32[]{:S(2)}, u32[]{:S(2)}) collective-permute-start(bf16[256,768]{1,0:T(8,128)(2,1)} %refs_0_.9), channel_id=1, source_target_pairs={{0,2},{1,3},{2,0},{3,1},{4,6},{5,7},{6,4},{7,5},{8,10},{9,11},{10,... | collective-permute-start | bytes 1179656 | tf_op jit(solution)/shard_map/ppermute | solution.py:155
  5.1 16.5 %collective-permute-start.10 = (bf16[256,768]{1,0:T(8,128)(2,1)}, bf16[256,768]{1,0:T(8,128)(2,1)S(1)}, u32[]{:S(2)}, u32[]{:S(2)}) collective-permute-start(bf16[256,768]{1,0:T(8,128)(2,1)} %refs_1_.9), channel_id=1, source_target_pairs={{0,8},{8,16},{16,24},{24,28},{28,20},{20,12},{12,4},{4,0},{1,9},{9... | collective-permute-start | bytes 1179656 | tf_op jit(solution)/shard_map/ppermute | solution.py:196
  6.6 17.1 %collective-permute-start.8 = (bf16[256,768]{1,0:T(8,128)(2,1)}, bf16[256,768]{1,0:T(8,128)(2,1)S(1)}, u32[]{:S(2)}, u32[]{:S(2)}) collective-permute-start(bf16[256,768]{1,0:T(8,128)(2,1)} %refs_0_.9), channel_id=1, source_target_pairs={{8,0},{16,8},{24,16},{28,24},{20,28},{12,20},{4,12},{0,4},{9,1},{1... | collective-permute-start | bytes 1179656 | tf_op jit(solution)/shard_map/ppermute | solution.py:197
  13.2 16.9 %collective-permute-start.3 = (bf16[256,768]{1,0:T(8,128)(2,1)S(1)}, bf16[256,768]{1,0:T(8,128)(2,1)S(1)}, u32[]{:S(2)}, u32[]{:S(2)}) collective-permute-start(bf16[256,768]{1,0:T(8,128)(2,1)S(1)} %collective-permute-done.2.refs_5_), channel_id=1, source_target_pairs={{0,8},{8,16},{16,24},{24,28},{28,20},{20,12},{12,4},{4,0},{1,9},{9... | collective-permute-start | bytes 1179656 | tf_op jit(solution)/shard_map/ppermute | solution.py:193
  15.3 16.9 %collective-permute-start.6 = (bf16[256,768]{1,0:T(8,128)(2,1)S(1)}, bf16[256,768]{1,0:T(8,128)(2,1)S(1)}, u32[]{:S(2)}, u32[]{:S(2)}) collective-permute-start(bf16[256,768]{1,0:T(8,128)(2,1)S(1)} %collective-permute-done.5.refs_8_), channel_id=1, source_target_pairs={{8,0},{16,8},{24,16},{28,24},{20,28},{12,20},{4,12},{0,4},{9,1},{1... | collective-permute-start | bytes 1179656 | tf_op jit(solution)/shard_map/ppermute | solution.py:194
  15.3 0.8 %copy-start.2 = (bf16[256,768]{1,0:T(8,128)(2,1)}, bf16[256,768]{1,0:T(8,128)(2,1)S(1)}, u32[]{:S(2)}) copy-start(bf16[256,768]{1,0:T(8,128)(2,1)S(1)} %collective-permute-done.5.refs_8_) | copy-start | bytes 1179652
  16.1 16.1 %collective-permute-start.1 = (bf16[256,768]{1,0:T(8,128)(2,1)}, bf16[256,768]{1,0:T(8,128)(2,1)S(1)}, u32[]{:S(2)}, u32[]{:S(2)}) collective-permute-start(bf16[256,768]{1,0:T(8,128)(2,1)} %refs_1_.9), channel_id=1, source_target_pairs={{0,2},{1,3},{2,0},{3,1},{4,6},{5,7},{6,4},{7,5},{8,10},{9,11},{10,... | collective-permute-start | bytes 1179656 | tf_op jit(solution)/shard_map/ppermute | solution.py:156
  21.6 13.2 %copy-start.4 = (bf16[256,768]{1,0:T(8,128)(2,1)}, bf16[256,768]{1,0:T(8,128)(2,1)S(1)}, u32[]{:S(2)}) copy-start(bf16[256,768]{1,0:T(8,128)(2,1)S(1)} %collective-permute-done.10.refs_7_) | copy-start | bytes 1179652
  21.6 17.0 %collective-permute-start.11 = (bf16[256,768]{1,0:T(8,128)(2,1)S(1)}, bf16[256,768]{1,0:T(8,128)(2,1)}, u32[]{:S(2)}, u32[]{:S(2)}) collective-permute-start(bf16[256,768]{1,0:T(8,128)(2,1)S(1)} %collective-permute-done.10.refs_7_), channel_id=1, source_target_pairs={{0,8},{8,16},{16,24},{24,28},{28,20},{20,12},{12,4},{4,0},{1,9},{9... | collective-permute-start | bytes 1179656 | tf_op jit(solution)/shard_map/ppermute | solution.py:196
  23.8 11.0 %copy-start.6 = (bf16[256,768]{1,0:T(8,128)(2,1)}, bf16[256,768]{1,0:T(8,128)(2,1)S(1)}, u32[]{:S(2)}) copy-start(bf16[256,768]{1,0:T(8,128)(2,1)S(1)} %collective-permute-done.8.refs_6_) | copy-start | bytes 1179652
  23.8 17.0 %collective-permute-start.9 = (bf16[256,768]{1,0:T(8,128)(2,1)S(1)}, bf16[256,768]{1,0:T(8,128)(2,1)}, u32[]{:S(2)}, u32[]{:S(2)}) collective-permute-start(bf16[256,768]{1,0:T(8,128)(2,1)S(1)} %collective-permute-done.8.refs_6_), channel_id=1, source_target_pairs={{8,0},{16,8},{24,16},{28,24},{20,28},{12,20},{4,12},{0,4},{9,1},{1... | collective-permute-start | bytes 1179656 | tf_op jit(solution)/shard_map/ppermute | solution.py:197
  30.0 4.8 %copy-start.8 = (bf16[256,768]{1,0:T(8,128)(2,1)}, bf16[256,768]{1,0:T(8,128)(2,1)S(1)}, u32[]{:S(2)}) copy-start(bf16[256,768]{1,0:T(8,128)(2,1)S(1)} %collective-permute-done.3.refs_5_) | copy-start | bytes 1179652
  30.0 16.1 %collective-permute-start.4 = (bf16[256,768]{1,0:T(8,128)(2,1)S(1)}, bf16[256,768]{1,0:T(8,128)(2,1)}, u32[]{:S(2)}, u32[]{:S(2)}) collective-permute-start(bf16[256,768]{1,0:T(8,128)(2,1)S(1)} %collective-permute-done.3.refs_5_), channel_id=1, source_target_pairs={{0,8},{8,16},{16,24},{24,28},{28,20},{20,12},{12,4},{4,0},{1,9},{9... | collective-permute-start | bytes 1179656 | tf_op jit(solution)/shard_map/ppermute | solution.py:193
  32.2 2.6 %copy-start.10 = (bf16[256,768]{1,0:T(8,128)(2,1)}, bf16[256,768]{1,0:T(8,128)(2,1)S(1)}, u32[]{:S(2)}) copy-start(bf16[256,768]{1,0:T(8,128)(2,1)S(1)} %collective-permute-done.6.refs_8_) | copy-start | bytes 1179652
  32.2 15.5 %collective-permute-start.7 = (bf16[256,768]{1,0:T(8,128)(2,1)S(1)}, bf16[256,768]{1,0:T(8,128)(2,1)}, u32[]{:S(2)}, u32[]{:S(2)}) collective-permute-start(bf16[256,768]{1,0:T(8,128)(2,1)S(1)} %collective-permute-done.6.refs_8_), channel_id=1, source_target_pairs={{8,0},{16,8},{24,16},{28,24},{20,28},{12,20},{4,12},{0,4},{9,1},{1... | collective-permute-start | bytes 1179656 | tf_op jit(solution)/shard_map/ppermute | solution.py:194
  47.7 7.3 %collective-permute-start.12 = (bf16[1024,768]{1,0:T(8,128)(2,1)}, bf16[1024,768]{1,0:T(8,128)(2,1)S(1)}, u32[]{:S(2)}, u32[]{:S(2)}) collective-permute-start(bf16[1024,768]{1,0:T(8,128)(2,1)} %pad_maximum_fusion), channel_id=1, source_target_pairs={{0,1},{1,0},{2,3},{3,2},{4,5},{5,4},{6,7},{7,6},{8,9},{9,8},{10,11... | collective-permute-start | bytes 4718600 | tf_op jit(solution)/shard_map/ppermute | solution.py:161
  47.7 16.4 %collective-permute-start.15 = (bf16[256,768]{1,0:T(8,128)(2,1)}, bf16[256,768]{1,0:T(8,128)(2,1)}, u32[]{:S(2)}, u32[]{:S(2)}) collective-permute-start(bf16[256,768]{1,0:T(8,128)(2,1)} %collective-permute-done.9.refs_6_), channel_id=1, source_target_pairs={{8,0},{16,8},{24,16},{28,24},{20,28},{12,20},{4,12},{0,4},{9,1},{1... | collective-permute-start | bytes 1179656 | tf_op jit(solution)/shard_map/ppermute | solution.py:197
  48.0 16.1 %collective-permute-start.16 = (bf16[256,768]{1,0:T(8,128)(2,1)}, bf16[256,768]{1,0:T(8,128)(2,1)}, u32[]{:S(2)}, u32[]{:S(2)}) collective-permute-start(bf16[256,768]{1,0:T(8,128)(2,1)} %collective-permute-done.11.refs_7_), channel_id=1, source_target_pairs={{0,8},{8,16},{16,24},{24,28},{28,20},{20,12},{12,4},{4,0},{1,9},{9... | collective-permute-start | bytes 1179656 | tf_op jit(solution)/shard_map/ppermute | solution.py:196
  49.7 18.2 %collective-permute-start.13 = (bf16[256,768]{1,0:T(8,128)(2,1)}, bf16[256,768]{1,0:T(8,128)(2,1)}, u32[]{:S(2)}, u32[]{:S(2)}) collective-permute-start(bf16[256,768]{1,0:T(8,128)(2,1)} %collective-permute-done.4.refs_5_), channel_id=1, source_target_pairs={{0,8},{8,16},{16,24},{24,28},{28,20},{20,12},{12,4},{4,0},{1,9},{9... | collective-permute-start | bytes 1179656 | tf_op jit(solution)/shard_map/ppermute | solution.py:193
  51.3 16.7 %collective-permute-start.14 = (bf16[256,768]{1,0:T(8,128)(2,1)}, bf16[256,768]{1,0:T(8,128)(2,1)}, u32[]{:S(2)}, u32[]{:S(2)}) collective-permute-start(bf16[256,768]{1,0:T(8,128)(2,1)} %collective-permute-done.7.refs_8_), channel_id=1, source_target_pairs={{8,0},{16,8},{24,16},{28,24},{20,28},{12,20},{4,12},{0,4},{9,1},{1... | collective-permute-start | bytes 1179656 | tf_op jit(solution)/shard_map/ppermute | solution.py:194
  56.3 0.7 copy-start.13
  56.9 1.8 %copy-start.3 = (bf16[256,768]{1,0:T(8,128)(2,1)S(1)}, bf16[256,768]{1,0:T(8,128)(2,1)}, u32[]{:S(2)}) copy-start(bf16[256,768]{1,0:T(8,128)(2,1)} %copy-done.2) | copy-start | bytes 1179652
  56.9 1.8 %copy-start.5 = (bf16[256,768]{1,0:T(8,128)(2,1)S(1)}, bf16[256,768]{1,0:T(8,128)(2,1)}, u32[]{:S(2)}) copy-start(bf16[256,768]{1,0:T(8,128)(2,1)} %copy-done.4) | copy-start | bytes 1179652
  56.9 1.9 %copy-start.7 = (bf16[256,768]{1,0:T(8,128)(2,1)S(1)}, bf16[256,768]{1,0:T(8,128)(2,1)}, u32[]{:S(2)}) copy-start(bf16[256,768]{1,0:T(8,128)(2,1)} %copy-done.6) | copy-start | bytes 1179652
  56.9 1.9 %copy-start.14 = (s32[106]{0:T(128)S(1)}, s32[106]{0:T(128)}, u32[]{:S(2)}) copy-start(s32[106]{0:T(128)} %slots.1.tab) | copy-start | bytes 1276
  58.8 2.4 %copy-start.9 = (bf16[256,768]{1,0:T(8,128)(2,1)S(1)}, bf16[256,768]{1,0:T(8,128)(2,1)}, u32[]{:S(2)}) copy-start(bf16[256,768]{1,0:T(8,128)(2,1)} %copy-done.8) | copy-start | bytes 1179652
  58.8 2.4 %copy-start.11 = (bf16[256,768]{1,0:T(8,128)(2,1)S(1)}, bf16[256,768]{1,0:T(8,128)(2,1)}, u32[]{:S(2)}) copy-start(bf16[256,768]{1,0:T(8,128)(2,1)} %copy-done.10) | copy-start | bytes 1179652

commit v2 on v1

--- a/solution.py
+++ b/solution.py
@@ -74,12 +74,10 @@
     )(where, source, mask)
 
 
-def step_kernel(hops, spots, ncol, nrow, split, tab, occ, vir, *refs):
-    kept = 1 + max(n for at in spots.values() for n, _ in at)
-    row_shards = refs[:kept]
-    refs = refs[kept:]
+def step_kernel(hops, ncol, nrow, split, tab, occ, vir, *refs):
+    amp_row, int_row = refs[:2]
+    refs = refs[2:]
     count = len(hops)
-    rows = split * BLOCK
     amp_b, int_b = refs[:count], refs[count : 2 * count]
     _, out, tiles, sem = refs[2 * count :]
     cells = ncol * nrow
@@ -96,28 +94,26 @@
     stores = []
     for n, s in enumerate(hops):
         i = tab[3 * cells + s]
-        for m in range(ncol):
-            j = jnp.bitwise_xor(col_at, m)
+        for j in range(ncol):
             at = j * nrow + i
             lead, trail = tab[cells + at], tab[2 * cells + at]
-            a, b = half(lead), half(trail)
-            amp_a, int_a = (row_shards[n_at].at[pl.ds(q * rows, rows)] for n_at, q in spots[m])
-            direct = lax.dot_general(amp_a[a, :], int_b[n][b, :], nt, preferred_element_type=jnp.float32)
-            mirror = lax.dot_general(int_a[a, :], amp_b[n][b, :], nt, preferred_element_type=jnp.float32)
+            a, b = half(j * split + lead), half(trail)
+            direct = lax.dot_general(amp_row[a, :], int_b[n][b, :], nt, preferred_element_type=jnp.float32)
+            mirror = lax.dot_general(int_row[a, :], amp_b[n][b, :], nt, preferred_element_type=jnp.float32)
             gap_a = gap((row_at * ncol + j) * split + lead)
             gap_b = gap((i * ncol + col_at) * split + trail)
             denom = jnp.broadcast_to(gap_a, (BLOCK, BLOCK)).T + gap_b
             total = direct.astype(jnp.bfloat16).astype(jnp.float32) + mirror.astype(jnp.bfloat16).astype(jnp.float32)
-            tiles[n, m] = (total / denom).astype(jnp.bfloat16)
+            tiles[n, j] = (total / denom).astype(jnp.bfloat16)
             slot = tab[at]
-            stores.append((slot, pltpu.make_async_copy(tiles.at[n, m], out.at[jnp.maximum(slot, 0)], sem.at[n, m])))
+            stores.append((slot, pltpu.make_async_copy(tiles.at[n, j], out.at[jnp.maximum(slot, 0)], sem.at[n, j])))
     for slot, store in stores:
         pl.when(slot >= 0)(store.start)
     for slot, store in stores:
         pl.when(slot >= 0)(store.wait)
 
 
-def step(hops, spots, tab, occ, vir, row_shards, amp_b, int_b, out, ncol, nrow, split):
+def step(hops, tab, occ, vir, row_shards, amp_b, int_b, out, ncol, nrow, split):
     rows, width = amp_b[0].shape
     count = len(hops)
     smem = pl.BlockSpec(memory_space=pltpu.SMEM)
@@ -125,7 +121,7 @@
     hbm = pl.BlockSpec(memory_space=pl.ANY)
     shard_count = len(row_shards) + 2 * count
     return pl.pallas_call(
-        functools.partial(step_kernel, hops, spots, ncol, nrow, split),
+        functools.partial(step_kernel, hops, ncol, nrow, split),
         in_specs=[smem, smem, vmem] + [vmem] * shard_count + [hbm],
         out_specs=hbm,
         scratch_shapes=[
@@ -144,29 +140,6 @@
     )(tab, occ, vir, *row_shards, *amp_b, *int_b, out)
 
 
-def gather_cols(amplitudes, integrals, ncol, held):
-    arrays, spots = [amplitudes, integrals], {0: ((0, 0), (1, 0))}
-    rows = amplitudes.shape[0]
-    bit = ncol // 2
-    while bit:
-        pairs = [(c, c ^ bit) for c in range(ncol)]
-        if len(arrays) == 2:
-            spots[bit] = ((2, 0), (3, 0))
-            arrays.append(lax.ppermute(amplitudes, "col", pairs))
-            arrays.append(lax.ppermute(after(integrals, arrays[2]), "col", pairs))
-        else:
-            starts = np.cumsum([0] + [array.shape[0] // rows for array in arrays])
-            moved = {m ^ bit: tuple((len(arrays), int(starts[n]) + q) for n, q in at) for m, at in spots.items()}
-            spots.update(moved)
-            arrays.append(lax.ppermute(after(jnp.concatenate(arrays), held), "col", pairs))
-        bit //= 2
-    return arrays, spots
-
-
-def after(x, gate):
-    return x if gate is None else lax.optimization_barrier((x, gate))[0]
-
-
 def shards(amplitudes, integrals, block_mask, occ_energy, vir_energy):
     nrow = lax.axis_size("row")
     ncol = lax.axis_size("col")
@@ -182,8 +155,10 @@
     vir = vir_energy.reshape(-1, BLOCK)
     out = jnp.zeros((limit, BLOCK, BLOCK), jnp.bfloat16)
 
+    row_shards = [lax.all_gather(x, "col", axis=0, tiled=True) for x in (amplitudes, integrals)]
+
     def update(hops, amp_b, int_b, out):
-        return step(hops, spots, tab, occ_energy, vir, row_shards, amp_b, int_b, out, ncol, nrow, split)
+        return step(hops, tab, occ_energy, vir, row_shards, amp_b, int_b, out, ncol, nrow, split)
 
     far = nrow // 2
     amp_up = amp_down = amplitudes
@@ -195,13 +170,10 @@
         if s < nrow - s:
             int_up = lax.ppermute(int_up, "row", ahead)
             amp_down = lax.ppermute(amp_down, "row", behind)
-        if s == min(3, far):
-            row_shards, spots = gather_cols(amplitudes, integrals, ncol, (amp_up, int_down, *last))
+        if s == min(2, far):
             out = update((0,), (amplitudes,), (integrals,), out)
-            out = update((1, nrow - 1), before[:2], before[2:], out)
-        if s >= 3:
+        if s >= 2:
             out = update((s - 1, nrow - s + 1), last[:2], last[2:], out)
-        before = last
     if far == nrow - far:
         out = update((far,), (amp_up,), (int_down,), out)
     else:

time: 70.6 us -> 85 us (1.20)
  between operations: 0.18 us -> 13.6 us
  waiting for transfers between devices: 29.6 us -> 34.9 us
  starting transfers between devices: 19.5 us -> 15.7 us
  other arithmetic: 3.17 us -> 0.65 us
  local copies, waits for them, and re-layouts: 2.69 us -> 4.71 us
    ppermute x3, waiting for transfers between devices: 2.22 us -> 16.8 us  [shards(): amp_down = lax.ppermute(amp_down, 'row', behind)]
    ppermute x3, waiting for transfers between devices: 7.26 us -> 0.01 us  [shards(): int_up = lax.ppermute(int_up, 'row', ahead)]
    ppermute x3 -> x0, starting transfers between devices: 3.93 us -> none  [the longest x1 1.97 us: gather_cols(): arrays.append(lax.ppermute(amplitudes, 'col', pairs))]
    concatenate x1 -> x0, other arithmetic: 2.55 us -> none  [gather_cols(): jnp.concatenate(arrays)]
    unnamed x32 -> x18, local copies, waits for them, and re-layouts: 1.49 us -> 3.5 us
    ppermute x4, waiting for transfers between devices: 18.5 us -> 16.5 us  [shards(): amp_up = lax.ppermute(amp_up, 'row', ahead)]
    ppermute x4, waiting for transfers between devices: 1.62 us -> 0.12 us  [shards(): int_down = lax.ppermute(int_down, 'row', behind)]
    unnamed x0 -> x2, waiting for transfers between devices: none -> 1.38 us
  transfers between devices with their start and end apart: 17 -> 16, of which waited for: 8 -> 5; matrix products, arithmetic and copies ran while one was open for 6% -> 2% of each run, Pallas kernels for 18% -> 15%
where the time goes in v2:
time: 85 us; the launch traced here: 84.7 us
  waiting for transfers between devices  34.9 us (41%)
  starting transfers between devices  15.7 us (18%)
  Pallas kernels  15.1 us (18%)
  between operations  13.6 us (16%)
  local copies, waits for them, and re-layouts  4.71 us (6%)
    ppermute x3, waiting for transfers between devices, shards(): amp_down = lax.ppermute(amp_down, 'row', behind)  16.8 us
    ppermute x4, waiting for transfers between devices, shards(): amp_up = lax.ppermute(amp_up, 'row', ahead)  16.5 us
    pallas_call x5, Pallas kernels, step(): pl.pallas_call(functools.partial(step_kernel, hops, ncol, nrow, split), i...  12.5 us
    ppermute x4, starting transfers between devices, shards(): amp_up = lax.ppermute(amp_up, 'row', ahead)  9.51 us
    ppermute x3, starting transfers between devices, shards(): int_up = lax.ppermute(int_up, 'row', ahead)  4.16 us
    unnamed x18, local copies, waits for them, and re-layouts  3.5 us
    pallas_call x1, Pallas kernels, slot_table(): pl.pallas_call(functools.partial(table_kernel, ncol, nrow, split), in_spe...  2.64 us
    ppermute x3, starting transfers between devices, shards(): amp_down = lax.ppermute(amp_down, 'row', behind)  1.94 us
  transfers between devices with their start and end apart: 16, of which 5 were waited for; matrix products, arithmetic and copies ran while one was open for 2% of the time, Pallas kernels for 15%

profile of v2, /device:TPU:0, one launch (start us, length us, event | category | flops | bytes accessed | tf_op | source)
XLA Modules:
  0.0 84.7 jit_solution(10256570110018105020)
XLA Ops:
  6.5 0.0 copy-start.3
  6.5 0.0 copy-start.4
  6.5 0.0 copy-start.5
  6.5 0.0 copy-start.8
  6.5 0.0 all-gather.3.cloned.1.call-start
  6.6 0.7 all-gather.3.cloned.1.call-update
  7.3 0.0 all-gather.5.cloned.1.call-start
  7.3 0.7 all-gather.5.cloned.1.call-update
  8.0 3.1 %collective-permute-start = (bf16[256,768]{1,0:T(8,128)(2,1)}, bf16[256,768]{1,0:T(8,128)(2,1)S(1)}, u32[]{:S(2)}, u32[]{:S(2)}) collective-permute-start(bf16[256,768]{1,0:T(8,128)(2,1)} %refs_2_.1), channel_id=1, source_target_pairs={{0,8},{8,16},{16,24},{24,28},{28,20},{20,12},{12,4},{4,0},{1,9},{9... | collective-permute-start | bytes 1179656 | tf_op jit(solution)/shard_map/ppermute | solution.py:168
  11.1 0.0 collective-permute-start.4
  11.1 1.9 %collective-permute-start.8 = (bf16[256,768]{1,0:T(8,128)(2,1)}, bf16[256,768]{1,0:T(8,128)(2,1)S(1)}, u32[]{:S(2)}, u32[]{:S(2)}) collective-permute-start(bf16[256,768]{1,0:T(8,128)(2,1)} %refs_2_.1), channel_id=1, source_target_pairs={{8,0},{16,8},{24,16},{28,24},{20,28},{12,20},{4,12},{0,4},{9,1},{1... | collective-permute-start | bytes 1179656 | tf_op jit(solution)/shard_map/ppermute | solution.py:172
  13.0 0.1 collective-permute-start.11
  13.2 8.0 %collective-permute-done.refs_2_ = bf16[256,768]{1,0:T(8,128)(2,1)S(1)} collective-permute-done((bf16[256,768]{1,0:T(8,128)(2,1)}, bf16[256,768]{1,0:T(8,128)(2,1)S(1)}, u32[]{:S(2)}, u32[]{:S(2)}) %collective-permute-start) | collective-permute-done | bytes 393248 | tf_op jit(solution)/shard_map/ppermute | solution.py:168
  21.2 2.1 %collective-permute-start.1 = (bf16[256,768]{1,0:T(8,128)(2,1)S(1)}, bf16[256,768]{1,0:T(8,128)(2,1)S(1)}, u32[]{:S(2)}, u32[]{:S(2)}) collective-permute-start(bf16[256,768]{1,0:T(8,128)(2,1)S(1)} %collective-permute-done.refs_2_), channel_id=1, source_target_pairs={{0,8},{8,16},{16,24},{24,28},{28,20},{20,12},{12,4},{4,0},{1,9},{9... | collective-permute-start | bytes 1179656 | tf_op jit(solution)/shard_map/ppermute | solution.py:168
  23.3 0.0 collective-permute-done.4.refs_5_
  23.3 0.0 collective-permute-start.5
  23.4 8.4 %collective-permute-done.8.refs_3_ = bf16[256,768]{1,0:T(8,128)(2,1)S(1)} collective-permute-done((bf16[256,768]{1,0:T(8,128)(2,1)}, bf16[256,768]{1,0:T(8,128)(2,1)S(1)}, u32[]{:S(2)}, u32[]{:S(2)}) %collective-permute-start.8) | collective-permute-done | bytes 393248 | tf_op jit(solution)/shard_map/ppermute | solution.py:172
  31.8 0.0 collective-permute-start.9
  31.8 0.0 collective-permute-done.11.refs_4_
  31.8 2.0 %collective-permute-start.12 = (bf16[256,768]{1,0:T(8,128)(2,1)S(1)}, bf16[256,768]{1,0:T(8,128)(2,1)}, u32[]{:S(2)}, u32[]{:S(2)}) collective-permute-start(bf16[256,768]{1,0:T(8,128)(2,1)S(1)} %collective-permute-done.11.refs_4_), channel_id=1, source_target_pairs={{0,8},{8,16},{16,24},{24,28},{28,20},{20,12},{12,4},{4,0},{1,9},{9... | collective-permute-start | bytes 1179656 | tf_op jit(solution)/shard_map/ppermute | solution.py:171
  33.8 4.2 %collective-permute-done.1.refs_2_ = bf16[256,768]{1,0:T(8,128)(2,1)S(1)} collective-permute-done((bf16[256,768]{1,0:T(8,128)(2,1)S(1)}, bf16[256,768]{1,0:T(8,128)(2,1)S(1)}, u32[]{:S(2)}, u32[]{:S(2)}) %collective-permute-start.1) | collective-permute-done | bytes 393248 | tf_op jit(solution)/shard_map/ppermute | solution.py:168
  38.0 2.1 %collective-permute-start.2 = (bf16[256,768]{1,0:T(8,128)(2,1)S(1)}, bf16[256,768]{1,0:T(8,128)(2,1)}, u32[]{:S(2)}, u32[]{:S(2)}) collective-permute-start(bf16[256,768]{1,0:T(8,128)(2,1)S(1)} %collective-permute-done.1.refs_2_), channel_id=1, source_target_pairs={{0,8},{8,16},{16,24},{24,28},{28,20},{20,12},{12,4},{4,0},{1,9},{9... | collective-permute-start | bytes 1179656 | tf_op jit(solution)/shard_map/ppermute | solution.py:168
  40.2 0.0 collective-permute-done.5.refs_5_
  40.2 0.0 collective-permute-start.6
  40.2 8.4 %collective-permute-done.9.refs_3_ = bf16[256,768]{1,0:T(8,128)(2,1)S(1)} collective-permute-done((bf16[256,768]{1,0:T(8,128)(2,1)S(1)}, bf16[256,768]{1,0:T(8,128)(2,1)S(1)}, u32[]{:S(2)}, u32[]{:S(2)}) %collective-permute-start.9) | collective-permute-done | bytes 393248 | tf_op jit(solution)/shard_map/ppermute | solution.py:172
  48.6 0.0 collective-permute-start.10
  48.6 0.0 collective-permute-done.12.refs_4_
  48.6 2.0 %collective-permute-start.13 = (bf16[256,768]{1,0:T(8,128)(2,1)}, bf16[256,768]{1,0:T(8,128)(2,1)}, u32[]{:S(2)}, u32[]{:S(2)}) collective-permute-start(bf16[256,768]{1,0:T(8,128)(2,1)} %collective-permute-done.12.refs_4_), channel_id=1, source_target_pairs={{0,8},{8,16},{16,24},{24,28},{28,20},{20,12},{12,4},{4,0},{1,9},{9... | collective-permute-start | bytes 1179656 | tf_op jit(solution)/shard_map/ppermute | solution.py:171
  50.7 4.3 %collective-permute-done.2.refs_2_ = bf16[256,768]{1,0:T(8,128)(2,1)} collective-permute-done((bf16[256,768]{1,0:T(8,128)(2,1)S(1)}, bf16[256,768]{1,0:T(8,128)(2,1)}, u32[]{:S(2)}, u32[]{:S(2)}) %collective-permute-start.2) | collective-permute-done | bytes 393248 | tf_op jit(solution)/shard_map/ppermute | solution.py:168
  55.0 2.1 %collective-permute-start.3 = (bf16[256,768]{1,0:T(8,128)(2,1)}, bf16[256,768]{1,0:T(8,128)(2,1)}, u32[]{:S(2)}, u32[]{:S(2)}) collective-permute-start(bf16[256,768]{1,0:T(8,128)(2,1)} %collective-permute-done.2.refs_2_), channel_id=1, source_target_pairs={{0,8},{8,16},{16,24},{24,28},{28,20},{20,12},{12,4},{4,0},{1,9},{9... | collective-permute-start | bytes 1179656 | tf_op jit(solution)/shard_map/ppermute | solution.py:168
  57.1 0.0 collective-permute-done.6.refs_5_
  57.2 0.0 collective-permute-start.7
  57.2 0.6 pad_add_fusion.where
  57.8 2.6 %slots.1.tab = s32[106]{0:T(128)} custom-call(s32[2]{0:T(128)} %pad_add_fusion.where, s32[64]{0:T(128)} %constant.13.clone.source, s32[8,64]{1,0:T(8,128)} %mask.1), custom_call_target="tpu_custom_call" | custom-call | tf_op jit(solution)/shard_map/slots/pallas_call | solution.py:68
  60.5 0.0 all-gather.3.cloned.1.call-done.refs_0_
  60.5 0.0 all-gather.5.cloned.1.call-done.refs_1_
  60.5 1.2 %broadcast_in_dim.6.refs_4_ = bf16[32,128,128]{2,1,0:T(8,128)(2,1)} broadcast(bf16[]{:T(256)} %constant.12.clone.1), dimensions={} | broadcast | bytes 1048578 | tf_op jit(solution)/shard_map/broadcast_in_dim | solution.py:156
  61.7 0.0 copy-done.3
  61.7 0.0 copy-done.4
  61.7 0.0 copy-done.5
  61.7 0.0 copy-done.8
  61.7 0.0 copy-start
  61.7 1.4 %copy-done = bf16[1024,768]{1,0:T(8,128)(2,1)S(1)} copy-done((bf16[1024,768]{1,0:T(8,128)(2,1)S(1)}, bf16[1024,768]{1,0:T(8,128)(2,1)}, u32[]{:S(2)}) %copy-start) | copy-done | bytes 1572888
  63.1 0.0 copy-start.2
  63.2 1.4 %copy-done.2 = bf16[1024,768]{1,0:T(8,128)(2,1)S(1)} copy-done((bf16[1024,768]{1,0:T(8,128)(2,1)S(1)}, bf16[1024,768]{1,0:T(8,128)(2,1)}, u32[]{:S(2)}) %copy-start.2) | copy-done | bytes 1572888
  64.6 0.0 copy-start.6
  64.6 0.7 copy-done.6
  65.2 0.0 copy-start.1
  65.2 0.0 copy-start.7
  65.2 1.8 %blocks.5.refs_6_ = bf16[32,128,128]{2,1,0:T(8,128)(2,1)} custom-call(s32[106]{0:T(128)S(1)} %copy-done.6, f32[8]{0:T(128)S(1)} %copy-done.8, f32[8,128]{1,0:T(8,128)S(1)} %bitcast.4, bf16[1024,768]{1,0:T(8,128)(2,1)S(1)} %copy-done, bf16[1024,768]{1,0:T(8,128)(2,1)S(1)} %copy-done.2, ...), custom_call_target="tpu_custom_call", output_to_operand_aliasing={{}: (7, {})} | custom-call | flops 201326592 | bytes 2359296 | tf_op jit(solution)/shard_map/blocks/pallas_call | solution.py:123
  67.1 0.0 copy-done.1
  67.1 0.0 copy-done.7
  67.1 2.3 %blocks.6.refs_6_ = bf16[32,128,128]{2,1,0:T(8,128)(2,1)} custom-call(s32[106]{0:T(128)S(1)} %copy-done.7, f32[8]{0:T(128)S(1)} %copy-done.8, f32[8,128]{1,0:T(8,128)S(1)} %bitcast.5, bf16[1024,768]{1,0:T(8,128)(2,1)S(1)} %copy-done.1, bf16[1024,768]{1,0:T(8,128)(2,1)S(1)} %copy-done.2, ...), custom_call_target="tpu_custom_call", output_to_operand_aliasing={{}: (9, {})} | custom-call | flops 402653184 | bytes 4718592 | tf_op jit(solution)/shard_map/blocks/pallas_call | solution.py:123
  69.4 2.8 %blocks.7.refs_6_ = bf16[32,128,128]{2,1,0:T(8,128)(2,1)} custom-call(s32[106]{0:T(128)S(1)} %copy-done.7, f32[8]{0:T(128)S(1)} %copy-done.8, f32[8,128]{1,0:T(8,128)S(1)} %bitcast.6, bf16[1024,768]{1,0:T(8,128)(2,1)S(1)} %copy-done.1, bf16[1024,768]{1,0:T(8,128)(2,1)S(1)} %copy-done.2, ...), custom_call_target="tpu_custom_call", output_to_operand_aliasing={{}: (9, {})} | custom-call | flops 402653184 | bytes 4718592 | tf_op jit(solution)/shard_map/blocks/pallas_call | solution.py:123
  72.2 0.0 collective-permute-done.10.refs_3_
  72.2 0.0 collective-permute-done.13.refs_4_
  72.2 3.1 %blocks.8.refs_4_ = bf16[32,128,128]{2,1,0:T(8,128)(2,1)} custom-call(s32[106]{0:T(128)S(1)} %copy-done.7, f32[8]{0:T(128)S(1)} %copy-done.8, f32[8,128]{1,0:T(8,128)S(1)} %bitcast.7, bf16[1024,768]{1,0:T(8,128)(2,1)S(1)} %copy-done.1, bf16[1024,768]{1,0:T(8,128)(2,1)S(1)} %copy-done.2, ...), custom_call_target="tpu_custom_call", output_to_operand_aliasing={{}: (9, {})} | custom-call | flops 402653184 | bytes 4718592 | tf_op jit(solution)/shard_map/blocks/pallas_call | solution.py:123
  75.4 0.0 collective-permute-done.3.refs_2_
  75.4 0.0 collective-permute-done.7.refs_3_
  75.4 2.4 %blocks.9 = bf16[32,128,128]{2,1,0:T(8,128)(2,1)} custom-call(s32[106]{0:T(128)S(1)} %copy-done.7, f32[8]{0:T(128)S(1)} %copy-done.8, f32[8,128]{1,0:T(8,128)S(1)} %bitcast.8, bf16[1024,768]{1,0:T(8,128)(2,1)S(1)} %copy-done.1, bf16[1024,768]{1,0:T(8,128)(2,1)S(1)} %copy-done.2, ...), custom_call_target="tpu_custom_call", output_to_operand_aliasing={{}: (7, {})} | custom-call | flops 201326592 | bytes 2359296 | tf_op jit(solution)/shard_map/blocks/pallas_call | solution.py:123
Async XLA Ops:
  6.5 55.2 %copy-start.3 = (bf16[256,768]{1,0:T(8,128)(2,1)S(1)}, bf16[256,768]{1,0:T(8,128)(2,1)}, u32[]{:S(2)}) copy-start(bf16[256,768]{1,0:T(8,128)(2,1)} %refs_2_.1) | copy-start | bytes 1179652
  6.5 55.2 %copy-start.4 = (bf16[256,768]{1,0:T(8,128)(2,1)S(1)}, bf16[256,768]{1,0:T(8,128)(2,1)}, u32[]{:S(2)}) copy-start(bf16[256,768]{1,0:T(8,128)(2,1)} %refs_3_.1) | copy-start | bytes 1179652
  6.5 55.2 %copy-start.5 = (f32[1024]{0:T(1024)S(1)}, f32[1024]{0:T(1024)}, u32[]{:S(2)}) copy-start(f32[1024]{0:T(1024)} %param.10) | copy-start | bytes 12292
  6.5 55.2 %copy-start.8 = (f32[8]{0:T(128)S(1)}, f32[8]{0:T(128)}, u32[]{:S(2)}) copy-start(f32[8]{0:T(128)} %occ.9) | copy-start | bytes 100
  6.5 53.9 %all-gather.3.cloned.1.call-start = ((), (), s32[]{:S(2)}) async-start(), calls=%async_computation | async-start | bytes 1966080 | tf_op jit(solution)/shard_map/all_gather | solution.py:158
  7.3 53.2 %all-gather.5.cloned.1.call-start = ((), (), s32[]{:S(2)}) async-start(), calls=%async_computation.1 | async-start | bytes 1966080 | tf_op jit(solution)/shard_map/all_gather | solution.py:158
  8.0 13.1 %collective-permute-start = (bf16[256,768]{1,0:T(8,128)(2,1)}, bf16[256,768]{1,0:T(8,128)(2,1)S(1)}, u32[]{:S(2)}, u32[]{:S(2)}) collective-permute-start(bf16[256,768]{1,0:T(8,128)(2,1)} %refs_2_.1), channel_id=1, source_target_pairs={{0,8},{8,16},{16,24},{24,28},{28,20},{20,12},{12,4},{4,0},{1,9},{9... | collective-permute-start | bytes 1179656 | tf_op jit(solution)/shard_map/ppermute | solution.py:168
  11.1 12.2 %collective-permute-start.4 = (bf16[256,768]{1,0:T(8,128)(2,1)}, bf16[256,768]{1,0:T(8,128)(2,1)S(1)}, u32[]{:S(2)}, u32[]{:S(2)}) collective-permute-start(bf16[256,768]{1,0:T(8,128)(2,1)} %refs_3_.1), channel_id=1, source_target_pairs={{8,0},{16,8},{24,16},{28,24},{20,28},{12,20},{4,12},{0,4},{9,1},{1... | collective-permute-start | bytes 1179656 | tf_op jit(solution)/shard_map/ppermute | solution.py:169
  11.1 20.7 %collective-permute-start.8 = (bf16[256,768]{1,0:T(8,128)(2,1)}, bf16[256,768]{1,0:T(8,128)(2,1)S(1)}, u32[]{:S(2)}, u32[]{:S(2)}) collective-permute-start(bf16[256,768]{1,0:T(8,128)(2,1)} %refs_2_.1), channel_id=1, source_target_pairs={{8,0},{16,8},{24,16},{28,24},{20,28},{12,20},{4,12},{0,4},{9,1},{1... | collective-permute-start | bytes 1179656 | tf_op jit(solution)/shard_map/ppermute | solution.py:172
  13.0 18.7 %collective-permute-start.11 = (bf16[256,768]{1,0:T(8,128)(2,1)}, bf16[256,768]{1,0:T(8,128)(2,1)S(1)}, u32[]{:S(2)}, u32[]{:S(2)}) collective-permute-start(bf16[256,768]{1,0:T(8,128)(2,1)} %refs_3_.1), channel_id=1, source_target_pairs={{0,8},{8,16},{16,24},{24,28},{28,20},{20,12},{12,4},{4,0},{1,9},{9... | collective-permute-start | bytes 1179656 | tf_op jit(solution)/shard_map/ppermute | solution.py:171
  21.2 16.9 %collective-permute-start.1 = (bf16[256,768]{1,0:T(8,128)(2,1)S(1)}, bf16[256,768]{1,0:T(8,128)(2,1)S(1)}, u32[]{:S(2)}, u32[]{:S(2)}) collective-permute-start(bf16[256,768]{1,0:T(8,128)(2,1)S(1)} %collective-permute-done.refs_2_), channel_id=1, source_target_pairs={{0,8},{8,16},{16,24},{24,28},{28,20},{20,12},{12,4},{4,0},{1,9},{9... | collective-permute-start | bytes 1179656 | tf_op jit(solution)/shard_map/ppermute | solution.py:168
  23.3 16.9 %collective-permute-start.5 = (bf16[256,768]{1,0:T(8,128)(2,1)S(1)}, bf16[256,768]{1,0:T(8,128)(2,1)S(1)}, u32[]{:S(2)}, u32[]{:S(2)}) collective-permute-start(bf16[256,768]{1,0:T(8,128)(2,1)S(1)} %collective-permute-done.4.refs_5_), channel_id=1, source_target_pairs={{8,0},{16,8},{24,16},{28,24},{20,28},{12,20},{4,12},{0,4},{9,1},{1... | collective-permute-start | bytes 1179656 | tf_op jit(solution)/shard_map/ppermute | solution.py:169
  31.8 16.9 %collective-permute-start.9 = (bf16[256,768]{1,0:T(8,128)(2,1)S(1)}, bf16[256,768]{1,0:T(8,128)(2,1)S(1)}, u32[]{:S(2)}, u32[]{:S(2)}) collective-permute-start(bf16[256,768]{1,0:T(8,128)(2,1)S(1)} %collective-permute-done.8.refs_3_), channel_id=1, source_target_pairs={{8,0},{16,8},{24,16},{28,24},{20,28},{12,20},{4,12},{0,4},{9,1},{1... | collective-permute-start | bytes 1179656 | tf_op jit(solution)/shard_map/ppermute | solution.py:172
  31.8 16.9 %collective-permute-start.12 = (bf16[256,768]{1,0:T(8,128)(2,1)S(1)}, bf16[256,768]{1,0:T(8,128)(2,1)}, u32[]{:S(2)}, u32[]{:S(2)}) collective-permute-start(bf16[256,768]{1,0:T(8,128)(2,1)S(1)} %collective-permute-done.11.refs_4_), channel_id=1, source_target_pairs={{0,8},{8,16},{16,24},{24,28},{28,20},{20,12},{12,4},{4,0},{1,9},{9... | collective-permute-start | bytes 1179656 | tf_op jit(solution)/shard_map/ppermute | solution.py:171
  38.0 17.0 %collective-permute-start.2 = (bf16[256,768]{1,0:T(8,128)(2,1)S(1)}, bf16[256,768]{1,0:T(8,128)(2,1)}, u32[]{:S(2)}, u32[]{:S(2)}) collective-permute-start(bf16[256,768]{1,0:T(8,128)(2,1)S(1)} %collective-permute-done.1.refs_2_), channel_id=1, source_target_pairs={{0,8},{8,16},{16,24},{24,28},{28,20},{20,12},{12,4},{4,0},{1,9},{9... | collective-permute-start | bytes 1179656 | tf_op jit(solution)/shard_map/ppermute | solution.py:168
  40.2 17.0 %collective-permute-start.6 = (bf16[256,768]{1,0:T(8,128)(2,1)S(1)}, bf16[256,768]{1,0:T(8,128)(2,1)}, u32[]{:S(2)}, u32[]{:S(2)}) collective-permute-start(bf16[256,768]{1,0:T(8,128)(2,1)S(1)} %collective-permute-done.5.refs_5_), channel_id=1, source_target_pairs={{8,0},{16,8},{24,16},{28,24},{20,28},{12,20},{4,12},{0,4},{9,1},{1... | collective-permute-start | bytes 1179656 | tf_op jit(solution)/shard_map/ppermute | solution.py:169
  48.6 23.6 %collective-permute-start.10 = (bf16[256,768]{1,0:T(8,128)(2,1)S(1)}, bf16[256,768]{1,0:T(8,128)(2,1)}, u32[]{:S(2)}, u32[]{:S(2)}) collective-permute-start(bf16[256,768]{1,0:T(8,128)(2,1)S(1)} %collective-permute-done.9.refs_3_), channel_id=1, source_target_pairs={{8,0},{16,8},{24,16},{28,24},{20,28},{12,20},{4,12},{0,4},{9,1},{1... | collective-permute-start | bytes 1179656 | tf_op jit(solution)/shard_map/ppermute | solution.py:172
  48.6 23.6 %collective-permute-start.13 = (bf16[256,768]{1,0:T(8,128)(2,1)}, bf16[256,768]{1,0:T(8,128)(2,1)}, u32[]{:S(2)}, u32[]{:S(2)}) collective-permute-start(bf16[256,768]{1,0:T(8,128)(2,1)} %collective-permute-done.12.refs_4_), channel_id=1, source_target_pairs={{0,8},{8,16},{16,24},{24,28},{28,20},{20,12},{12,4},{4,0},{1,9},{9... | collective-permute-start | bytes 1179656 | tf_op jit(solution)/shard_map/ppermute | solution.py:171
  55.0 20.4 %collective-permute-start.3 = (bf16[256,768]{1,0:T(8,128)(2,1)}, bf16[256,768]{1,0:T(8,128)(2,1)}, u32[]{:S(2)}, u32[]{:S(2)}) collective-permute-start(bf16[256,768]{1,0:T(8,128)(2,1)} %collective-permute-done.2.refs_2_), channel_id=1, source_target_pairs={{0,8},{8,16},{16,24},{24,28},{28,20},{20,12},{12,4},{4,0},{1,9},{9... | collective-permute-start | bytes 1179656 | tf_op jit(solution)/shard_map/ppermute | solution.py:168
  57.2 18.2 %collective-permute-start.7 = (bf16[256,768]{1,0:T(8,128)(2,1)}, bf16[256,768]{1,0:T(8,128)(2,1)}, u32[]{:S(2)}, u32[]{:S(2)}) collective-permute-start(bf16[256,768]{1,0:T(8,128)(2,1)} %collective-permute-done.6.refs_5_), channel_id=1, source_target_pairs={{8,0},{16,8},{24,16},{28,24},{20,28},{12,20},{4,12},{0,4},{9,1},{1... | collective-permute-start | bytes 1179656 | tf_op jit(solution)/shard_map/ppermute | solution.py:169
  61.7 1.4 %copy-start = (bf16[1024,768]{1,0:T(8,128)(2,1)S(1)}, bf16[1024,768]{1,0:T(8,128)(2,1)}, u32[]{:S(2)}) copy-start(bf16[1024,768]{1,0:T(8,128)(2,1)} %all-gather.3.cloned.1.call-done.refs_0_) | copy-start | bytes 4718596
  63.1 1.4 %copy-start.2 = (bf16[1024,768]{1,0:T(8,128)(2,1)S(1)}, bf16[1024,768]{1,0:T(8,128)(2,1)}, u32[]{:S(2)}) copy-start(bf16[1024,768]{1,0:T(8,128)(2,1)} %all-gather.5.cloned.1.call-done.refs_1_) | copy-start | bytes 4718596
  64.6 0.7 copy-start.6
  65.2 1.8 %copy-start.1 = (bf16[1024,768]{1,0:T(8,128)(2,1)S(1)}, bf16[1024,768]{1,0:T(8,128)(2,1)}, u32[]{:S(2)}) copy-start(bf16[1024,768]{1,0:T(8,128)(2,1)} %all-gather.3.cloned.1.call-done.refs_0_) | copy-start | bytes 4718596
  65.2 1.8 %copy-start.7 = (s32[106]{0:T(128)S(1)}, s32[106]{0:T(128)}, u32[]{:S(2)}) copy-start(s32[106]{0:T(128)} %slots.1.tab) | copy-start | bytes 1276
Sparse Core Ops, SparseCore 0:
  8.9 22.3 all-gather.2
  32.9 19.6 all-gather.4

commit v3 on v1

--- a/solution.py
+++ b/solution.py
@@ -144,27 +144,22 @@
     )(tab, occ, vir, *row_shards, *amp_b, *int_b, out)
 
 
-def gather_cols(amplitudes, integrals, ncol, held):
+def gather_cols(amplitudes, integrals, ncol):
     arrays, spots = [amplitudes, integrals], {0: ((0, 0), (1, 0))}
-    rows = amplitudes.shape[0]
     bit = ncol // 2
     while bit:
         pairs = [(c, c ^ bit) for c in range(ncol)]
         if len(arrays) == 2:
             spots[bit] = ((2, 0), (3, 0))
             arrays.append(lax.ppermute(amplitudes, "col", pairs))
-            arrays.append(lax.ppermute(after(integrals, arrays[2]), "col", pairs))
+            arrays.append(lax.ppermute(integrals, "col", pairs))
         else:
-            starts = np.cumsum([0] + [array.shape[0] // rows for array in arrays])
-            moved = {m ^ bit: tuple((len(arrays), int(starts[n]) + q) for n, q in at) for m, at in spots.items()}
-            spots.update(moved)
-            arrays.append(lax.ppermute(after(jnp.concatenate(arrays), held), "col", pairs))
+            for n, array in enumerate(list(arrays)):
+                arrays.append(lax.ppermute(array, "col", pairs))
+            known = len(arrays) // 2
+            spots.update({m ^ bit: tuple((n + known, q) for n, q in at) for m, at in spots.items()})
         bit //= 2
     return arrays, spots
-
-
-def after(x, gate):
-    return x if gate is None else lax.optimization_barrier((x, gate))[0]
 
 
 def shards(amplitudes, integrals, block_mask, occ_energy, vir_energy):
@@ -188,6 +183,7 @@
     far = nrow // 2
     amp_up = amp_down = amplitudes
     int_up = int_down = integrals
+    waiting = []
     for s in range(1, far + 1):
         last = (amp_up, amp_down, int_up, int_down)
         amp_up = lax.ppermute(amp_up, "row", ahead)
@@ -196,12 +192,14 @@
             int_up = lax.ppermute(int_up, "row", ahead)
             amp_down = lax.ppermute(amp_down, "row", behind)
         if s == min(3, far):
-            row_shards, spots = gather_cols(amplitudes, integrals, ncol, (amp_up, int_down, *last))
-            out = update((0,), (amplitudes,), (integrals,), out)
-            out = update((1, nrow - 1), before[:2], before[2:], out)
-        if s >= 3:
-            out = update((s - 1, nrow - s + 1), last[:2], last[2:], out)
-        before = last
+            row_shards, spots = gather_cols(amplitudes, integrals, ncol)
+        waiting.append((s - 1, last[0], last[2]))
+        if s >= 2:
+            waiting.append((nrow - s + 1, last[1], last[3]))
+        if s >= min(3, far):
+            hops, amp_b, int_b = zip(*waiting)
+            out = update(hops, amp_b, int_b, out)
+            waiting = []
     if far == nrow - far:
         out = update((far,), (amp_up,), (int_down,), out)
     else:

time: 70.6 us -> 71.2 us (level)
  local copies, waits for them, and re-layouts: 2.69 us -> 6.48 us
  Pallas kernels: 15.2 us -> 12.6 us
  other arithmetic: 3.17 us -> 0.65 us
  waiting for transfers between devices: 29.6 us -> 31.3 us
    ppermute x4, waiting for transfers between devices: 18.5 us -> 0.01 us  [shards(): amp_up = lax.ppermute(amp_up, 'row', ahead)]
    ppermute x4, waiting for transfers between devices: 1.62 us -> 13 us  [shards(): int_down = lax.ppermute(int_down, 'row', behind)]
    ppermute x4, starting transfers between devices: 8.95 us -> 1.65 us  [shards(): amp_up = lax.ppermute(amp_up, 'row', ahead)]
    ppermute x3, waiting for transfers between devices: 7.26 us -> 0.62 us  [shards(): int_up = lax.ppermute(int_up, 'row', ahead)]
    ppermute x4, starting transfers between devices: 0.46 us -> 6.84 us  [shards(): int_down = lax.ppermute(int_down, 'row', behind)]
    ppermute x1, waiting for transfers between devices: 0.01 us -> 6.12 us  [gather_cols(): arrays.append(lax.ppermute(amplitudes, 'col', pairs))]
    ppermute x2 -> x5, waiting for transfers between devices: 0.01 us -> 5.49 us  [the longest x1 5.48 us: gather_cols(): arrays.append(lax.ppermute(integrals, 'col', pairs))]
    ppermute x3, starting transfers between devices: 0.74 us -> 4.78 us  [shards(): amp_down = lax.ppermute(amp_down, 'row', behind)]
  transfers between devices with their start and end apart: 17 -> 20, of which waited for: 8 -> 7; matrix products, arithmetic and copies ran while one was open for 6% -> 3% of each run, Pallas kernels for 18% -> 14%
where the time goes in v3:
time: 71.2 us; the launch traced here: 70.9 us
  waiting for transfers between devices  31.3 us (44%)
  starting transfers between devices  19.8 us (28%)
  Pallas kernels  12.6 us (18%)
  local copies, waits for them, and re-layouts  6.48 us (9%)
    ppermute x4, waiting for transfers between devices, shards(): int_down = lax.ppermute(int_down, 'row', behind)  13 us
    pallas_call x3, Pallas kernels, step(): pl.pallas_call(functools.partial(step_kernel, hops, spots, ncol, nrow, sp...  9.93 us
    ppermute x4, starting transfers between devices, shards(): int_down = lax.ppermute(int_down, 'row', behind)  6.84 us
    ppermute x1, waiting for transfers between devices, gather_cols(): arrays.append(lax.ppermute(amplitudes, 'col', pairs))  6.12 us
    ppermute x3, waiting for transfers between devices, shards(): amp_down = lax.ppermute(amp_down, 'row', behind)  6.03 us
    ppermute x1, waiting for transfers between devices, gather_cols(): arrays.append(lax.ppermute(integrals, 'col', pairs))  5.48 us
    unnamed x22, local copies, waits for them, and re-layouts  5.27 us
    ppermute x3, starting transfers between devices, shards(): amp_down = lax.ppermute(amp_down, 'row', behind)  4.78 us
  transfers between devices with their start and end apart: 20, of which 7 were waited for; matrix products, arithmetic and copies ran while one was open for 3% of the time, Pallas kernels for 14%

profile of v3, /device:TPU:0, one launch (start us, length us, event | category | flops | bytes accessed | tf_op | source)
XLA Modules:
  0.0 70.9 jit_solution(6008402477312256037)
XLA Ops:
  0.0 3.0 %collective-permute-start = (bf16[256,768]{1,0:T(8,128)(2,1)}, bf16[256,768]{1,0:T(8,128)(2,1)S(1)}, u32[]{:S(2)}, u32[]{:S(2)}) collective-permute-start(bf16[256,768]{1,0:T(8,128)(2,1)} %refs_0_.5), channel_id=1, source_target_pairs={{0,2},{1,3},{2,0},{3,1},{4,6},{5,7},{6,4},{7,5},{8,10},{9,11},{10,... | collective-permute-start | bytes 1179656 | tf_op jit(solution)/shard_map/ppermute | solution.py:154
  3.0 0.0 collective-permute-start.1
  3.0 2.0 %collective-permute-start.10 = (bf16[256,768]{1,0:T(8,128)(2,1)}, bf16[256,768]{1,0:T(8,128)(2,1)S(1)}, u32[]{:S(2)}, u32[]{:S(2)}) collective-permute-start(bf16[256,768]{1,0:T(8,128)(2,1)} %refs_1_.5), channel_id=1, source_target_pairs={{8,0},{16,8},{24,16},{28,24},{20,28},{12,20},{4,12},{0,4},{9,1},{1... | collective-permute-start | bytes 1179656 | tf_op jit(solution)/shard_map/ppermute | solution.py:190
  5.0 1.6 %collective-permute-start.14 = (bf16[256,768]{1,0:T(8,128)(2,1)}, bf16[256,768]{1,0:T(8,128)(2,1)S(1)}, u32[]{:S(2)}, u32[]{:S(2)}) collective-permute-start(bf16[256,768]{1,0:T(8,128)(2,1)} %refs_0_.5), channel_id=1, source_target_pairs={{8,0},{16,8},{24,16},{28,24},{20,28},{12,20},{4,12},{0,4},{9,1},{1... | collective-permute-start | bytes 1179656 | tf_op jit(solution)/shard_map/ppermute | solution.py:193
  6.5 0.4 collective-permute-start.6
  7.0 6.1 %collective-permute-done.refs_2_ = bf16[256,768]{1,0:T(8,128)(2,1)S(1)} collective-permute-done((bf16[256,768]{1,0:T(8,128)(2,1)}, bf16[256,768]{1,0:T(8,128)(2,1)S(1)}, u32[]{:S(2)}, u32[]{:S(2)}) %collective-permute-start) | collective-permute-done | bytes 393248 | tf_op jit(solution)/shard_map/ppermute | solution.py:154
  13.1 2.1 %collective-permute-start.17 = (bf16[256,768]{1,0:T(8,128)(2,1)}, bf16[256,768]{1,0:T(8,128)(2,1)S(1)}, u32[]{:S(2)}, u32[]{:S(2)}) collective-permute-start(bf16[256,768]{1,0:T(8,128)(2,1)} %refs_1_.5), channel_id=1, source_target_pairs={{0,8},{8,16},{16,24},{24,28},{28,20},{20,12},{12,4},{4,0},{1,9},{9... | collective-permute-start | bytes 1179656 | tf_op jit(solution)/shard_map/ppermute | solution.py:192
  15.2 5.5 %collective-permute-done.1.refs_3_ = bf16[256,768]{1,0:T(8,128)(2,1)S(1)} collective-permute-done((bf16[256,768]{1,0:T(8,128)(2,1)}, bf16[256,768]{1,0:T(8,128)(2,1)S(1)}, u32[]{:S(2)}, u32[]{:S(2)}) %collective-permute-start.1) | collective-permute-done | bytes 393248 | tf_op jit(solution)/shard_map/ppermute | solution.py:155
  20.7 0.0 collective-permute-start.2
  20.7 0.0 collective-permute-done.10.refs_15_
  20.7 0.5 collective-permute-start.3
  21.2 1.0 %collective-permute-done.14.refs_10_ = bf16[256,768]{1,0:T(8,128)(2,1)S(1)} collective-permute-done((bf16[256,768]{1,0:T(8,128)(2,1)}, bf16[256,768]{1,0:T(8,128)(2,1)S(1)}, u32[]{:S(2)}, u32[]{:S(2)}) %collective-permute-start.14) | collective-permute-done | bytes 393248 | tf_op jit(solution)/shard_map/ppermute | solution.py:193
  22.3 1.6 %collective-permute-start.11 = (bf16[256,768]{1,0:T(8,128)(2,1)S(1)}, bf16[256,768]{1,0:T(8,128)(2,1)S(1)}, u32[]{:S(2)}, u32[]{:S(2)}) collective-permute-start(bf16[256,768]{1,0:T(8,128)(2,1)S(1)} %collective-permute-done.10.refs_15_), channel_id=1, source_target_pairs={{8,0},{16,8},{24,16},{28,24},{20,28},{12,20},{4,12},{0,4},{9,1},{1... | collective-permute-start | bytes 1179656 | tf_op jit(solution)/shard_map/ppermute | solution.py:190
  23.9 0.0 collective-permute-done.6.refs_9_
  23.9 0.4 collective-permute-start.7
  24.3 0.6 collective-permute-done.17.refs_14_
  24.9 0.0 collective-permute-start.4
  24.9 0.0 collective-permute-done.2.refs_4_
  24.9 1.6 %collective-permute-start.15 = (bf16[256,768]{1,0:T(8,128)(2,1)S(1)}, bf16[256,768]{1,0:T(8,128)(2,1)}, u32[]{:S(2)}, u32[]{:S(2)}) collective-permute-start(bf16[256,768]{1,0:T(8,128)(2,1)S(1)} %collective-permute-done.14.refs_10_), channel_id=1, source_target_pairs={{8,0},{16,8},{24,16},{28,24},{20,28},{12,20},{4,12},{0,4},{9,1},{1... | collective-permute-start | bytes 1179656 | tf_op jit(solution)/shard_map/ppermute | solution.py:193
  26.5 0.0 collective-permute-done.3.refs_5_
  26.5 0.5 collective-permute-start.18
  27.0 0.0 copy-start.2
  27.0 0.8 %copy-done.2 = bf16[256,768]{1,0:T(8,128)(2,1)} copy-done((bf16[256,768]{1,0:T(8,128)(2,1)}, bf16[256,768]{1,0:T(8,128)(2,1)S(1)}, u32[]{:S(2)}) %copy-start.2) | copy-done | bytes 393240
  27.7 6.6 %collective-permute-done.11.refs_17_ = bf16[256,768]{1,0:T(8,128)(2,1)S(1)} collective-permute-done((bf16[256,768]{1,0:T(8,128)(2,1)S(1)}, bf16[256,768]{1,0:T(8,128)(2,1)S(1)}, u32[]{:S(2)}, u32[]{:S(2)}) %collective-permute-start.11) | collective-permute-done | bytes 393248 | tf_op jit(solution)/shard_map/ppermute | solution.py:190
  34.3 1.6 %collective-permute-start.12 = (bf16[256,768]{1,0:T(8,128)(2,1)S(1)}, bf16[256,768]{1,0:T(8,128)(2,1)}, u32[]{:S(2)}, u32[]{:S(2)}) collective-permute-start(bf16[256,768]{1,0:T(8,128)(2,1)S(1)} %collective-permute-done.11.refs_17_), channel_id=1, source_target_pairs={{8,0},{16,8},{24,16},{28,24},{20,28},{12,20},{4,12},{0,4},{9,1},{1... | collective-permute-start | bytes 1179656 | tf_op jit(solution)/shard_map/ppermute | solution.py:190
  36.0 0.7 %copy-done.4 = bf16[256,768]{1,0:T(8,128)(2,1)} copy-done((bf16[256,768]{1,0:T(8,128)(2,1)}, bf16[256,768]{1,0:T(8,128)(2,1)S(1)}, u32[]{:S(2)}) %copy-start.4) | copy-done | bytes 393240
  36.7 0.0 collective-permute-done.7.refs_11_
  36.7 0.4 collective-permute-start.8
  37.1 0.8 %copy-done.6 = bf16[256,768]{1,0:T(8,128)(2,1)} copy-done((bf16[256,768]{1,0:T(8,128)(2,1)}, bf16[256,768]{1,0:T(8,128)(2,1)S(1)}, u32[]{:S(2)}) %copy-start.6) | copy-done | bytes 393240
  37.9 0.0 collective-permute-done.4.refs_6_
  37.9 0.0 collective-permute-start.5
  37.9 5.0 %collective-permute-done.15.refs_12_ = bf16[256,768]{1,0:T(8,128)(2,1)} collective-permute-done((bf16[256,768]{1,0:T(8,128)(2,1)S(1)}, bf16[256,768]{1,0:T(8,128)(2,1)}, u32[]{:S(2)}, u32[]{:S(2)}) %collective-permute-start.15) | collective-permute-done | bytes 393248 | tf_op jit(solution)/shard_map/ppermute | solution.py:193
  42.9 1.6 %collective-permute-start.16 = (bf16[256,768]{1,0:T(8,128)(2,1)}, bf16[256,768]{1,0:T(8,128)(2,1)}, u32[]{:S(2)}, u32[]{:S(2)}) collective-permute-start(bf16[256,768]{1,0:T(8,128)(2,1)} %collective-permute-done.15.refs_12_), channel_id=1, source_target_pairs={{8,0},{16,8},{24,16},{28,24},{20,28},{12,20},{4,12},{0,4},{9,1},{1... | collective-permute-start | bytes 1179656 | tf_op jit(solution)/shard_map/ppermute | solution.py:193
  44.5 0.0 collective-permute-done.18.refs_16_
  44.5 0.4 collective-permute-start.19
  44.9 6.4 %collective-permute-done.12.refs_11_ = bf16[256,768]{1,0:T(8,128)(2,1)} collective-permute-done((bf16[256,768]{1,0:T(8,128)(2,1)S(1)}, bf16[256,768]{1,0:T(8,128)(2,1)}, u32[]{:S(2)}, u32[]{:S(2)}) %collective-permute-start.12) | collective-permute-done | bytes 393248 | tf_op jit(solution)/shard_map/ppermute | solution.py:190
  51.3 1.6 %collective-permute-start.13 = (bf16[256,768]{1,0:T(8,128)(2,1)}, bf16[256,768]{1,0:T(8,128)(2,1)}, u32[]{:S(2)}, u32[]{:S(2)}) collective-permute-start(bf16[256,768]{1,0:T(8,128)(2,1)} %collective-permute-done.12.refs_11_), channel_id=1, source_target_pairs={{8,0},{16,8},{24,16},{28,24},{20,28},{12,20},{4,12},{0,4},{9,1},{1... | collective-permute-start | bytes 1179656 | tf_op jit(solution)/shard_map/ppermute | solution.py:190
  52.9 0.0 collective-permute-done.8.refs_8_
  52.9 0.4 collective-permute-start.9
  53.3 0.6 pad_add_fusion.where
  54.0 2.6 %slots.1.tab = s32[106]{0:T(128)} custom-call(s32[2]{0:T(128)} %pad_add_fusion.where, s32[64]{0:T(128)} %constant.13.clone.source, s32[8,64]{1,0:T(8,128)} %mask.1), custom_call_target="tpu_custom_call" | custom-call | tf_op jit(solution)/shard_map/slots/pallas_call | solution.py:68
  56.6 0.0 collective-permute-done.5.refs_7_
  56.6 0.0 copy-start
  56.6 0.0 copy-start.1
  56.6 0.0 copy-start.8
  56.7 0.0 copy-start.9
  56.7 0.0 copy-start.10
  56.7 1.2 %broadcast_in_dim.6.refs_18_ = bf16[32,128,128]{2,1,0:T(8,128)(2,1)} broadcast(bf16[]{:T(256)} %constant.12.clone.1), dimensions={} | broadcast | bytes 1048578 | tf_op jit(solution)/shard_map/broadcast_in_dim | solution.py:178
  57.9 0.0 copy-done
  57.9 0.0 copy-done.1
  57.9 0.0 copy-done.8
  57.9 0.0 copy-done.9
  57.9 0.0 copy-done.10
  57.9 0.0 copy-start.3
  57.9 1.0 %copy-done.3 = bf16[256,768]{1,0:T(8,128)(2,1)S(1)} copy-done((bf16[256,768]{1,0:T(8,128)(2,1)S(1)}, bf16[256,768]{1,0:T(8,128)(2,1)}, u32[]{:S(2)}) %copy-start.3) | copy-done | bytes 393240
  58.9 1.0 %copy-done.5 = bf16[256,768]{1,0:T(8,128)(2,1)S(1)} copy-done((bf16[256,768]{1,0:T(8,128)(2,1)S(1)}, bf16[256,768]{1,0:T(8,128)(2,1)}, u32[]{:S(2)}) %copy-start.5) | copy-done | bytes 393240
  59.9 1.0 %copy-done.7 = bf16[256,768]{1,0:T(8,128)(2,1)S(1)} copy-done((bf16[256,768]{1,0:T(8,128)(2,1)S(1)}, bf16[256,768]{1,0:T(8,128)(2,1)}, u32[]{:S(2)}) %copy-start.7) | copy-done | bytes 393240
  60.9 4.4 %blocks.3.refs_12_ = bf16[32,128,128]{2,1,0:T(8,128)(2,1)} custom-call(s32[106]{0:T(128)S(1)} %copy-done.9, f32[8]{0:T(128)S(1)} %copy-done.10, f32[8,128]{1,0:T(8,128)S(1)} %bitcast.4, bf16[256,768]{1,0:T(8,128)(2,1)S(1)} %copy-done, bf16[256,768]{1,0:T(8,128)(2,1)S(1)} %copy-done.1, ...), custom_call_target="tpu_custom_call", output_to_operand_aliasing={{}: (21, {})} | custom-call | flops 1006632960 | bytes 11796480 | tf_op jit(solution)/shard_map/blocks/pallas_call | solution.py:127
  65.3 0.0 collective-permute-done.16.refs_9_
  65.3 0.0 collective-permute-done.19.refs_10_
  65.3 3.1 %blocks.4.refs_10_ = bf16[32,128,128]{2,1,0:T(8,128)(2,1)} custom-call(s32[106]{0:T(128)S(1)} %copy-done.9, f32[8]{0:T(128)S(1)} %copy-done.10, f32[8,128]{1,0:T(8,128)S(1)} %bitcast.5, bf16[256,768]{1,0:T(8,128)(2,1)S(1)} %copy-done, bf16[256,768]{1,0:T(8,128)(2,1)S(1)} %copy-done.1, ...), custom_call_target="tpu_custom_call", output_to_operand_aliasing={{}: (15, {})} | custom-call | flops 402653184 | bytes 4718592 | tf_op jit(solution)/shard_map/blocks/pallas_call | solution.py:127
  68.5 0.0 collective-permute-done.13.refs_9_
  68.5 0.0 collective-permute-done.9.refs_8_
  68.5 2.4 %blocks.5 = bf16[32,128,128]{2,1,0:T(8,128)(2,1)} custom-call(s32[106]{0:T(128)S(1)} %copy-done.9, f32[8]{0:T(128)S(1)} %copy-done.10, f32[8,128]{1,0:T(8,128)S(1)} %bitcast.6, bf16[256,768]{1,0:T(8,128)(2,1)S(1)} %copy-done, bf16[256,768]{1,0:T(8,128)(2,1)S(1)} %copy-done.1, ...), custom_call_target="tpu_custom_call", output_to_operand_aliasing={{}: (13, {})} | custom-call | flops 201326592 | bytes 2359296 | tf_op jit(solution)/shard_map/blocks/pallas_call | solution.py:127
  (4 shorter events, 0.0 us)
Async XLA Ops:
  0.0 13.1 %collective-permute-start = (bf16[256,768]{1,0:T(8,128)(2,1)}, bf16[256,768]{1,0:T(8,128)(2,1)S(1)}, u32[]{:S(2)}, u32[]{:S(2)}) collective-permute-start(bf16[256,768]{1,0:T(8,128)(2,1)} %refs_0_.5), channel_id=1, source_target_pairs={{0,2},{1,3},{2,0},{3,1},{4,6},{5,7},{6,4},{7,5},{8,10},{9,11},{10,... | collective-permute-start | bytes 1179656 | tf_op jit(solution)/shard_map/ppermute | solution.py:154
  3.0 17.7 %collective-permute-start.1 = (bf16[256,768]{1,0:T(8,128)(2,1)}, bf16[256,768]{1,0:T(8,128)(2,1)S(1)}, u32[]{:S(2)}, u32[]{:S(2)}) collective-permute-start(bf16[256,768]{1,0:T(8,128)(2,1)} %refs_1_.5), channel_id=1, source_target_pairs={{0,2},{1,3},{2,0},{3,1},{4,6},{5,7},{6,4},{7,5},{8,10},{9,11},{10,... | collective-permute-start | bytes 1179656 | tf_op jit(solution)/shard_map/ppermute | solution.py:155
  3.0 17.7 %collective-permute-start.10 = (bf16[256,768]{1,0:T(8,128)(2,1)}, bf16[256,768]{1,0:T(8,128)(2,1)S(1)}, u32[]{:S(2)}, u32[]{:S(2)}) collective-permute-start(bf16[256,768]{1,0:T(8,128)(2,1)} %refs_1_.5), channel_id=1, source_target_pairs={{8,0},{16,8},{24,16},{28,24},{20,28},{12,20},{4,12},{0,4},{9,1},{1... | collective-permute-start | bytes 1179656 | tf_op jit(solution)/shard_map/ppermute | solution.py:190
  5.0 17.3 %collective-permute-start.14 = (bf16[256,768]{1,0:T(8,128)(2,1)}, bf16[256,768]{1,0:T(8,128)(2,1)S(1)}, u32[]{:S(2)}, u32[]{:S(2)}) collective-permute-start(bf16[256,768]{1,0:T(8,128)(2,1)} %refs_0_.5), channel_id=1, source_target_pairs={{8,0},{16,8},{24,16},{28,24},{20,28},{12,20},{4,12},{0,4},{9,1},{1... | collective-permute-start | bytes 1179656 | tf_op jit(solution)/shard_map/ppermute | solution.py:193
  6.5 17.4 %collective-permute-start.6 = (bf16[256,768]{1,0:T(8,128)(2,1)}, bf16[256,768]{1,0:T(8,128)(2,1)S(1)}, u32[]{:S(2)}, u32[]{:S(2)}) collective-permute-start(bf16[256,768]{1,0:T(8,128)(2,1)} %refs_0_.5), channel_id=1, source_target_pairs={{0,8},{8,16},{16,24},{24,28},{28,20},{20,12},{12,4},{4,0},{1,9},{9... | collective-permute-start | bytes 1179656 | tf_op jit(solution)/shard_map/ppermute | solution.py:189
  13.1 11.8 %collective-permute-start.17 = (bf16[256,768]{1,0:T(8,128)(2,1)}, bf16[256,768]{1,0:T(8,128)(2,1)S(1)}, u32[]{:S(2)}, u32[]{:S(2)}) collective-permute-start(bf16[256,768]{1,0:T(8,128)(2,1)} %refs_1_.5), channel_id=1, source_target_pairs={{0,8},{8,16},{16,24},{24,28},{28,20},{20,12},{12,4},{4,0},{1,9},{9... | collective-permute-start | bytes 1179656 | tf_op jit(solution)/shard_map/ppermute | solution.py:192
  20.7 4.2 %collective-permute-start.2 = (bf16[256,768]{1,0:T(8,128)(2,1)}, bf16[256,768]{1,0:T(8,128)(2,1)S(1)}, u32[]{:S(2)}, u32[]{:S(2)}) collective-permute-start(bf16[256,768]{1,0:T(8,128)(2,1)} %refs_0_.5), channel_id=1, source_target_pairs={{0,1},{1,0},{2,3},{3,2},{4,5},{5,4},{6,7},{7,6},{8,9},{9,8},{10,11... | collective-permute-start | bytes 1179656 | tf_op jit(solution)/shard_map/ppermute | solution.py:158
  20.7 5.8 %collective-permute-start.3 = (bf16[256,768]{1,0:T(8,128)(2,1)}, bf16[256,768]{1,0:T(8,128)(2,1)S(1)}, u32[]{:S(2)}, u32[]{:S(2)}) collective-permute-start(bf16[256,768]{1,0:T(8,128)(2,1)} %refs_1_.5), channel_id=1, source_target_pairs={{0,1},{1,0},{2,3},{3,2},{4,5},{5,4},{6,7},{7,6},{8,9},{9,8},{10,11... | collective-permute-start | bytes 1179656 | tf_op jit(solution)/shard_map/ppermute | solution.py:158
  22.3 12.1 %collective-permute-start.11 = (bf16[256,768]{1,0:T(8,128)(2,1)S(1)}, bf16[256,768]{1,0:T(8,128)(2,1)S(1)}, u32[]{:S(2)}, u32[]{:S(2)}) collective-permute-start(bf16[256,768]{1,0:T(8,128)(2,1)S(1)} %collective-permute-done.10.refs_15_), channel_id=1, source_target_pairs={{8,0},{16,8},{24,16},{28,24},{20,28},{12,20},{4,12},{0,4},{9,1},{1... | collective-permute-start | bytes 1179656 | tf_op jit(solution)/shard_map/ppermute | solution.py:190
  23.9 12.8 %collective-permute-start.7 = (bf16[256,768]{1,0:T(8,128)(2,1)S(1)}, bf16[256,768]{1,0:T(8,128)(2,1)S(1)}, u32[]{:S(2)}, u32[]{:S(2)}) collective-permute-start(bf16[256,768]{1,0:T(8,128)(2,1)S(1)} %collective-permute-done.6.refs_9_), channel_id=1, source_target_pairs={{0,8},{8,16},{16,24},{24,28},{28,20},{20,12},{12,4},{4,0},{1,9},{9... | collective-permute-start | bytes 1179656 | tf_op jit(solution)/shard_map/ppermute | solution.py:189
  24.9 13.0 %collective-permute-start.4 = (bf16[256,768]{1,0:T(8,128)(2,1)S(1)}, bf16[256,768]{1,0:T(8,128)(2,1)S(1)}, u32[]{:S(2)}, u32[]{:S(2)}) collective-permute-start(bf16[256,768]{1,0:T(8,128)(2,1)S(1)} %collective-permute-done.refs_2_), channel_id=1, source_target_pairs={{0,1},{1,0},{2,3},{3,2},{4,5},{5,4},{6,7},{7,6},{8,9},{9,8},{10,11... | collective-permute-start | bytes 1179656 | tf_op jit(solution)/shard_map/ppermute | solution.py:158
  24.9 17.9 %collective-permute-start.15 = (bf16[256,768]{1,0:T(8,128)(2,1)S(1)}, bf16[256,768]{1,0:T(8,128)(2,1)}, u32[]{:S(2)}, u32[]{:S(2)}) collective-permute-start(bf16[256,768]{1,0:T(8,128)(2,1)S(1)} %collective-permute-done.14.refs_10_), channel_id=1, source_target_pairs={{8,0},{16,8},{24,16},{28,24},{20,28},{12,20},{4,12},{0,4},{9,1},{1... | collective-permute-start | bytes 1179656 | tf_op jit(solution)/shard_map/ppermute | solution.py:193
  26.5 18.0 %collective-permute-start.18 = (bf16[256,768]{1,0:T(8,128)(2,1)S(1)}, bf16[256,768]{1,0:T(8,128)(2,1)}, u32[]{:S(2)}, u32[]{:S(2)}) collective-permute-start(bf16[256,768]{1,0:T(8,128)(2,1)S(1)} %collective-permute-done.17.refs_14_), channel_id=1, source_target_pairs={{0,8},{8,16},{16,24},{24,28},{28,20},{20,12},{12,4},{4,0},{1,9},{9... | collective-permute-start | bytes 1179656 | tf_op jit(solution)/shard_map/ppermute | solution.py:192
  27.0 0.8 %copy-start.2 = (bf16[256,768]{1,0:T(8,128)(2,1)}, bf16[256,768]{1,0:T(8,128)(2,1)S(1)}, u32[]{:S(2)}) copy-start(bf16[256,768]{1,0:T(8,128)(2,1)S(1)} %collective-permute-done.17.refs_14_) | copy-start | bytes 1179652
  34.3 17.0 %collective-permute-start.12 = (bf16[256,768]{1,0:T(8,128)(2,1)S(1)}, bf16[256,768]{1,0:T(8,128)(2,1)}, u32[]{:S(2)}, u32[]{:S(2)}) collective-permute-start(bf16[256,768]{1,0:T(8,128)(2,1)S(1)} %collective-permute-done.11.refs_17_), channel_id=1, source_target_pairs={{8,0},{16,8},{24,16},{28,24},{20,28},{12,20},{4,12},{0,4},{9,1},{1... | collective-permute-start | bytes 1179656 | tf_op jit(solution)/shard_map/ppermute | solution.py:190
  36.0 0.7 %copy-start.4 = (bf16[256,768]{1,0:T(8,128)(2,1)}, bf16[256,768]{1,0:T(8,128)(2,1)S(1)}, u32[]{:S(2)}) copy-start(bf16[256,768]{1,0:T(8,128)(2,1)S(1)} %collective-permute-done.11.refs_17_) | copy-start | bytes 1179652
  36.7 16.2 %collective-permute-start.8 = (bf16[256,768]{1,0:T(8,128)(2,1)S(1)}, bf16[256,768]{1,0:T(8,128)(2,1)}, u32[]{:S(2)}, u32[]{:S(2)}) collective-permute-start(bf16[256,768]{1,0:T(8,128)(2,1)S(1)} %collective-permute-done.7.refs_11_), channel_id=1, source_target_pairs={{0,8},{8,16},{16,24},{24,28},{28,20},{20,12},{12,4},{4,0},{1,9},{9... | collective-permute-start | bytes 1179656 | tf_op jit(solution)/shard_map/ppermute | solution.py:189
  37.1 0.8 %copy-start.6 = (bf16[256,768]{1,0:T(8,128)(2,1)}, bf16[256,768]{1,0:T(8,128)(2,1)S(1)}, u32[]{:S(2)}) copy-start(bf16[256,768]{1,0:T(8,128)(2,1)S(1)} %collective-permute-done.7.refs_11_) | copy-start | bytes 1179652
  37.9 18.7 %collective-permute-start.5 = (bf16[256,768]{1,0:T(8,128)(2,1)S(1)}, bf16[256,768]{1,0:T(8,128)(2,1)S(1)}, u32[]{:S(2)}, u32[]{:S(2)}) collective-permute-start(bf16[256,768]{1,0:T(8,128)(2,1)S(1)} %collective-permute-done.1.refs_3_), channel_id=1, source_target_pairs={{0,1},{1,0},{2,3},{3,2},{4,5},{5,4},{6,7},{7,6},{8,9},{9,8},{10,11... | collective-permute-start | bytes 1179656 | tf_op jit(solution)/shard_map/ppermute | solution.py:158
  42.9 22.4 %collective-permute-start.16 = (bf16[256,768]{1,0:T(8,128)(2,1)}, bf16[256,768]{1,0:T(8,128)(2,1)}, u32[]{:S(2)}, u32[]{:S(2)}) collective-permute-start(bf16[256,768]{1,0:T(8,128)(2,1)} %collective-permute-done.15.refs_12_), channel_id=1, source_target_pairs={{8,0},{16,8},{24,16},{28,24},{20,28},{12,20},{4,12},{0,4},{9,1},{1... | collective-permute-start | bytes 1179656 | tf_op jit(solution)/shard_map/ppermute | solution.py:193
  44.5 20.8 %collective-permute-start.19 = (bf16[256,768]{1,0:T(8,128)(2,1)}, bf16[256,768]{1,0:T(8,128)(2,1)}, u32[]{:S(2)}, u32[]{:S(2)}) collective-permute-start(bf16[256,768]{1,0:T(8,128)(2,1)} %collective-permute-done.18.refs_16_), channel_id=1, source_target_pairs={{0,8},{8,16},{16,24},{24,28},{28,20},{20,12},{12,4},{4,0},{1,9},{9... | collective-permute-start | bytes 1179656 | tf_op jit(solution)/shard_map/ppermute | solution.py:192
  51.3 17.2 %collective-permute-start.13 = (bf16[256,768]{1,0:T(8,128)(2,1)}, bf16[256,768]{1,0:T(8,128)(2,1)}, u32[]{:S(2)}, u32[]{:S(2)}) collective-permute-start(bf16[256,768]{1,0:T(8,128)(2,1)} %collective-permute-done.12.refs_11_), channel_id=1, source_target_pairs={{8,0},{16,8},{24,16},{28,24},{20,28},{12,20},{4,12},{0,4},{9,1},{1... | collective-permute-start | bytes 1179656 | tf_op jit(solution)/shard_map/ppermute | solution.py:190
  52.9 15.6 %collective-permute-start.9 = (bf16[256,768]{1,0:T(8,128)(2,1)}, bf16[256,768]{1,0:T(8,128)(2,1)}, u32[]{:S(2)}, u32[]{:S(2)}) collective-permute-start(bf16[256,768]{1,0:T(8,128)(2,1)} %collective-permute-done.8.refs_8_), channel_id=1, source_target_pairs={{0,8},{8,16},{16,24},{24,28},{28,20},{20,12},{12,4},{4,0},{1,9},{9... | collective-permute-start | bytes 1179656 | tf_op jit(solution)/shard_map/ppermute | solution.py:189
  56.6 1.3 %copy-start = (bf16[256,768]{1,0:T(8,128)(2,1)S(1)}, bf16[256,768]{1,0:T(8,128)(2,1)}, u32[]{:S(2)}) copy-start(bf16[256,768]{1,0:T(8,128)(2,1)} %refs_0_.5) | copy-start | bytes 1179652
  56.6 1.3 %copy-start.1 = (bf16[256,768]{1,0:T(8,128)(2,1)S(1)}, bf16[256,768]{1,0:T(8,128)(2,1)}, u32[]{:S(2)}) copy-start(bf16[256,768]{1,0:T(8,128)(2,1)} %refs_1_.5) | copy-start | bytes 1179652
  56.6 1.3 %copy-start.8 = (f32[1024]{0:T(1024)S(1)}, f32[1024]{0:T(1024)}, u32[]{:S(2)}) copy-start(f32[1024]{0:T(1024)} %param.10) | copy-start | bytes 12292
  56.7 1.2 %copy-start.9 = (s32[106]{0:T(128)S(1)}, s32[106]{0:T(128)}, u32[]{:S(2)}) copy-start(s32[106]{0:T(128)} %slots.1.tab) | copy-start | bytes 1276
  56.7 1.2 %copy-start.10 = (f32[8]{0:T(128)S(1)}, f32[8]{0:T(128)}, u32[]{:S(2)}) copy-start(f32[8]{0:T(128)} %occ.5) | copy-start | bytes 100
  57.9 1.0 %copy-start.3 = (bf16[256,768]{1,0:T(8,128)(2,1)S(1)}, bf16[256,768]{1,0:T(8,128)(2,1)}, u32[]{:S(2)}) copy-start(bf16[256,768]{1,0:T(8,128)(2,1)} %copy-done.2) | copy-start | bytes 1179652
  58.9 1.0 %copy-start.5 = (bf16[256,768]{1,0:T(8,128)(2,1)S(1)}, bf16[256,768]{1,0:T(8,128)(2,1)}, u32[]{:S(2)}) copy-start(bf16[256,768]{1,0:T(8,128)(2,1)} %copy-done.4) | copy-start | bytes 1179652
  59.9 1.0 %copy-start.7 = (bf16[256,768]{1,0:T(8,128)(2,1)S(1)}, bf16[256,768]{1,0:T(8,128)(2,1)}, u32[]{:S(2)}) copy-start(bf16[256,768]{1,0:T(8,128)(2,1)} %copy-done.6) | copy-start | bytes 1179652

commit v4 on v3

--- a/solution.py
+++ b/solution.py
@@ -27,7 +27,7 @@
     return walk
 
 
-def table_kernel(ncol, nrow, split, where, source, mask, tab):
+def table_kernel(ncol, nrow, split, where, source, mask, tab, empty):
     cells = ncol * nrow
     row_at, col_at = where[0], where[1]
     for s in range(nrow):
@@ -62,14 +62,24 @@
 
     lax.fori_loop(0, ncol * split, rows, jnp.int32(0))
 
-
-def slot_table(where, source, mask, ncol, nrow, split):
+    def blank(slot, carry):
+        empty[slot] = jnp.zeros((BLOCK, BLOCK), empty.dtype)
+        return carry
+
+    lax.fori_loop(0, empty.shape[0], blank, 0)
+
+
+def slot_table(where, source, mask, ncol, nrow, split, limit):
     smem = pl.BlockSpec(memory_space=pltpu.SMEM)
     return pl.pallas_call(
         functools.partial(table_kernel, ncol, nrow, split),
         in_specs=[smem, smem, smem],
-        out_specs=smem,
-        out_shape=jax.ShapeDtypeStruct((3 * ncol * nrow + nrow + 2,), jnp.int32),
+        out_specs=(smem, pl.BlockSpec(memory_space=pltpu.VMEM)),
+        out_shape=(
+            jax.ShapeDtypeStruct((3 * ncol * nrow + nrow + 2,), jnp.int32),
+            jax.ShapeDtypeStruct((limit, BLOCK, BLOCK), jnp.bfloat16),
+        ),
+        compiler_params=pltpu.CompilerParams(vmem_limit_bytes=2 * limit * BLOCK * BLOCK + (4 << 20)),
         name="slots",
     )(where, source, mask)
 
@@ -162,6 +172,10 @@
     return arrays, spots
 
 
+def after(x, gate):
+    return x if gate is None else lax.optimization_barrier((x, gate))[0]
+
+
 def shards(amplitudes, integrals, block_mask, occ_energy, vir_energy):
     nrow = lax.axis_size("row")
     ncol = lax.axis_size("col")
@@ -173,9 +187,8 @@
     source = np.array([order[(spot[row] - s) % nrow] for row in range(nrow) for s in range(nrow)], np.int32)
     ahead = [(order[p], order[(p + 1) % nrow]) for p in range(nrow)]
     behind = [(b, a) for a, b in ahead]
-    tab = slot_table(where, source, block_mask, ncol, nrow, split)
+    tab, out = slot_table(where, source, block_mask, ncol, nrow, split, limit)
     vir = vir_energy.reshape(-1, BLOCK)
-    out = jnp.zeros((limit, BLOCK, BLOCK), jnp.bfloat16)
 
     def update(hops, amp_b, int_b, out):
         return step(hops, spots, tab, occ_energy, vir, row_shards, amp_b, int_b, out, ncol, nrow, split)
@@ -186,8 +199,9 @@
     waiting = []
     for s in range(1, far + 1):
         last = (amp_up, amp_down, int_up, int_down)
-        amp_up = lax.ppermute(amp_up, "row", ahead)
-        int_down = lax.ppermute(int_down, "row", behind)
+        gate = tab if s == 2 else None
+        amp_up = lax.ppermute(after(amp_up, gate), "row", ahead)
+        int_down = lax.ppermute(after(int_down, gate), "row", behind)
         if s < nrow - s:
             int_up = lax.ppermute(int_up, "row", ahead)
             amp_down = lax.ppermute(amp_down, "row", behind)

time: 71.2 us -> 68.8 us (0.966)
  local copies, waits for them, and re-layouts: 6.48 us -> 3.24 us
  waiting for transfers between devices: 31.3 us -> 34.3 us
  Pallas kernels: 12.6 us -> 11.1 us
    ppermute x8, waiting for transfers between devices: 13 us -> 23.6 us  [the longest x4 22.6 us: shards(): int_down = lax.ppermute(after(int_down, gate), 'row', behind)]
    ppermute x1, waiting for transfers between devices: 6.12 us -> 0.04 us  [gather_cols(): arrays.append(lax.ppermute(amplitudes, 'col', pairs))]
    ppermute x1, waiting for transfers between devices: 5.48 us -> 2.66 us  [gather_cols(): arrays.append(lax.ppermute(integrals, 'col', pairs))]
    unnamed x22 -> x16, local copies, waits for them, and re-layouts: 5.27 us -> 3.24 us
    pallas_call x3, Pallas kernels: 9.93 us -> 7.92 us  [step(): pl.pallas_call(functools.partial(step_kernel, hops, spots, ncol, nrow, sp...]
    broadcast_in_dim x1 -> x0, local copies, waits for them, and re-layouts: 1.21 us -> none  [shards(): out = jnp.zeros((limit, BLOCK, BLOCK), jnp.bfloat16)]
    ppermute x1, starting transfers between devices: 2.97 us -> 1.97 us  [gather_cols(): arrays.append(lax.ppermute(amplitudes, 'col', pairs))]
    ppermute x3, waiting for transfers between devices: 0.62 us -> 1.59 us  [shards(): int_up = lax.ppermute(int_up, 'row', ahead)]
  transfers between devices with their start and end apart: 20 -> 20, of which waited for: 7 -> 8; matrix products, arithmetic and copies ran while one was open for 3% -> 0% of each run, Pallas kernels for 14% -> 14%
where the time goes in v4:
time: 68.8 us; the launch traced here: 68.5 us
  waiting for transfers between devices  34.3 us (50%)
  starting transfers between devices  19.7 us (29%)
  Pallas kernels  11.1 us (16%)
  local copies, waits for them, and re-layouts  3.24 us (5%)
    ppermute x4, waiting for transfers between devices, shards(): int_down = lax.ppermute(after(int_down, gate), 'row', behind)  22.6 us
    pallas_call x3, Pallas kernels, step(): pl.pallas_call(functools.partial(step_kernel, hops, spots, ncol, nrow, sp...  7.92 us
    ppermute x4, starting transfers between devices, shards(): int_down = lax.ppermute(after(int_down, gate), 'row', behind)  7.87 us
    ppermute x3, waiting for transfers between devices, shards(): amp_down = lax.ppermute(amp_down, 'row', behind)  6.39 us
    ppermute x3, starting transfers between devices, shards(): amp_down = lax.ppermute(amp_down, 'row', behind)  5.28 us
    unnamed x16, local copies, waits for them, and re-layouts  3.24 us
    pallas_call x1, Pallas kernels, slot_table(): pl.pallas_call(functools.partial(table_kernel, ncol, nrow, split), in_spe...  3.16 us
    ppermute x3, starting transfers between devices, shards(): int_up = lax.ppermute(int_up, 'row', ahead)  2.83 us
  transfers between devices with their start and end apart: 20, of which 8 were waited for; matrix products, arithmetic and copies ran while one was open for 0% of the time, Pallas kernels for 14%

profile of v4, /device:TPU:0, one launch (start us, length us, event | category | flops | bytes accessed | tf_op | source)
XLA Modules:
  0.0 68.5 jit_solution(15767355765983240012)
XLA Ops:
  0.0 2.9 %collective-permute-start.10 = (bf16[256,768]{1,0:T(8,128)(2,1)}, bf16[256,768]{1,0:T(8,128)(2,1)S(1)}, u32[]{:S(2)}, u32[]{:S(2)}) collective-permute-start(bf16[256,768]{1,0:T(8,128)(2,1)} %refs_1_.5), channel_id=1, source_target_pairs={{8,0},{16,8},{24,16},{28,24},{20,28},{12,20},{4,12},{0,4},{9,1},{1... | collective-permute-start | bytes 1179656 | tf_op jit(solution)/shard_map/ppermute | solution.py:204
  2.9 0.1 collective-permute-start.6
  3.0 2.0 %collective-permute-start = (bf16[256,768]{1,0:T(8,128)(2,1)}, bf16[256,768]{1,0:T(8,128)(2,1)S(1)}, u32[]{:S(2)}, u32[]{:S(2)}) collective-permute-start(bf16[256,768]{1,0:T(8,128)(2,1)} %refs_0_.5), channel_id=1, source_target_pairs={{0,2},{1,3},{2,0},{3,1},{4,6},{5,7},{6,4},{7,5},{8,10},{9,11},{10,... | collective-permute-start | bytes 1179656 | tf_op jit(solution)/shard_map/ppermute | solution.py:164
  5.0 0.1 collective-permute-start.1
  5.1 1.9 %collective-permute-start.14 = (bf16[256,768]{1,0:T(8,128)(2,1)}, bf16[256,768]{1,0:T(8,128)(2,1)S(1)}, u32[]{:S(2)}, u32[]{:S(2)}) collective-permute-start(bf16[256,768]{1,0:T(8,128)(2,1)} %refs_0_.5), channel_id=1, source_target_pairs={{8,0},{16,8},{24,16},{28,24},{20,28},{12,20},{4,12},{0,4},{9,1},{1... | collective-permute-start | bytes 1179656 | tf_op jit(solution)/shard_map/ppermute | solution.py:207
  7.0 6.2 %collective-permute-done.10.refs_15_ = bf16[256,768]{1,0:T(8,128)(2,1)S(1)} collective-permute-done((bf16[256,768]{1,0:T(8,128)(2,1)}, bf16[256,768]{1,0:T(8,128)(2,1)S(1)}, u32[]{:S(2)}, u32[]{:S(2)}) %collective-permute-start.10) | collective-permute-done | bytes 393248 | tf_op jit(solution)/shard_map/ppermute | solution.py:204
  13.2 2.1 %collective-permute-start.17 = (bf16[256,768]{1,0:T(8,128)(2,1)}, bf16[256,768]{1,0:T(8,128)(2,1)S(1)}, u32[]{:S(2)}, u32[]{:S(2)}) collective-permute-start(bf16[256,768]{1,0:T(8,128)(2,1)} %refs_1_.5), channel_id=1, source_target_pairs={{0,8},{8,16},{16,24},{24,28},{28,20},{20,12},{12,4},{4,0},{1,9},{9... | collective-permute-start | bytes 1179656 | tf_op jit(solution)/shard_map/ppermute | solution.py:206
  15.2 0.0 copy-start.6
  15.2 0.0 collective-permute-done.6.refs_9_
  15.2 0.0 collective-permute-start.2
  15.2 0.0 collective-permute-done.refs_2_
  15.3 0.5 collective-permute-start.3
  15.8 0.0 copy-start.7
  15.8 0.1 pad_add_fusion.where
  15.8 0.1 copy-done.6
  15.9 0.5 copy-done.7
  16.4 3.2 %slots.1 = (s32[106]{0:T(128)S(1)}, bf16[32,128,128]{2,1,0:T(8,128)(2,1)}) custom-call(s32[2]{0:T(128)S(1)} %pad_add_fusion.where, s32[64]{0:T(128)S(1)} %copy-done.7, s32[8,64]{1,0:T(8,128)S(1)} %copy-done.6), custom_call_target="tpu_custom_call" | custom-call | tf_op jit(solution)/shard_map/slots/pallas_call | solution.py:74
  19.6 0.0 copy-start.4
  19.6 2.7 %collective-permute-done.1.refs_3_ = bf16[256,768]{1,0:T(8,128)(2,1)S(1)} collective-permute-done((bf16[256,768]{1,0:T(8,128)(2,1)}, bf16[256,768]{1,0:T(8,128)(2,1)S(1)}, u32[]{:S(2)}, u32[]{:S(2)}) %collective-permute-start.1) | collective-permute-done | bytes 393248 | tf_op jit(solution)/shard_map/ppermute | solution.py:165
  22.3 1.6 %collective-permute-start.11 = (bf16[256,768]{1,0:T(8,128)(2,1)S(1)}, bf16[256,768]{1,0:T(8,128)(2,1)S(1)}, u32[]{:S(2)}, u32[]{:S(2)}) collective-permute-start(bf16[256,768]{1,0:T(8,128)(2,1)S(1)} %collective-permute-done.10.refs_15_), channel_id=1, source_target_pairs={{8,0},{16,8},{24,16},{28,24},{20,28},{12,20},{4,12},{0,4},{9,1},{1... | collective-permute-start | bytes 1179656 | tf_op jit(solution)/shard_map/ppermute | solution.py:204
  23.9 0.0 collective-permute-done.14.refs_10_
  23.9 0.4 collective-permute-start.7
  24.3 0.0 collective-permute-done.17.refs_14_
  24.3 0.0 collective-permute-start.4
  24.3 0.0 collective-permute-done.2.refs_4_
  24.3 1.7 %collective-permute-start.15 = (bf16[256,768]{1,0:T(8,128)(2,1)S(1)}, bf16[256,768]{1,0:T(8,128)(2,1)S(1)}, u32[]{:S(2)}, u32[]{:S(2)}) collective-permute-start(bf16[256,768]{1,0:T(8,128)(2,1)S(1)} %collective-permute-done.14.refs_10_), channel_id=1, source_target_pairs={{8,0},{16,8},{24,16},{28,24},{20,28},{12,20},{4,12},{0,4},{9,1},{1... | collective-permute-start | bytes 1179656 | tf_op jit(solution)/shard_map/ppermute | solution.py:207
  26.0 0.0 collective-permute-done.3.refs_5_
  26.0 0.4 collective-permute-start.18
  26.4 7.9 %collective-permute-done.11.refs_17_ = bf16[256,768]{1,0:T(8,128)(2,1)S(1)} collective-permute-done((bf16[256,768]{1,0:T(8,128)(2,1)S(1)}, bf16[256,768]{1,0:T(8,128)(2,1)S(1)}, u32[]{:S(2)}, u32[]{:S(2)}) %collective-permute-start.11) | collective-permute-done | bytes 393248 | tf_op jit(solution)/shard_map/ppermute | solution.py:204
  34.3 1.6 %collective-permute-start.12 = (bf16[256,768]{1,0:T(8,128)(2,1)S(1)}, bf16[256,768]{1,0:T(8,128)(2,1)S(1)}, u32[]{:S(2)}, u32[]{:S(2)}) collective-permute-start(bf16[256,768]{1,0:T(8,128)(2,1)S(1)} %collective-permute-done.11.refs_17_), channel_id=1, source_target_pairs={{8,0},{16,8},{24,16},{28,24},{20,28},{12,20},{4,12},{0,4},{9,1},{1... | collective-permute-start | bytes 1179656 | tf_op jit(solution)/shard_map/ppermute | solution.py:204
  36.0 0.0 collective-permute-done.7.refs_11_
  36.0 0.4 collective-permute-start.8
  36.3 0.0 collective-permute-done.4.refs_6_
  36.3 0.0 collective-permute-start.5
  36.3 6.4 %collective-permute-done.15.refs_12_ = bf16[256,768]{1,0:T(8,128)(2,1)S(1)} collective-permute-done((bf16[256,768]{1,0:T(8,128)(2,1)S(1)}, bf16[256,768]{1,0:T(8,128)(2,1)S(1)}, u32[]{:S(2)}, u32[]{:S(2)}) %collective-permute-start.15) | collective-permute-done | bytes 393248 | tf_op jit(solution)/shard_map/ppermute | solution.py:207
  42.7 1.6 %collective-permute-start.16 = (bf16[256,768]{1,0:T(8,128)(2,1)S(1)}, bf16[256,768]{1,0:T(8,128)(2,1)S(1)}, u32[]{:S(2)}, u32[]{:S(2)}) collective-permute-start(bf16[256,768]{1,0:T(8,128)(2,1)S(1)} %collective-permute-done.15.refs_12_), channel_id=1, source_target_pairs={{8,0},{16,8},{24,16},{28,24},{20,28},{12,20},{4,12},{0,4},{9,1},{1... | collective-permute-start | bytes 1179656 | tf_op jit(solution)/shard_map/ppermute | solution.py:207
  44.4 0.0 collective-permute-done.18.refs_16_
  44.4 0.4 collective-permute-start.19
  44.8 6.4 %collective-permute-done.12.refs_11_ = bf16[256,768]{1,0:T(8,128)(2,1)S(1)} collective-permute-done((bf16[256,768]{1,0:T(8,128)(2,1)S(1)}, bf16[256,768]{1,0:T(8,128)(2,1)S(1)}, u32[]{:S(2)}, u32[]{:S(2)}) %collective-permute-start.12) | collective-permute-done | bytes 393248 | tf_op jit(solution)/shard_map/ppermute | solution.py:204
  51.2 1.6 %collective-permute-start.13 = (bf16[256,768]{1,0:T(8,128)(2,1)S(1)}, bf16[256,768]{1,0:T(8,128)(2,1)S(1)}, u32[]{:S(2)}, u32[]{:S(2)}) collective-permute-start(bf16[256,768]{1,0:T(8,128)(2,1)S(1)} %collective-permute-done.12.refs_11_), channel_id=1, source_target_pairs={{8,0},{16,8},{24,16},{28,24},{20,28},{12,20},{4,12},{0,4},{9,1},{1... | collective-permute-start | bytes 1179656 | tf_op jit(solution)/shard_map/ppermute | solution.py:204
  52.8 0.0 collective-permute-done.8.refs_8_
  52.8 0.4 collective-permute-start.9
  53.2 0.0 collective-permute-done.5.refs_7_
  53.2 0.0 copy-start.5
  53.2 0.0 copy-done.4
  53.2 0.7 copy-done.5
  53.9 0.0 copy-start
  53.9 1.0 %copy-done = bf16[256,768]{1,0:T(8,128)(2,1)S(1)} copy-done((bf16[256,768]{1,0:T(8,128)(2,1)S(1)}, bf16[256,768]{1,0:T(8,128)(2,1)}, u32[]{:S(2)}) %copy-start) | copy-done | bytes 393240
  54.8 0.0 copy-start.2
  54.8 1.0 %copy-done.2 = bf16[256,768]{1,0:T(8,128)(2,1)S(1)} copy-done((bf16[256,768]{1,0:T(8,128)(2,1)S(1)}, bf16[256,768]{1,0:T(8,128)(2,1)}, u32[]{:S(2)}) %copy-start.2) | copy-done | bytes 393240
  55.8 0.0 copy-start.1
  55.8 0.0 copy-start.3
  55.8 3.8 %blocks.3.refs_12_ = bf16[32,128,128]{2,1,0:T(8,128)(2,1)} custom-call(s32[106]{0:T(128)S(1)} %get-tuple-element.9.tab, f32[8]{0:T(128)S(1)} %copy-done.5, f32[8,128]{1,0:T(8,128)S(1)} %bitcast.4, bf16[256,768]{1,0:T(8,128)(2,1)S(1)} %copy-done, bf16[256,768]{1,0:T(8,128)(2,1)S(1)} %copy-done.2, ...), custom_call_target="tpu_custom_call", output_to_operand_aliasing={{}: (21, {})} | custom-call | flops 1006632960 | bytes 11796480 | tf_op jit(solution)/shard_map/blocks/pallas_call | solution.py:137
  59.6 0.0 collective-permute-done.16.refs_9_
  59.7 1.6 %collective-permute-done.19.refs_10_ = bf16[256,768]{1,0:T(8,128)(2,1)S(1)} collective-permute-done((bf16[256,768]{1,0:T(8,128)(2,1)S(1)}, bf16[256,768]{1,0:T(8,128)(2,1)S(1)}, u32[]{:S(2)}, u32[]{:S(2)}) %collective-permute-start.19) | collective-permute-done | bytes 393248 | tf_op jit(solution)/shard_map/ppermute | solution.py:206
  61.2 0.0 copy-done.1
  61.2 0.0 copy-done.3
  61.2 2.3 %blocks.4.refs_10_ = bf16[32,128,128]{2,1,0:T(8,128)(2,1)} custom-call(s32[106]{0:T(128)S(1)} %get-tuple-element.9.tab, f32[8]{0:T(128)S(1)} %copy-done.5, f32[8,128]{1,0:T(8,128)S(1)} %bitcast.5, bf16[256,768]{1,0:T(8,128)(2,1)S(1)} %copy-done.1, bf16[256,768]{1,0:T(8,128)(2,1)S(1)} %copy-done.3, ...), custom_call_target="tpu_custom_call", output_to_operand_aliasing={{}: (15, {})} | custom-call | flops 402653184 | bytes 4718592 | tf_op jit(solution)/shard_map/blocks/pallas_call | solution.py:137
  63.6 2.1 %collective-permute-done.13.refs_9_ = bf16[256,768]{1,0:T(8,128)(2,1)S(1)} collective-permute-done((bf16[256,768]{1,0:T(8,128)(2,1)S(1)}, bf16[256,768]{1,0:T(8,128)(2,1)S(1)}, u32[]{:S(2)}, u32[]{:S(2)}) %collective-permute-start.13) | collective-permute-done | bytes 393248 | tf_op jit(solution)/shard_map/ppermute | solution.py:204
  65.6 1.1 %collective-permute-done.9.refs_8_ = bf16[256,768]{1,0:T(8,128)(2,1)S(1)} collective-permute-done((bf16[256,768]{1,0:T(8,128)(2,1)S(1)}, bf16[256,768]{1,0:T(8,128)(2,1)S(1)}, u32[]{:S(2)}, u32[]{:S(2)}) %collective-permute-start.9) | collective-permute-done | bytes 393248 | tf_op jit(solution)/shard_map/ppermute | solution.py:203
  66.7 1.8 %blocks.5 = bf16[32,128,128]{2,1,0:T(8,128)(2,1)} custom-call(s32[106]{0:T(128)S(1)} %get-tuple-element.9.tab, f32[8]{0:T(128)S(1)} %copy-done.5, f32[8,128]{1,0:T(8,128)S(1)} %bitcast.6, bf16[256,768]{1,0:T(8,128)(2,1)S(1)} %copy-done.1, bf16[256,768]{1,0:T(8,128)(2,1)S(1)} %copy-done.3, ...), custom_call_target="tpu_custom_call", output_to_operand_aliasing={{}: (13, {})} | custom-call | flops 201326592 | bytes 2359296 | tf_op jit(solution)/shard_map/blocks/pallas_call | solution.py:137
Async XLA Ops:
  0.0 13.2 %collective-permute-start.10 = (bf16[256,768]{1,0:T(8,128)(2,1)}, bf16[256,768]{1,0:T(8,128)(2,1)S(1)}, u32[]{:S(2)}, u32[]{:S(2)}) collective-permute-start(bf16[256,768]{1,0:T(8,128)(2,1)} %refs_1_.5), channel_id=1, source_target_pairs={{8,0},{16,8},{24,16},{28,24},{20,28},{12,20},{4,12},{0,4},{9,1},{1... | collective-permute-start | bytes 1179656 | tf_op jit(solution)/shard_map/ppermute | solution.py:204
  2.9 12.3 %collective-permute-start.6 = (bf16[256,768]{1,0:T(8,128)(2,1)}, bf16[256,768]{1,0:T(8,128)(2,1)S(1)}, u32[]{:S(2)}, u32[]{:S(2)}) collective-permute-start(bf16[256,768]{1,0:T(8,128)(2,1)} %refs_0_.5), channel_id=1, source_target_pairs={{0,8},{8,16},{16,24},{24,28},{28,20},{20,12},{12,4},{4,0},{1,9},{9... | collective-permute-start | bytes 1179656 | tf_op jit(solution)/shard_map/ppermute | solution.py:203
  3.0 12.3 %collective-permute-start = (bf16[256,768]{1,0:T(8,128)(2,1)}, bf16[256,768]{1,0:T(8,128)(2,1)S(1)}, u32[]{:S(2)}, u32[]{:S(2)}) collective-permute-start(bf16[256,768]{1,0:T(8,128)(2,1)} %refs_0_.5), channel_id=1, source_target_pairs={{0,2},{1,3},{2,0},{3,1},{4,6},{5,7},{6,4},{7,5},{8,10},{9,11},{10,... | collective-permute-start | bytes 1179656 | tf_op jit(solution)/shard_map/ppermute | solution.py:164
  5.0 17.3 %collective-permute-start.1 = (bf16[256,768]{1,0:T(8,128)(2,1)}, bf16[256,768]{1,0:T(8,128)(2,1)S(1)}, u32[]{:S(2)}, u32[]{:S(2)}) collective-permute-start(bf16[256,768]{1,0:T(8,128)(2,1)} %refs_1_.5), channel_id=1, source_target_pairs={{0,2},{1,3},{2,0},{3,1},{4,6},{5,7},{6,4},{7,5},{8,10},{9,11},{10,... | collective-permute-start | bytes 1179656 | tf_op jit(solution)/shard_map/ppermute | solution.py:165
  5.1 18.8 %collective-permute-start.14 = (bf16[256,768]{1,0:T(8,128)(2,1)}, bf16[256,768]{1,0:T(8,128)(2,1)S(1)}, u32[]{:S(2)}, u32[]{:S(2)}) collective-permute-start(bf16[256,768]{1,0:T(8,128)(2,1)} %refs_0_.5), channel_id=1, source_target_pairs={{8,0},{16,8},{24,16},{28,24},{20,28},{12,20},{4,12},{0,4},{9,1},{1... | collective-permute-start | bytes 1179656 | tf_op jit(solution)/shard_map/ppermute | solution.py:207
  13.2 11.1 %collective-permute-start.17 = (bf16[256,768]{1,0:T(8,128)(2,1)}, bf16[256,768]{1,0:T(8,128)(2,1)S(1)}, u32[]{:S(2)}, u32[]{:S(2)}) collective-permute-start(bf16[256,768]{1,0:T(8,128)(2,1)} %refs_1_.5), channel_id=1, source_target_pairs={{0,8},{8,16},{16,24},{24,28},{28,20},{20,12},{12,4},{4,0},{1,9},{9... | collective-permute-start | bytes 1179656 | tf_op jit(solution)/shard_map/ppermute | solution.py:206
  15.2 0.7 %copy-start.6 = (s32[8,64]{1,0:T(8,128)S(1)}, s32[8,64]{1,0:T(8,128)}, u32[]{:S(2)}) copy-start(s32[8,64]{1,0:T(8,128)} %mask.1) | copy-start | bytes 6148
  15.2 9.1 %collective-permute-start.2 = (bf16[256,768]{1,0:T(8,128)(2,1)}, bf16[256,768]{1,0:T(8,128)(2,1)S(1)}, u32[]{:S(2)}, u32[]{:S(2)}) collective-permute-start(bf16[256,768]{1,0:T(8,128)(2,1)} %refs_0_.5), channel_id=1, source_target_pairs={{0,1},{1,0},{2,3},{3,2},{4,5},{5,4},{6,7},{7,6},{8,9},{9,8},{10,11... | collective-permute-start | bytes 1179656 | tf_op jit(solution)/shard_map/ppermute | solution.py:168
  15.3 10.7 %collective-permute-start.3 = (bf16[256,768]{1,0:T(8,128)(2,1)}, bf16[256,768]{1,0:T(8,128)(2,1)S(1)}, u32[]{:S(2)}, u32[]{:S(2)}) collective-permute-start(bf16[256,768]{1,0:T(8,128)(2,1)} %refs_1_.5), channel_id=1, source_target_pairs={{0,1},{1,0},{2,3},{3,2},{4,5},{5,4},{6,7},{7,6},{8,9},{9,8},{10,11... | collective-permute-start | bytes 1179656 | tf_op jit(solution)/shard_map/ppermute | solution.py:168
  15.8 0.7 copy-start.7
  19.6 33.6 %copy-start.4 = (f32[1024]{0:T(1024)S(1)}, f32[1024]{0:T(1024)}, u32[]{:S(2)}) copy-start(f32[1024]{0:T(1024)} %param.10) | copy-start | bytes 12292
  22.3 12.1 %collective-permute-start.11 = (bf16[256,768]{1,0:T(8,128)(2,1)S(1)}, bf16[256,768]{1,0:T(8,128)(2,1)S(1)}, u32[]{:S(2)}, u32[]{:S(2)}) collective-permute-start(bf16[256,768]{1,0:T(8,128)(2,1)S(1)} %collective-permute-done.10.refs_15_), channel_id=1, source_target_pairs={{8,0},{16,8},{24,16},{28,24},{20,28},{12,20},{4,12},{0,4},{9,1},{1... | collective-permute-start | bytes 1179656 | tf_op jit(solution)/shard_map/ppermute | solution.py:204
  23.9 12.1 %collective-permute-start.7 = (bf16[256,768]{1,0:T(8,128)(2,1)S(1)}, bf16[256,768]{1,0:T(8,128)(2,1)S(1)}, u32[]{:S(2)}, u32[]{:S(2)}) collective-permute-start(bf16[256,768]{1,0:T(8,128)(2,1)S(1)} %collective-permute-done.6.refs_9_), channel_id=1, source_target_pairs={{0,8},{8,16},{16,24},{24,28},{28,20},{20,12},{12,4},{4,0},{1,9},{9... | collective-permute-start | bytes 1179656 | tf_op jit(solution)/shard_map/ppermute | solution.py:203
  24.3 12.1 %collective-permute-start.4 = (bf16[256,768]{1,0:T(8,128)(2,1)S(1)}, bf16[256,768]{1,0:T(8,128)(2,1)S(1)}, u32[]{:S(2)}, u32[]{:S(2)}) collective-permute-start(bf16[256,768]{1,0:T(8,128)(2,1)S(1)} %collective-permute-done.refs_2_), channel_id=1, source_target_pairs={{0,1},{1,0},{2,3},{3,2},{4,5},{5,4},{6,7},{7,6},{8,9},{9,8},{10,11... | collective-permute-start | bytes 1179656 | tf_op jit(solution)/shard_map/ppermute | solution.py:168
  24.3 18.4 %collective-permute-start.15 = (bf16[256,768]{1,0:T(8,128)(2,1)S(1)}, bf16[256,768]{1,0:T(8,128)(2,1)S(1)}, u32[]{:S(2)}, u32[]{:S(2)}) collective-permute-start(bf16[256,768]{1,0:T(8,128)(2,1)S(1)} %collective-permute-done.14.refs_10_), channel_id=1, source_target_pairs={{8,0},{16,8},{24,16},{28,24},{20,28},{12,20},{4,12},{0,4},{9,1},{1... | collective-permute-start | bytes 1179656 | tf_op jit(solution)/shard_map/ppermute | solution.py:207
  26.0 18.4 %collective-permute-start.18 = (bf16[256,768]{1,0:T(8,128)(2,1)S(1)}, bf16[256,768]{1,0:T(8,128)(2,1)S(1)}, u32[]{:S(2)}, u32[]{:S(2)}) collective-permute-start(bf16[256,768]{1,0:T(8,128)(2,1)S(1)} %collective-permute-done.17.refs_14_), channel_id=1, source_target_pairs={{0,8},{8,16},{16,24},{24,28},{28,20},{20,12},{12,4},{4,0},{1,9},{9... | collective-permute-start | bytes 1179656 | tf_op jit(solution)/shard_map/ppermute | solution.py:206
  34.3 16.9 %collective-permute-start.12 = (bf16[256,768]{1,0:T(8,128)(2,1)S(1)}, bf16[256,768]{1,0:T(8,128)(2,1)S(1)}, u32[]{:S(2)}, u32[]{:S(2)}) collective-permute-start(bf16[256,768]{1,0:T(8,128)(2,1)S(1)} %collective-permute-done.11.refs_17_), channel_id=1, source_target_pairs={{8,0},{16,8},{24,16},{28,24},{20,28},{12,20},{4,12},{0,4},{9,1},{1... | collective-permute-start | bytes 1179656 | tf_op jit(solution)/shard_map/ppermute | solution.py:204
  36.0 16.9 %collective-permute-start.8 = (bf16[256,768]{1,0:T(8,128)(2,1)S(1)}, bf16[256,768]{1,0:T(8,128)(2,1)S(1)}, u32[]{:S(2)}, u32[]{:S(2)}) collective-permute-start(bf16[256,768]{1,0:T(8,128)(2,1)S(1)} %collective-permute-done.7.refs_11_), channel_id=1, source_target_pairs={{0,8},{8,16},{16,24},{24,28},{28,20},{20,12},{12,4},{4,0},{1,9},{9... | collective-permute-start | bytes 1179656 | tf_op jit(solution)/shard_map/ppermute | solution.py:203
  36.3 16.9 %collective-permute-start.5 = (bf16[256,768]{1,0:T(8,128)(2,1)S(1)}, bf16[256,768]{1,0:T(8,128)(2,1)S(1)}, u32[]{:S(2)}, u32[]{:S(2)}) collective-permute-start(bf16[256,768]{1,0:T(8,128)(2,1)S(1)} %collective-permute-done.1.refs_3_), channel_id=1, source_target_pairs={{0,1},{1,0},{2,3},{3,2},{4,5},{5,4},{6,7},{7,6},{8,9},{9,8},{10,11... | collective-permute-start | bytes 1179656 | tf_op jit(solution)/shard_map/ppermute | solution.py:168
  42.7 16.9 %collective-permute-start.16 = (bf16[256,768]{1,0:T(8,128)(2,1)S(1)}, bf16[256,768]{1,0:T(8,128)(2,1)S(1)}, u32[]{:S(2)}, u32[]{:S(2)}) collective-permute-start(bf16[256,768]{1,0:T(8,128)(2,1)S(1)} %collective-permute-done.15.refs_12_), channel_id=1, source_target_pairs={{8,0},{16,8},{24,16},{28,24},{20,28},{12,20},{4,12},{0,4},{9,1},{1... | collective-permute-start | bytes 1179656 | tf_op jit(solution)/shard_map/ppermute | solution.py:207
  44.4 16.9 %collective-permute-start.19 = (bf16[256,768]{1,0:T(8,128)(2,1)S(1)}, bf16[256,768]{1,0:T(8,128)(2,1)S(1)}, u32[]{:S(2)}, u32[]{:S(2)}) collective-permute-start(bf16[256,768]{1,0:T(8,128)(2,1)S(1)} %collective-permute-done.18.refs_16_), channel_id=1, source_target_pairs={{0,8},{8,16},{16,24},{24,28},{28,20},{20,12},{12,4},{4,0},{1,9},{9... | collective-permute-start | bytes 1179656 | tf_op jit(solution)/shard_map/ppermute | solution.py:206
  51.2 14.5 %collective-permute-start.13 = (bf16[256,768]{1,0:T(8,128)(2,1)S(1)}, bf16[256,768]{1,0:T(8,128)(2,1)S(1)}, u32[]{:S(2)}, u32[]{:S(2)}) collective-permute-start(bf16[256,768]{1,0:T(8,128)(2,1)S(1)} %collective-permute-done.12.refs_11_), channel_id=1, source_target_pairs={{8,0},{16,8},{24,16},{28,24},{20,28},{12,20},{4,12},{0,4},{9,1},{1... | collective-permute-start | bytes 1179656 | tf_op jit(solution)/shard_map/ppermute | solution.py:204
  52.8 13.9 %collective-permute-start.9 = (bf16[256,768]{1,0:T(8,128)(2,1)S(1)}, bf16[256,768]{1,0:T(8,128)(2,1)S(1)}, u32[]{:S(2)}, u32[]{:S(2)}) collective-permute-start(bf16[256,768]{1,0:T(8,128)(2,1)S(1)} %collective-permute-done.8.refs_8_), channel_id=1, source_target_pairs={{0,8},{8,16},{16,24},{24,28},{28,20},{20,12},{12,4},{4,0},{1,9},{9... | collective-permute-start | bytes 1179656 | tf_op jit(solution)/shard_map/ppermute | solution.py:203
  53.2 0.7 copy-start.5
  53.9 1.0 %copy-start = (bf16[256,768]{1,0:T(8,128)(2,1)S(1)}, bf16[256,768]{1,0:T(8,128)(2,1)}, u32[]{:S(2)}) copy-start(bf16[256,768]{1,0:T(8,128)(2,1)} %refs_0_.5) | copy-start | bytes 1179652
  54.8 1.0 %copy-start.2 = (bf16[256,768]{1,0:T(8,128)(2,1)S(1)}, bf16[256,768]{1,0:T(8,128)(2,1)}, u32[]{:S(2)}) copy-start(bf16[256,768]{1,0:T(8,128)(2,1)} %refs_1_.5) | copy-start | bytes 1179652
  55.8 5.4 %copy-start.1 = (bf16[256,768]{1,0:T(8,128)(2,1)S(1)}, bf16[256,768]{1,0:T(8,128)(2,1)}, u32[]{:S(2)}) copy-start(bf16[256,768]{1,0:T(8,128)(2,1)} %refs_0_.5) | copy-start | bytes 1179652
  55.8 5.4 %copy-start.3 = (bf16[256,768]{1,0:T(8,128)(2,1)S(1)}, bf16[256,768]{1,0:T(8,128)(2,1)}, u32[]{:S(2)}) copy-start(bf16[256,768]{1,0:T(8,128)(2,1)} %refs_1_.5) | copy-start | bytes 1179652

commit v5 on v4

--- a/solution.py
+++ b/solution.py
@@ -162,7 +162,7 @@
         if len(arrays) == 2:
             spots[bit] = ((2, 0), (3, 0))
             arrays.append(lax.ppermute(amplitudes, "col", pairs))
-            arrays.append(lax.ppermute(integrals, "col", pairs))
+            arrays.append(lax.ppermute(after(integrals, arrays[2]), "col", pairs))
         else:
             for n, array in enumerate(list(arrays)):
                 arrays.append(lax.ppermute(array, "col", pairs))

time: 68.8 us -> 67.3 us (0.978)
  waiting for transfers between devices: 34.3 us -> 26.1 us
  starting transfers between devices: 19.7 us -> 26.5 us
    ppermute x4, waiting for transfers between devices: 22.6 us -> 15.1 us  [shards(): int_down = lax.ppermute(after(int_down, gate), 'row', behind)]
    ppermute x4, starting transfers between devices: 1.24 us -> 5.47 us  [shards(): amp_up = lax.ppermute(after(amp_up, gate), 'row', ahead)]
    ppermute x4, waiting for transfers between devices: 1.08 us -> 3.98 us  [shards(): amp_up = lax.ppermute(after(amp_up, gate), 'row', ahead)]
    ppermute x1, waiting for transfers between devices: 2.66 us -> 0.02 us  [gather_cols(): arrays.append(lax.ppermute(after(integrals, arrays[2]), 'col', pairs))]
    ppermute x3, starting transfers between devices: 2.83 us -> 4.66 us  [shards(): int_up = lax.ppermute(int_up, 'row', ahead)]
    ppermute x1, starting transfers between devices: 0.06 us -> 1.52 us  [gather_cols(): arrays.append(lax.ppermute(after(integrals, arrays[2]), 'col', pairs))]
    ppermute x3, waiting for transfers between devices: 6.39 us -> 5.29 us  [shards(): amp_down = lax.ppermute(amp_down, 'row', behind)]
  transfers between devices with their start and end apart: 20 -> 20, of which waited for: 8 -> 9; matrix products, arithmetic and copies ran while one was open for 0% -> 0% of each run, Pallas kernels for 14% -> 14%
where the time goes in v5:
time: 67.3 us; the launch traced here: 67 us
  starting transfers between devices  26.5 us (39%)
  waiting for transfers between devices  26.1 us (39%)
  Pallas kernels  11.1 us (16%)
  local copies, waits for them, and re-layouts  3.24 us (5%)
    ppermute x4, waiting for transfers between devices, shards(): int_down = lax.ppermute(after(int_down, gate), 'row', behind)  15.1 us
    pallas_call x3, Pallas kernels, step(): pl.pallas_call(functools.partial(step_kernel, hops, spots, ncol, nrow, sp...  7.91 us
    ppermute x4, starting transfers between devices, shards(): int_down = lax.ppermute(after(int_down, gate), 'row', behind)  7.67 us
    ppermute x4, starting transfers between devices, shards(): amp_up = lax.ppermute(after(amp_up, gate), 'row', ahead)  5.47 us
    ppermute x3, waiting for transfers between devices, shards(): amp_down = lax.ppermute(amp_down, 'row', behind)  5.29 us
    ppermute x3, starting transfers between devices, shards(): int_up = lax.ppermute(int_up, 'row', ahead)  4.66 us
    ppermute x3, starting transfers between devices, shards(): amp_down = lax.ppermute(amp_down, 'row', behind)  4.61 us
    ppermute x4, waiting for transfers between devices, shards(): amp_up = lax.ppermute(after(amp_up, gate), 'row', ahead)  3.98 us
  transfers between devices with their start and end apart: 20, of which 9 were waited for; matrix products, arithmetic and copies ran while one was open for 0% of the time, Pallas kernels for 14%

profile of v5, /device:TPU:0, one launch (start us, length us, event | category | flops | bytes accessed | tf_op | source)
XLA Modules:
  0.0 67.0 jit_solution(8641178360851833622)
XLA Ops:
  0.0 2.9 %collective-permute-start.10 = (bf16[256,768]{1,0:T(8,128)(2,1)}, bf16[256,768]{1,0:T(8,128)(2,1)S(1)}, u32[]{:S(2)}, u32[]{:S(2)}) collective-permute-start(bf16[256,768]{1,0:T(8,128)(2,1)} %refs_1_.5), channel_id=1, source_target_pairs={{8,0},{16,8},{24,16},{28,24},{20,28},{12,20},{4,12},{0,4},{9,1},{1... | collective-permute-start | bytes 1179656 | tf_op jit(solution)/shard_map/ppermute | solution.py:204
  2.9 0.1 collective-permute-start.6
  3.0 2.0 %collective-permute-start = (bf16[256,768]{1,0:T(8,128)(2,1)}, bf16[256,768]{1,0:T(8,128)(2,1)S(1)}, u32[]{:S(2)}, u32[]{:S(2)}) collective-permute-start(bf16[256,768]{1,0:T(8,128)(2,1)} %refs_0_.5), channel_id=1, source_target_pairs={{0,2},{1,3},{2,0},{3,1},{4,6},{5,7},{6,4},{7,5},{8,10},{9,11},{10,... | collective-permute-start | bytes 1179656 | tf_op jit(solution)/shard_map/ppermute | solution.py:164
  5.0 1.5 %collective-permute-start.14 = (bf16[256,768]{1,0:T(8,128)(2,1)}, bf16[256,768]{1,0:T(8,128)(2,1)S(1)}, u32[]{:S(2)}, u32[]{:S(2)}) collective-permute-start(bf16[256,768]{1,0:T(8,128)(2,1)} %refs_0_.5), channel_id=1, source_target_pairs={{8,0},{16,8},{24,16},{28,24},{20,28},{12,20},{4,12},{0,4},{9,1},{1... | collective-permute-start | bytes 1179656 | tf_op jit(solution)/shard_map/ppermute | solution.py:207
  6.5 0.5 collective-permute-start.17
  7.0 0.0 copy-start.6
  7.0 6.2 %collective-permute-done.10.refs_15_ = bf16[256,768]{1,0:T(8,128)(2,1)S(1)} collective-permute-done((bf16[256,768]{1,0:T(8,128)(2,1)}, bf16[256,768]{1,0:T(8,128)(2,1)S(1)}, u32[]{:S(2)}, u32[]{:S(2)}) %collective-permute-start.10) | collective-permute-done | bytes 393248 | tf_op jit(solution)/shard_map/ppermute | solution.py:204
  13.2 0.0 collective-permute-start.2
  13.2 0.0 copy-start.7
  13.2 0.1 pad_add_fusion.where
  13.3 0.0 copy-done.6
  13.3 0.6 copy-done.7
  13.8 3.2 %slots.1 = (s32[106]{0:T(128)S(1)}, bf16[32,128,128]{2,1,0:T(8,128)(2,1)}) custom-call(s32[2]{0:T(128)S(1)} %pad_add_fusion.where, s32[64]{0:T(128)S(1)} %copy-done.7, s32[8,64]{1,0:T(8,128)S(1)} %copy-done.6), custom_call_target="tpu_custom_call" | custom-call | tf_op jit(solution)/shard_map/slots/pallas_call | solution.py:74
  17.0 0.0 copy-start.4
  17.0 0.0 collective-permute-done.6.refs_9_
  17.0 0.6 collective-permute-start.3
  17.6 0.0 collective-permute-done.refs_2_
  17.6 2.0 %collective-permute-start.11 = (bf16[256,768]{1,0:T(8,128)(2,1)S(1)}, bf16[256,768]{1,0:T(8,128)(2,1)S(1)}, u32[]{:S(2)}, u32[]{:S(2)}) collective-permute-start(bf16[256,768]{1,0:T(8,128)(2,1)S(1)} %collective-permute-done.10.refs_15_), channel_id=1, source_target_pairs={{8,0},{16,8},{24,16},{28,24},{20,28},{12,20},{4,12},{0,4},{9,1},{1... | collective-permute-start | bytes 1179656 | tf_op jit(solution)/shard_map/ppermute | solution.py:204
  19.6 1.3 %collective-permute-done.14.refs_10_ = bf16[256,768]{1,0:T(8,128)(2,1)S(1)} collective-permute-done((bf16[256,768]{1,0:T(8,128)(2,1)}, bf16[256,768]{1,0:T(8,128)(2,1)S(1)}, u32[]{:S(2)}, u32[]{:S(2)}) %collective-permute-start.14) | collective-permute-done | bytes 393248 | tf_op jit(solution)/shard_map/ppermute | solution.py:207
  20.9 1.7 %collective-permute-start.7 = (bf16[256,768]{1,0:T(8,128)(2,1)S(1)}, bf16[256,768]{1,0:T(8,128)(2,1)S(1)}, u32[]{:S(2)}, u32[]{:S(2)}) collective-permute-start(bf16[256,768]{1,0:T(8,128)(2,1)S(1)} %collective-permute-done.6.refs_9_), channel_id=1, source_target_pairs={{0,8},{8,16},{16,24},{24,28},{28,20},{20,12},{12,4},{4,0},{1,9},{9... | collective-permute-start | bytes 1179656 | tf_op jit(solution)/shard_map/ppermute | solution.py:203
  22.6 0.0 collective-permute-done.17.refs_14_
  22.6 1.5 %collective-permute-start.1 = (bf16[256,768]{1,0:T(8,128)(2,1)}, bf16[256,768]{1,0:T(8,128)(2,1)S(1)}, u32[]{:S(2)}, u32[]{:S(2)}) collective-permute-start(bf16[256,768]{1,0:T(8,128)(2,1)} %refs_1_.5), channel_id=1, source_target_pairs={{0,2},{1,3},{2,0},{3,1},{4,6},{5,7},{6,4},{7,5},{8,10},{9,11},{10,... | collective-permute-start | bytes 1179656 | tf_op jit(solution)/shard_map/ppermute | solution.py:165
  24.2 0.0 collective-permute-done.2.refs_4_
  24.2 0.0 collective-permute-start.4
  24.2 0.0 collective-permute-done.3.refs_5_
  24.2 1.1 %collective-permute-start.15 = (bf16[256,768]{1,0:T(8,128)(2,1)S(1)}, bf16[256,768]{1,0:T(8,128)(2,1)S(1)}, u32[]{:S(2)}, u32[]{:S(2)}) collective-permute-start(bf16[256,768]{1,0:T(8,128)(2,1)S(1)} %collective-permute-done.14.refs_10_), channel_id=1, source_target_pairs={{8,0},{16,8},{24,16},{28,24},{20,28},{12,20},{4,12},{0,4},{9,1},{1... | collective-permute-start | bytes 1179656 | tf_op jit(solution)/shard_map/ppermute | solution.py:207
  25.3 4.3 %collective-permute-done.11.refs_17_ = bf16[256,768]{1,0:T(8,128)(2,1)S(1)} collective-permute-done((bf16[256,768]{1,0:T(8,128)(2,1)S(1)}, bf16[256,768]{1,0:T(8,128)(2,1)S(1)}, u32[]{:S(2)}, u32[]{:S(2)}) %collective-permute-start.11) | collective-permute-done | bytes 393248 | tf_op jit(solution)/shard_map/ppermute | solution.py:204
  29.6 2.1 %collective-permute-start.18 = (bf16[256,768]{1,0:T(8,128)(2,1)S(1)}, bf16[256,768]{1,0:T(8,128)(2,1)S(1)}, u32[]{:S(2)}, u32[]{:S(2)}) collective-permute-start(bf16[256,768]{1,0:T(8,128)(2,1)S(1)} %collective-permute-done.17.refs_14_), channel_id=1, source_target_pairs={{0,8},{8,16},{16,24},{24,28},{28,20},{20,12},{12,4},{4,0},{1,9},{9... | collective-permute-start | bytes 1179656 | tf_op jit(solution)/shard_map/ppermute | solution.py:206
  31.6 0.0 collective-permute-done.7.refs_11_
  31.6 0.8 %collective-permute-start.12 = (bf16[256,768]{1,0:T(8,128)(2,1)S(1)}, bf16[256,768]{1,0:T(8,128)(2,1)S(1)}, u32[]{:S(2)}, u32[]{:S(2)}) collective-permute-start(bf16[256,768]{1,0:T(8,128)(2,1)S(1)} %collective-permute-done.11.refs_17_), channel_id=1, source_target_pairs={{8,0},{16,8},{24,16},{28,24},{20,28},{12,20},{4,12},{0,4},{9,1},{1... | collective-permute-start | bytes 1179656 | tf_op jit(solution)/shard_map/ppermute | solution.py:204
  32.4 0.0 collective-permute-done.1.refs_3_
  32.4 1.6 %collective-permute-start.8 = (bf16[256,768]{1,0:T(8,128)(2,1)S(1)}, bf16[256,768]{1,0:T(8,128)(2,1)S(1)}, u32[]{:S(2)}, u32[]{:S(2)}) collective-permute-start(bf16[256,768]{1,0:T(8,128)(2,1)S(1)} %collective-permute-done.7.refs_11_), channel_id=1, source_target_pairs={{0,8},{8,16},{16,24},{24,28},{28,20},{20,12},{12,4},{4,0},{1,9},{9... | collective-permute-start | bytes 1179656 | tf_op jit(solution)/shard_map/ppermute | solution.py:203
  34.0 0.0 collective-permute-done.4.refs_6_
  34.0 0.0 collective-permute-start.5
  34.0 4.0 %collective-permute-done.15.refs_12_ = bf16[256,768]{1,0:T(8,128)(2,1)S(1)} collective-permute-done((bf16[256,768]{1,0:T(8,128)(2,1)S(1)}, bf16[256,768]{1,0:T(8,128)(2,1)S(1)}, u32[]{:S(2)}, u32[]{:S(2)}) %collective-permute-start.15) | collective-permute-done | bytes 393248 | tf_op jit(solution)/shard_map/ppermute | solution.py:207
  38.0 2.0 %collective-permute-start.16 = (bf16[256,768]{1,0:T(8,128)(2,1)S(1)}, bf16[256,768]{1,0:T(8,128)(2,1)S(1)}, u32[]{:S(2)}, u32[]{:S(2)}) collective-permute-start(bf16[256,768]{1,0:T(8,128)(2,1)S(1)} %collective-permute-done.15.refs_12_), channel_id=1, source_target_pairs={{8,0},{16,8},{24,16},{28,24},{20,28},{12,20},{4,12},{0,4},{9,1},{1... | collective-permute-start | bytes 1179656 | tf_op jit(solution)/shard_map/ppermute | solution.py:207
  40.0 1.6 %collective-permute-done.18.refs_16_ = bf16[256,768]{1,0:T(8,128)(2,1)S(1)} collective-permute-done((bf16[256,768]{1,0:T(8,128)(2,1)S(1)}, bf16[256,768]{1,0:T(8,128)(2,1)S(1)}, u32[]{:S(2)}, u32[]{:S(2)}) %collective-permute-start.18) | collective-permute-done | bytes 393248 | tf_op jit(solution)/shard_map/ppermute | solution.py:206
  41.6 2.1 %collective-permute-start.19 = (bf16[256,768]{1,0:T(8,128)(2,1)S(1)}, bf16[256,768]{1,0:T(8,128)(2,1)S(1)}, u32[]{:S(2)}, u32[]{:S(2)}) collective-permute-start(bf16[256,768]{1,0:T(8,128)(2,1)S(1)} %collective-permute-done.18.refs_16_), channel_id=1, source_target_pairs={{0,8},{8,16},{16,24},{24,28},{28,20},{20,12},{12,4},{4,0},{1,9},{9... | collective-permute-start | bytes 1179656 | tf_op jit(solution)/shard_map/ppermute | solution.py:206
  43.7 2.7 %collective-permute-done.12.refs_11_ = bf16[256,768]{1,0:T(8,128)(2,1)S(1)} collective-permute-done((bf16[256,768]{1,0:T(8,128)(2,1)S(1)}, bf16[256,768]{1,0:T(8,128)(2,1)S(1)}, u32[]{:S(2)}, u32[]{:S(2)}) %collective-permute-start.12) | collective-permute-done | bytes 393248 | tf_op jit(solution)/shard_map/ppermute | solution.py:204
  46.4 2.0 %collective-permute-start.13 = (bf16[256,768]{1,0:T(8,128)(2,1)S(1)}, bf16[256,768]{1,0:T(8,128)(2,1)S(1)}, u32[]{:S(2)}, u32[]{:S(2)}) collective-permute-start(bf16[256,768]{1,0:T(8,128)(2,1)S(1)} %collective-permute-done.12.refs_11_), channel_id=1, source_target_pairs={{8,0},{16,8},{24,16},{28,24},{20,28},{12,20},{4,12},{0,4},{9,1},{1... | collective-permute-start | bytes 1179656 | tf_op jit(solution)/shard_map/ppermute | solution.py:204
  48.4 1.6 %collective-permute-done.8.refs_8_ = bf16[256,768]{1,0:T(8,128)(2,1)S(1)} collective-permute-done((bf16[256,768]{1,0:T(8,128)(2,1)S(1)}, bf16[256,768]{1,0:T(8,128)(2,1)S(1)}, u32[]{:S(2)}, u32[]{:S(2)}) %collective-permute-start.8) | collective-permute-done | bytes 393248 | tf_op jit(solution)/shard_map/ppermute | solution.py:203
  50.1 2.1 %collective-permute-start.9 = (bf16[256,768]{1,0:T(8,128)(2,1)S(1)}, bf16[256,768]{1,0:T(8,128)(2,1)S(1)}, u32[]{:S(2)}, u32[]{:S(2)}) collective-permute-start(bf16[256,768]{1,0:T(8,128)(2,1)S(1)} %collective-permute-done.8.refs_8_), channel_id=1, source_target_pairs={{0,8},{8,16},{16,24},{24,28},{28,20},{20,12},{12,4},{4,0},{1,9},{9... | collective-permute-start | bytes 1179656 | tf_op jit(solution)/shard_map/ppermute | solution.py:203
  52.1 0.0 collective-permute-done.5.refs_7_
  52.1 0.0 copy-start.5
  52.1 0.0 copy-done.4
  52.1 0.7 copy-done.5
  52.8 0.0 copy-start
  52.8 1.0 %copy-done = bf16[256,768]{1,0:T(8,128)(2,1)S(1)} copy-done((bf16[256,768]{1,0:T(8,128)(2,1)S(1)}, bf16[256,768]{1,0:T(8,128)(2,1)}, u32[]{:S(2)}) %copy-start) | copy-done | bytes 393240
  53.8 0.0 copy-start.2
  53.8 1.0 %copy-done.2 = bf16[256,768]{1,0:T(8,128)(2,1)S(1)} copy-done((bf16[256,768]{1,0:T(8,128)(2,1)S(1)}, bf16[256,768]{1,0:T(8,128)(2,1)}, u32[]{:S(2)}) %copy-start.2) | copy-done | bytes 393240
  54.8 0.0 copy-start.1
  54.8 0.0 copy-start.3
  54.8 3.8 %blocks.3.refs_12_ = bf16[32,128,128]{2,1,0:T(8,128)(2,1)} custom-call(s32[106]{0:T(128)S(1)} %get-tuple-element.10.tab, f32[8]{0:T(128)S(1)} %copy-done.5, f32[8,128]{1,0:T(8,128)S(1)} %bitcast.4, bf16[256,768]{1,0:T(8,128)(2,1)S(1)} %copy-done, bf16[256,768]{1,0:T(8,128)(2,1)S(1)} %copy-done.2, ...), custom_call_target="tpu_custom_call", output_to_operand_aliasing={{}: (21, {})} | custom-call | flops 1006632960 | bytes 11796480 | tf_op jit(solution)/shard_map/blocks/pallas_call | solution.py:137
  58.6 0.0 collective-permute-done.16.refs_9_
  58.6 0.0 collective-permute-done.19.refs_10_
  58.6 0.0 copy-done.1
  58.6 0.0 copy-done.3
  58.6 2.3 %blocks.4.refs_10_ = bf16[32,128,128]{2,1,0:T(8,128)(2,1)} custom-call(s32[106]{0:T(128)S(1)} %get-tuple-element.10.tab, f32[8]{0:T(128)S(1)} %copy-done.5, f32[8,128]{1,0:T(8,128)S(1)} %bitcast.5, bf16[256,768]{1,0:T(8,128)(2,1)S(1)} %copy-done.1, bf16[256,768]{1,0:T(8,128)(2,1)S(1)} %copy-done.3, ...), custom_call_target="tpu_custom_call", output_to_operand_aliasing={{}: (15, {})} | custom-call | flops 402653184 | bytes 4718592 | tf_op jit(solution)/shard_map/blocks/pallas_call | solution.py:137
  60.9 2.0 %collective-permute-done.13.refs_9_ = bf16[256,768]{1,0:T(8,128)(2,1)S(1)} collective-permute-done((bf16[256,768]{1,0:T(8,128)(2,1)S(1)}, bf16[256,768]{1,0:T(8,128)(2,1)S(1)}, u32[]{:S(2)}, u32[]{:S(2)}) %collective-permute-start.13) | collective-permute-done | bytes 393248 | tf_op jit(solution)/shard_map/ppermute | solution.py:204
  62.9 2.3 %collective-permute-done.9.refs_8_ = bf16[256,768]{1,0:T(8,128)(2,1)S(1)} collective-permute-done((bf16[256,768]{1,0:T(8,128)(2,1)S(1)}, bf16[256,768]{1,0:T(8,128)(2,1)S(1)}, u32[]{:S(2)}, u32[]{:S(2)}) %collective-permute-start.9) | collective-permute-done | bytes 393248 | tf_op jit(solution)/shard_map/ppermute | solution.py:203
  65.2 1.8 %blocks.5 = bf16[32,128,128]{2,1,0:T(8,128)(2,1)} custom-call(s32[106]{0:T(128)S(1)} %get-tuple-element.10.tab, f32[8]{0:T(128)S(1)} %copy-done.5, f32[8,128]{1,0:T(8,128)S(1)} %bitcast.6, bf16[256,768]{1,0:T(8,128)(2,1)S(1)} %copy-done.1, bf16[256,768]{1,0:T(8,128)(2,1)S(1)} %copy-done.3, ...), custom_call_target="tpu_custom_call", output_to_operand_aliasing={{}: (13, {})} | custom-call | flops 201326592 | bytes 2359296 | tf_op jit(solution)/shard_map/blocks/pallas_call | solution.py:137
Async XLA Ops:
  0.0 13.2 %collective-permute-start.10 = (bf16[256,768]{1,0:T(8,128)(2,1)}, bf16[256,768]{1,0:T(8,128)(2,1)S(1)}, u32[]{:S(2)}, u32[]{:S(2)}) collective-permute-start(bf16[256,768]{1,0:T(8,128)(2,1)} %refs_1_.5), channel_id=1, source_target_pairs={{8,0},{16,8},{24,16},{28,24},{20,28},{12,20},{4,12},{0,4},{9,1},{1... | collective-permute-start | bytes 1179656 | tf_op jit(solution)/shard_map/ppermute | solution.py:204
  2.9 14.1 %collective-permute-start.6 = (bf16[256,768]{1,0:T(8,128)(2,1)}, bf16[256,768]{1,0:T(8,128)(2,1)S(1)}, u32[]{:S(2)}, u32[]{:S(2)}) collective-permute-start(bf16[256,768]{1,0:T(8,128)(2,1)} %refs_0_.5), channel_id=1, source_target_pairs={{0,8},{8,16},{16,24},{24,28},{28,20},{20,12},{12,4},{4,0},{1,9},{9... | collective-permute-start | bytes 1179656 | tf_op jit(solution)/shard_map/ppermute | solution.py:203
  3.0 14.6 %collective-permute-start = (bf16[256,768]{1,0:T(8,128)(2,1)}, bf16[256,768]{1,0:T(8,128)(2,1)S(1)}, u32[]{:S(2)}, u32[]{:S(2)}) collective-permute-start(bf16[256,768]{1,0:T(8,128)(2,1)} %refs_0_.5), channel_id=1, source_target_pairs={{0,2},{1,3},{2,0},{3,1},{4,6},{5,7},{6,4},{7,5},{8,10},{9,11},{10,... | collective-permute-start | bytes 1179656 | tf_op jit(solution)/shard_map/ppermute | solution.py:164
  5.0 15.9 %collective-permute-start.14 = (bf16[256,768]{1,0:T(8,128)(2,1)}, bf16[256,768]{1,0:T(8,128)(2,1)S(1)}, u32[]{:S(2)}, u32[]{:S(2)}) collective-permute-start(bf16[256,768]{1,0:T(8,128)(2,1)} %refs_0_.5), channel_id=1, source_target_pairs={{8,0},{16,8},{24,16},{28,24},{20,28},{12,20},{4,12},{0,4},{9,1},{1... | collective-permute-start | bytes 1179656 | tf_op jit(solution)/shard_map/ppermute | solution.py:207
  6.5 16.1 %collective-permute-start.17 = (bf16[256,768]{1,0:T(8,128)(2,1)}, bf16[256,768]{1,0:T(8,128)(2,1)S(1)}, u32[]{:S(2)}, u32[]{:S(2)}) collective-permute-start(bf16[256,768]{1,0:T(8,128)(2,1)} %refs_1_.5), channel_id=1, source_target_pairs={{0,8},{8,16},{16,24},{24,28},{28,20},{20,12},{12,4},{4,0},{1,9},{9... | collective-permute-start | bytes 1179656 | tf_op jit(solution)/shard_map/ppermute | solution.py:206
  7.0 6.2 %copy-start.6 = (s32[8,64]{1,0:T(8,128)S(1)}, s32[8,64]{1,0:T(8,128)}, u32[]{:S(2)}) copy-start(s32[8,64]{1,0:T(8,128)} %mask.1) | copy-start | bytes 6148
  13.2 11.0 %collective-permute-start.2 = (bf16[256,768]{1,0:T(8,128)(2,1)}, bf16[256,768]{1,0:T(8,128)(2,1)S(1)}, u32[]{:S(2)}, u32[]{:S(2)}) collective-permute-start(bf16[256,768]{1,0:T(8,128)(2,1)} %refs_0_.5), channel_id=1, source_target_pairs={{0,1},{1,0},{2,3},{3,2},{4,5},{5,4},{6,7},{7,6},{8,9},{9,8},{10,11... | collective-permute-start | bytes 1179656 | tf_op jit(solution)/shard_map/ppermute | solution.py:168
  13.2 0.7 copy-start.7
  17.0 35.1 %copy-start.4 = (f32[1024]{0:T(1024)S(1)}, f32[1024]{0:T(1024)}, u32[]{:S(2)}) copy-start(f32[1024]{0:T(1024)} %param.10) | copy-start | bytes 12292
  17.0 7.1 %collective-permute-start.3 = (bf16[256,768]{1,0:T(8,128)(2,1)}, bf16[256,768]{1,0:T(8,128)(2,1)S(1)}, u32[]{:S(2)}, u32[]{:S(2)}) collective-permute-start(bf16[256,768]{1,0:T(8,128)(2,1)} %refs_1_.5), channel_id=1, source_target_pairs={{0,1},{1,0},{2,3},{3,2},{4,5},{5,4},{6,7},{7,6},{8,9},{9,8},{10,11... | collective-permute-start | bytes 1179656 | tf_op jit(solution)/shard_map/ppermute | solution.py:168
  17.6 12.0 %collective-permute-start.11 = (bf16[256,768]{1,0:T(8,128)(2,1)S(1)}, bf16[256,768]{1,0:T(8,128)(2,1)S(1)}, u32[]{:S(2)}, u32[]{:S(2)}) collective-permute-start(bf16[256,768]{1,0:T(8,128)(2,1)S(1)} %collective-permute-done.10.refs_15_), channel_id=1, source_target_pairs={{8,0},{16,8},{24,16},{28,24},{20,28},{12,20},{4,12},{0,4},{9,1},{1... | collective-permute-start | bytes 1179656 | tf_op jit(solution)/shard_map/ppermute | solution.py:204
  20.9 10.7 %collective-permute-start.7 = (bf16[256,768]{1,0:T(8,128)(2,1)S(1)}, bf16[256,768]{1,0:T(8,128)(2,1)S(1)}, u32[]{:S(2)}, u32[]{:S(2)}) collective-permute-start(bf16[256,768]{1,0:T(8,128)(2,1)S(1)} %collective-permute-done.6.refs_9_), channel_id=1, source_target_pairs={{0,8},{8,16},{16,24},{24,28},{28,20},{20,12},{12,4},{4,0},{1,9},{9... | collective-permute-start | bytes 1179656 | tf_op jit(solution)/shard_map/ppermute | solution.py:203
  22.6 9.8 %collective-permute-start.1 = (bf16[256,768]{1,0:T(8,128)(2,1)}, bf16[256,768]{1,0:T(8,128)(2,1)S(1)}, u32[]{:S(2)}, u32[]{:S(2)}) collective-permute-start(bf16[256,768]{1,0:T(8,128)(2,1)} %refs_1_.5), channel_id=1, source_target_pairs={{0,2},{1,3},{2,0},{3,1},{4,6},{5,7},{6,4},{7,5},{8,10},{9,11},{10,... | collective-permute-start | bytes 1179656 | tf_op jit(solution)/shard_map/ppermute | solution.py:165
  24.2 9.9 %collective-permute-start.4 = (bf16[256,768]{1,0:T(8,128)(2,1)S(1)}, bf16[256,768]{1,0:T(8,128)(2,1)S(1)}, u32[]{:S(2)}, u32[]{:S(2)}) collective-permute-start(bf16[256,768]{1,0:T(8,128)(2,1)S(1)} %collective-permute-done.refs_2_), channel_id=1, source_target_pairs={{0,1},{1,0},{2,3},{3,2},{4,5},{5,4},{6,7},{7,6},{8,9},{9,8},{10,11... | collective-permute-start | bytes 1179656 | tf_op jit(solution)/shard_map/ppermute | solution.py:168
  24.2 13.8 %collective-permute-start.15 = (bf16[256,768]{1,0:T(8,128)(2,1)S(1)}, bf16[256,768]{1,0:T(8,128)(2,1)S(1)}, u32[]{:S(2)}, u32[]{:S(2)}) collective-permute-start(bf16[256,768]{1,0:T(8,128)(2,1)S(1)} %collective-permute-done.14.refs_10_), channel_id=1, source_target_pairs={{8,0},{16,8},{24,16},{28,24},{20,28},{12,20},{4,12},{0,4},{9,1},{1... | collective-permute-start | bytes 1179656 | tf_op jit(solution)/shard_map/ppermute | solution.py:207
  29.6 12.1 %collective-permute-start.18 = (bf16[256,768]{1,0:T(8,128)(2,1)S(1)}, bf16[256,768]{1,0:T(8,128)(2,1)S(1)}, u32[]{:S(2)}, u32[]{:S(2)}) collective-permute-start(bf16[256,768]{1,0:T(8,128)(2,1)S(1)} %collective-permute-done.17.refs_14_), channel_id=1, source_target_pairs={{0,8},{8,16},{16,24},{24,28},{28,20},{20,12},{12,4},{4,0},{1,9},{9... | collective-permute-start | bytes 1179656 | tf_op jit(solution)/shard_map/ppermute | solution.py:206
  31.6 14.8 %collective-permute-start.12 = (bf16[256,768]{1,0:T(8,128)(2,1)S(1)}, bf16[256,768]{1,0:T(8,128)(2,1)S(1)}, u32[]{:S(2)}, u32[]{:S(2)}) collective-permute-start(bf16[256,768]{1,0:T(8,128)(2,1)S(1)} %collective-permute-done.11.refs_17_), channel_id=1, source_target_pairs={{8,0},{16,8},{24,16},{28,24},{20,28},{12,20},{4,12},{0,4},{9,1},{1... | collective-permute-start | bytes 1179656 | tf_op jit(solution)/shard_map/ppermute | solution.py:204
  32.4 17.6 %collective-permute-start.8 = (bf16[256,768]{1,0:T(8,128)(2,1)S(1)}, bf16[256,768]{1,0:T(8,128)(2,1)S(1)}, u32[]{:S(2)}, u32[]{:S(2)}) collective-permute-start(bf16[256,768]{1,0:T(8,128)(2,1)S(1)} %collective-permute-done.7.refs_11_), channel_id=1, source_target_pairs={{0,8},{8,16},{16,24},{24,28},{28,20},{20,12},{12,4},{4,0},{1,9},{9... | collective-permute-start | bytes 1179656 | tf_op jit(solution)/shard_map/ppermute | solution.py:203
  34.0 18.1 %collective-permute-start.5 = (bf16[256,768]{1,0:T(8,128)(2,1)S(1)}, bf16[256,768]{1,0:T(8,128)(2,1)S(1)}, u32[]{:S(2)}, u32[]{:S(2)}) collective-permute-start(bf16[256,768]{1,0:T(8,128)(2,1)S(1)} %collective-permute-done.1.refs_3_), channel_id=1, source_target_pairs={{0,1},{1,0},{2,3},{3,2},{4,5},{5,4},{6,7},{7,6},{8,9},{9,8},{10,11... | collective-permute-start | bytes 1179656 | tf_op jit(solution)/shard_map/ppermute | solution.py:168
  38.0 20.6 %collective-permute-start.16 = (bf16[256,768]{1,0:T(8,128)(2,1)S(1)}, bf16[256,768]{1,0:T(8,128)(2,1)S(1)}, u32[]{:S(2)}, u32[]{:S(2)}) collective-permute-start(bf16[256,768]{1,0:T(8,128)(2,1)S(1)} %collective-permute-done.15.refs_12_), channel_id=1, source_target_pairs={{8,0},{16,8},{24,16},{28,24},{20,28},{12,20},{4,12},{0,4},{9,1},{1... | collective-permute-start | bytes 1179656 | tf_op jit(solution)/shard_map/ppermute | solution.py:207
  41.6 16.9 %collective-permute-start.19 = (bf16[256,768]{1,0:T(8,128)(2,1)S(1)}, bf16[256,768]{1,0:T(8,128)(2,1)S(1)}, u32[]{:S(2)}, u32[]{:S(2)}) collective-permute-start(bf16[256,768]{1,0:T(8,128)(2,1)S(1)} %collective-permute-done.18.refs_16_), channel_id=1, source_target_pairs={{0,8},{8,16},{16,24},{24,28},{28,20},{20,12},{12,4},{4,0},{1,9},{9... | collective-permute-start | bytes 1179656 | tf_op jit(solution)/shard_map/ppermute | solution.py:206
  46.4 16.5 %collective-permute-start.13 = (bf16[256,768]{1,0:T(8,128)(2,1)S(1)}, bf16[256,768]{1,0:T(8,128)(2,1)S(1)}, u32[]{:S(2)}, u32[]{:S(2)}) collective-permute-start(bf16[256,768]{1,0:T(8,128)(2,1)S(1)} %collective-permute-done.12.refs_11_), channel_id=1, source_target_pairs={{8,0},{16,8},{24,16},{28,24},{20,28},{12,20},{4,12},{0,4},{9,1},{1... | collective-permute-start | bytes 1179656 | tf_op jit(solution)/shard_map/ppermute | solution.py:204
  50.1 15.2 %collective-permute-start.9 = (bf16[256,768]{1,0:T(8,128)(2,1)S(1)}, bf16[256,768]{1,0:T(8,128)(2,1)S(1)}, u32[]{:S(2)}, u32[]{:S(2)}) collective-permute-start(bf16[256,768]{1,0:T(8,128)(2,1)S(1)} %collective-permute-done.8.refs_8_), channel_id=1, source_target_pairs={{0,8},{8,16},{16,24},{24,28},{28,20},{20,12},{12,4},{4,0},{1,9},{9... | collective-permute-start | bytes 1179656 | tf_op jit(solution)/shard_map/ppermute | solution.py:203
  52.1 0.7 copy-start.5
  52.8 1.0 %copy-start = (bf16[256,768]{1,0:T(8,128)(2,1)S(1)}, bf16[256,768]{1,0:T(8,128)(2,1)}, u32[]{:S(2)}) copy-start(bf16[256,768]{1,0:T(8,128)(2,1)} %refs_0_.5) | copy-start | bytes 1179652
  53.8 1.0 %copy-start.2 = (bf16[256,768]{1,0:T(8,128)(2,1)S(1)}, bf16[256,768]{1,0:T(8,128)(2,1)}, u32[]{:S(2)}) copy-start(bf16[256,768]{1,0:T(8,128)(2,1)} %refs_1_.5) | copy-start | bytes 1179652
  54.8 3.8 %copy-start.1 = (bf16[256,768]{1,0:T(8,128)(2,1)S(1)}, bf16[256,768]{1,0:T(8,128)(2,1)}, u32[]{:S(2)}) copy-start(bf16[256,768]{1,0:T(8,128)(2,1)} %refs_0_.5) | copy-start | bytes 1179652
  54.8 3.8 %copy-start.3 = (bf16[256,768]{1,0:T(8,128)(2,1)S(1)}, bf16[256,768]{1,0:T(8,128)(2,1)}, u32[]{:S(2)}) copy-start(bf16[256,768]{1,0:T(8,128)(2,1)} %refs_1_.5) | copy-start | bytes 1179652

commit v6 on v5

--- a/solution.py
+++ b/solution.py
@@ -154,7 +154,7 @@
     )(tab, occ, vir, *row_shards, *amp_b, *int_b, out)
 
 
-def gather_cols(amplitudes, integrals, ncol):
+def gather_cols(amplitudes, integrals, ncol, held):
     arrays, spots = [amplitudes, integrals], {0: ((0, 0), (1, 0))}
     bit = ncol // 2
     while bit:
@@ -164,9 +164,10 @@
             arrays.append(lax.ppermute(amplitudes, "col", pairs))
             arrays.append(lax.ppermute(after(integrals, arrays[2]), "col", pairs))
         else:
+            known = len(arrays)
             for n, array in enumerate(list(arrays)):
-                arrays.append(lax.ppermute(array, "col", pairs))
-            known = len(arrays) // 2
+                gate = held if n == 0 else arrays[known] if n == 1 else None
+                arrays.append(lax.ppermute(after(array, gate), "col", pairs))
             spots.update({m ^ bit: tuple((n + known, q) for n, q in at) for m, at in spots.items()})
         bit //= 2
     return arrays, spots
@@ -196,8 +197,9 @@
     far = nrow // 2
     amp_up = amp_down = amplitudes
     int_up = int_down = integrals
-    waiting = []
+    waiting, held = [], None
     for s in range(1, far + 1):
+        held = (amp_up, int_down) if s == 2 else held
         last = (amp_up, amp_down, int_up, int_down)
         gate = tab if s == 2 else None
         amp_up = lax.ppermute(after(amp_up, gate), "row", ahead)
@@ -206,7 +208,7 @@
             int_up = lax.ppermute(int_up, "row", ahead)
             amp_down = lax.ppermute(amp_down, "row", behind)
         if s == min(3, far):
-            row_shards, spots = gather_cols(amplitudes, integrals, ncol)
+            row_shards, spots = gather_cols(amplitudes, integrals, ncol, held)
         waiting.append((s - 1, last[0], last[2]))
         if s >= 2:
             waiting.append((nrow - s + 1, last[1], last[3]))

time: 67.3 us -> 68.7 us (1.021)
  waiting for transfers between devices: 26.1 us -> 35.5 us
  starting transfers between devices: 26.5 us -> 18.5 us
    ppermute x4, waiting for transfers between devices: 3.98 us -> 13.5 us  [shards(): amp_up = lax.ppermute(after(amp_up, gate), 'row', ahead)]
    ppermute x4, starting transfers between devices: 5.47 us -> 1.54 us  [shards(): amp_up = lax.ppermute(after(amp_up, gate), 'row', ahead)]
    ppermute x3, starting transfers between devices: 4.66 us -> 1.15 us  [shards(): int_up = lax.ppermute(int_up, 'row', ahead)]
    ppermute x4, waiting for transfers between devices: 15.1 us -> 12.9 us  [shards(): int_down = lax.ppermute(after(int_down, gate), 'row', behind)]
    ppermute x3, waiting for transfers between devices: 1.65 us -> 3.63 us  [shards(): int_up = lax.ppermute(int_up, 'row', ahead)]
where the time goes in v6:
time: 68.7 us; the launch traced here: 68.5 us
  waiting for transfers between devices  35.5 us (52%)
  starting transfers between devices  18.5 us (27%)
  Pallas kernels  11.1 us (16%)
  local copies, waits for them, and re-layouts  3.24 us (5%)
    ppermute x4, waiting for transfers between devices, shards(): amp_up = lax.ppermute(after(amp_up, gate), 'row', ahead)  13.5 us
    ppermute x4, waiting for transfers between devices, shards(): int_down = lax.ppermute(after(int_down, gate), 'row', behind)  12.9 us
    pallas_call x3, Pallas kernels, step(): pl.pallas_call(functools.partial(step_kernel, hops, spots, ncol, nrow, sp...  7.92 us
    ppermute x4, starting transfers between devices, shards(): int_down = lax.ppermute(after(int_down, gate), 'row', behind)  7.61 us
    ppermute x3, waiting for transfers between devices, shards(): amp_down = lax.ppermute(amp_down, 'row', behind)  5.1 us
    ppermute x3, starting transfers between devices, shards(): amp_down = lax.ppermute(amp_down, 'row', behind)  4.7 us
    ppermute x3, waiting for transfers between devices, shards(): int_up = lax.ppermute(int_up, 'row', ahead)  3.63 us
    unnamed x16, local copies, waits for them, and re-layouts  3.24 us
  transfers between devices with their start and end apart: 20, of which 9 were waited for; matrix products, arithmetic and copies ran while one was open for 0% of the time, Pallas kernels for 14%

profile of v6, /device:TPU:0, one launch (start us, length us, event | category | flops | bytes accessed | tf_op | source)
XLA Modules:
  0.0 68.5 jit_solution(15522441604957059345)
XLA Ops:
  0.0 2.9 %collective-permute-start.3 = (bf16[256,768]{1,0:T(8,128)(2,1)}, bf16[256,768]{1,0:T(8,128)(2,1)S(1)}, u32[]{:S(2)}, u32[]{:S(2)}) collective-permute-start(bf16[256,768]{1,0:T(8,128)(2,1)} %refs_1_.5), channel_id=1, source_target_pairs={{8,0},{16,8},{24,16},{28,24},{20,28},{12,20},{4,12},{0,4},{9,1},{1... | collective-permute-start | bytes 1179656 | tf_op jit(solution)/shard_map/ppermute | solution.py:206
  2.9 0.1 collective-permute-start.2
  3.0 2.0 %collective-permute-start = (bf16[256,768]{1,0:T(8,128)(2,1)}, bf16[256,768]{1,0:T(8,128)(2,1)S(1)}, u32[]{:S(2)}, u32[]{:S(2)}) collective-permute-start(bf16[256,768]{1,0:T(8,128)(2,1)} %refs_0_.5), channel_id=1, source_target_pairs={{0,2},{1,3},{2,0},{3,1},{4,6},{5,7},{6,4},{7,5},{8,10},{9,11},{10,... | collective-permute-start | bytes 1179656 | tf_op jit(solution)/shard_map/ppermute | solution.py:164
  5.0 1.5 %collective-permute-start.14 = (bf16[256,768]{1,0:T(8,128)(2,1)}, bf16[256,768]{1,0:T(8,128)(2,1)S(1)}, u32[]{:S(2)}, u32[]{:S(2)}) collective-permute-start(bf16[256,768]{1,0:T(8,128)(2,1)} %refs_0_.5), channel_id=1, source_target_pairs={{8,0},{16,8},{24,16},{28,24},{20,28},{12,20},{4,12},{0,4},{9,1},{1... | collective-permute-start | bytes 1179656 | tf_op jit(solution)/shard_map/ppermute | solution.py:209
  6.5 0.5 collective-permute-start.17
  7.0 0.0 copy-start.6
  7.0 6.2 %collective-permute-done.3.refs_15_ = bf16[256,768]{1,0:T(8,128)(2,1)S(1)} collective-permute-done((bf16[256,768]{1,0:T(8,128)(2,1)}, bf16[256,768]{1,0:T(8,128)(2,1)S(1)}, u32[]{:S(2)}, u32[]{:S(2)}) %collective-permute-start.3) | collective-permute-done | bytes 393248 | tf_op jit(solution)/shard_map/ppermute | solution.py:206
  13.2 2.0 %collective-permute-done.2.refs_9_ = bf16[256,768]{1,0:T(8,128)(2,1)S(1)} collective-permute-done((bf16[256,768]{1,0:T(8,128)(2,1)}, bf16[256,768]{1,0:T(8,128)(2,1)S(1)}, u32[]{:S(2)}, u32[]{:S(2)}) %collective-permute-start.2) | collective-permute-done | bytes 393248 | tf_op jit(solution)/shard_map/ppermute | solution.py:205
  15.2 0.0 collective-permute-start.4
  15.2 0.0 copy-start.7
  15.2 0.1 pad_add_fusion.where
  15.3 0.0 copy-done.6
  15.3 0.6 copy-done.7
  15.8 3.2 %slots.1 = (s32[106]{0:T(128)S(1)}, bf16[32,128,128]{2,1,0:T(8,128)(2,1)}) custom-call(s32[2]{0:T(128)S(1)} %pad_add_fusion.where, s32[64]{0:T(128)S(1)} %copy-done.7, s32[8,64]{1,0:T(8,128)S(1)} %copy-done.6), custom_call_target="tpu_custom_call" | custom-call | tf_op jit(solution)/shard_map/slots/pallas_call | solution.py:74
  19.0 0.0 copy-start.4
  19.0 1.6 %collective-permute-start.11 = (bf16[256,768]{1,0:T(8,128)(2,1)S(1)}, bf16[256,768]{1,0:T(8,128)(2,1)S(1)}, u32[]{:S(2)}, u32[]{:S(2)}) collective-permute-start(bf16[256,768]{1,0:T(8,128)(2,1)S(1)} %collective-permute-done.3.refs_15_), channel_id=1, source_target_pairs={{8,0},{16,8},{24,16},{28,24},{20,28},{12,20},{4,12},{0,4},{9,1},{1... | collective-permute-start | bytes 1179656 | tf_op jit(solution)/shard_map/ppermute | solution.py:206
  20.7 0.0 collective-permute-done.refs_2_
  20.7 0.5 collective-permute-start.8
  21.1 0.0 collective-permute-done.14.refs_10_
  21.1 1.5 %collective-permute-start.1 = (bf16[256,768]{1,0:T(8,128)(2,1)}, bf16[256,768]{1,0:T(8,128)(2,1)S(1)}, u32[]{:S(2)}, u32[]{:S(2)}) collective-permute-start(bf16[256,768]{1,0:T(8,128)(2,1)} %refs_1_.5), channel_id=1, source_target_pairs={{0,2},{1,3},{2,0},{3,1},{4,6},{5,7},{6,4},{7,5},{8,10},{9,11},{10,... | collective-permute-start | bytes 1179656 | tf_op jit(solution)/shard_map/ppermute | solution.py:165
  22.6 0.0 collective-permute-done.17.refs_14_
  22.6 0.0 collective-permute-start.6
  22.6 0.0 collective-permute-done.4.refs_4_
  22.6 1.6 %collective-permute-start.15 = (bf16[256,768]{1,0:T(8,128)(2,1)S(1)}, bf16[256,768]{1,0:T(8,128)(2,1)S(1)}, u32[]{:S(2)}, u32[]{:S(2)}) collective-permute-start(bf16[256,768]{1,0:T(8,128)(2,1)S(1)} %collective-permute-done.14.refs_10_), channel_id=1, source_target_pairs={{8,0},{16,8},{24,16},{28,24},{20,28},{12,20},{4,12},{0,4},{9,1},{1... | collective-permute-start | bytes 1179656 | tf_op jit(solution)/shard_map/ppermute | solution.py:209
  24.3 6.7 %collective-permute-done.11.refs_17_ = bf16[256,768]{1,0:T(8,128)(2,1)S(1)} collective-permute-done((bf16[256,768]{1,0:T(8,128)(2,1)S(1)}, bf16[256,768]{1,0:T(8,128)(2,1)S(1)}, u32[]{:S(2)}, u32[]{:S(2)}) %collective-permute-start.11) | collective-permute-done | bytes 393248 | tf_op jit(solution)/shard_map/ppermute | solution.py:206
  31.0 0.2 collective-permute-start.18
  31.2 0.7 %collective-permute-done.8.refs_11_ = bf16[256,768]{1,0:T(8,128)(2,1)S(1)} collective-permute-done((bf16[256,768]{1,0:T(8,128)(2,1)S(1)}, bf16[256,768]{1,0:T(8,128)(2,1)S(1)}, u32[]{:S(2)}, u32[]{:S(2)}) %collective-permute-start.8) | collective-permute-done | bytes 393248 | tf_op jit(solution)/shard_map/ppermute | solution.py:205
  31.9 0.0 collective-permute-start.5
  31.9 0.4 collective-permute-done.1.refs_3_
  32.3 0.9 %collective-permute-start.9 = (bf16[256,768]{1,0:T(8,128)(2,1)S(1)}, bf16[256,768]{1,0:T(8,128)(2,1)S(1)}, u32[]{:S(2)}, u32[]{:S(2)}) collective-permute-start(bf16[256,768]{1,0:T(8,128)(2,1)S(1)} %collective-permute-done.8.refs_11_), channel_id=1, source_target_pairs={{0,8},{8,16},{16,24},{24,28},{28,20},{20,12},{12,4},{4,0},{1,9},{9... | collective-permute-start | bytes 1179656 | tf_op jit(solution)/shard_map/ppermute | solution.py:205
  33.2 0.0 collective-permute-done.6.refs_6_
  33.2 1.2 %collective-permute-start.12 = (bf16[256,768]{1,0:T(8,128)(2,1)S(1)}, bf16[256,768]{1,0:T(8,128)(2,1)S(1)}, u32[]{:S(2)}, u32[]{:S(2)}) collective-permute-start(bf16[256,768]{1,0:T(8,128)(2,1)S(1)} %collective-permute-done.11.refs_17_), channel_id=1, source_target_pairs={{8,0},{16,8},{24,16},{28,24},{20,28},{12,20},{4,12},{0,4},{9,1},{1... | collective-permute-start | bytes 1179656 | tf_op jit(solution)/shard_map/ppermute | solution.py:206
  34.3 5.1 %collective-permute-done.15.refs_12_ = bf16[256,768]{1,0:T(8,128)(2,1)S(1)} collective-permute-done((bf16[256,768]{1,0:T(8,128)(2,1)S(1)}, bf16[256,768]{1,0:T(8,128)(2,1)S(1)}, u32[]{:S(2)}, u32[]{:S(2)}) %collective-permute-start.15) | collective-permute-done | bytes 393248 | tf_op jit(solution)/shard_map/ppermute | solution.py:209
  39.4 0.0 collective-permute-start.7
  39.4 3.6 %collective-permute-done.18.refs_16_ = bf16[256,768]{1,0:T(8,128)(2,1)S(1)} collective-permute-done((bf16[256,768]{1,0:T(8,128)(2,1)S(1)}, bf16[256,768]{1,0:T(8,128)(2,1)S(1)}, u32[]{:S(2)}, u32[]{:S(2)}) %collective-permute-start.18) | collective-permute-done | bytes 393248 | tf_op jit(solution)/shard_map/ppermute | solution.py:208
  43.0 1.6 %collective-permute-start.16 = (bf16[256,768]{1,0:T(8,128)(2,1)S(1)}, bf16[256,768]{1,0:T(8,128)(2,1)S(1)}, u32[]{:S(2)}, u32[]{:S(2)}) collective-permute-start(bf16[256,768]{1,0:T(8,128)(2,1)S(1)} %collective-permute-done.15.refs_12_), channel_id=1, source_target_pairs={{8,0},{16,8},{24,16},{28,24},{20,28},{12,20},{4,12},{0,4},{9,1},{1... | collective-permute-start | bytes 1179656 | tf_op jit(solution)/shard_map/ppermute | solution.py:209
  44.6 0.0 collective-permute-done.5.refs_5_
  44.6 0.5 collective-permute-start.19
  45.1 6.4 %collective-permute-done.9.refs_8_ = bf16[256,768]{1,0:T(8,128)(2,1)S(1)} collective-permute-done((bf16[256,768]{1,0:T(8,128)(2,1)S(1)}, bf16[256,768]{1,0:T(8,128)(2,1)S(1)}, u32[]{:S(2)}, u32[]{:S(2)}) %collective-permute-start.9) | collective-permute-done | bytes 393248 | tf_op jit(solution)/shard_map/ppermute | solution.py:205
  51.5 0.1 collective-permute-start.10
  51.6 0.0 collective-permute-done.12.refs_11_
  51.6 1.9 %collective-permute-start.13 = (bf16[256,768]{1,0:T(8,128)(2,1)S(1)}, bf16[256,768]{1,0:T(8,128)(2,1)S(1)}, u32[]{:S(2)}, u32[]{:S(2)}) collective-permute-start(bf16[256,768]{1,0:T(8,128)(2,1)S(1)} %collective-permute-done.12.refs_11_), channel_id=1, source_target_pairs={{8,0},{16,8},{24,16},{28,24},{20,28},{12,20},{4,12},{0,4},{9,1},{1... | collective-permute-start | bytes 1179656 | tf_op jit(solution)/shard_map/ppermute | solution.py:206
  53.5 0.0 collective-permute-done.7.refs_7_
  53.5 0.0 copy-start.5
  53.5 0.0 copy-done.4
  53.5 0.7 copy-done.5
  54.2 0.0 copy-start
  54.2 1.0 %copy-done = bf16[256,768]{1,0:T(8,128)(2,1)S(1)} copy-done((bf16[256,768]{1,0:T(8,128)(2,1)S(1)}, bf16[256,768]{1,0:T(8,128)(2,1)}, u32[]{:S(2)}) %copy-start) | copy-done | bytes 393240
  55.2 0.0 copy-start.2
  55.2 1.0 %copy-done.2 = bf16[256,768]{1,0:T(8,128)(2,1)S(1)} copy-done((bf16[256,768]{1,0:T(8,128)(2,1)S(1)}, bf16[256,768]{1,0:T(8,128)(2,1)}, u32[]{:S(2)}) %copy-start.2) | copy-done | bytes 393240
  56.2 0.0 copy-start.1
  56.2 0.0 copy-start.3
  56.2 3.8 %blocks.3.refs_12_ = bf16[32,128,128]{2,1,0:T(8,128)(2,1)} custom-call(s32[106]{0:T(128)S(1)} %get-tuple-element.12.tab, f32[8]{0:T(128)S(1)} %copy-done.5, f32[8,128]{1,0:T(8,128)S(1)} %bitcast.4, bf16[256,768]{1,0:T(8,128)(2,1)S(1)} %copy-done, bf16[256,768]{1,0:T(8,128)(2,1)S(1)} %copy-done.2, ...), custom_call_target="tpu_custom_call", output_to_operand_aliasing={{}: (21, {})} | custom-call | flops 1006632960 | bytes 11796480 | tf_op jit(solution)/shard_map/blocks/pallas_call | solution.py:137
  60.0 0.0 collective-permute-done.16.refs_9_
  60.0 0.0 collective-permute-done.19.refs_10_
  60.0 0.0 copy-done.1
  60.0 0.0 copy-done.3
  60.0 2.3 %blocks.4.refs_10_ = bf16[32,128,128]{2,1,0:T(8,128)(2,1)} custom-call(s32[106]{0:T(128)S(1)} %get-tuple-element.12.tab, f32[8]{0:T(128)S(1)} %copy-done.5, f32[8,128]{1,0:T(8,128)S(1)} %bitcast.5, bf16[256,768]{1,0:T(8,128)(2,1)S(1)} %copy-done.1, bf16[256,768]{1,0:T(8,128)(2,1)S(1)} %copy-done.3, ...), custom_call_target="tpu_custom_call", output_to_operand_aliasing={{}: (15, {})} | custom-call | flops 402653184 | bytes 4718592 | tf_op jit(solution)/shard_map/blocks/pallas_call | solution.py:137
  62.3 4.3 %collective-permute-done.10.refs_8_ = bf16[256,768]{1,0:T(8,128)(2,1)S(1)} collective-permute-done((bf16[256,768]{1,0:T(8,128)(2,1)S(1)}, bf16[256,768]{1,0:T(8,128)(2,1)S(1)}, u32[]{:S(2)}, u32[]{:S(2)}) %collective-permute-start.10) | collective-permute-done | bytes 393248 | tf_op jit(solution)/shard_map/ppermute | solution.py:205
  66.6 0.0 collective-permute-done.13.refs_9_
  66.6 1.8 %blocks.5 = bf16[32,128,128]{2,1,0:T(8,128)(2,1)} custom-call(s32[106]{0:T(128)S(1)} %get-tuple-element.12.tab, f32[8]{0:T(128)S(1)} %copy-done.5, f32[8,128]{1,0:T(8,128)S(1)} %bitcast.6, bf16[256,768]{1,0:T(8,128)(2,1)S(1)} %copy-done.1, bf16[256,768]{1,0:T(8,128)(2,1)S(1)} %copy-done.3, ...), custom_call_target="tpu_custom_call", output_to_operand_aliasing={{}: (13, {})} | custom-call | flops 201326592 | bytes 2359296 | tf_op jit(solution)/shard_map/blocks/pallas_call | solution.py:137
Async XLA Ops:
  0.0 13.2 %collective-permute-start.3 = (bf16[256,768]{1,0:T(8,128)(2,1)}, bf16[256,768]{1,0:T(8,128)(2,1)S(1)}, u32[]{:S(2)}, u32[]{:S(2)}) collective-permute-start(bf16[256,768]{1,0:T(8,128)(2,1)} %refs_1_.5), channel_id=1, source_target_pairs={{8,0},{16,8},{24,16},{28,24},{20,28},{12,20},{4,12},{0,4},{9,1},{1... | collective-permute-start | bytes 1179656 | tf_op jit(solution)/shard_map/ppermute | solution.py:206
  2.9 12.2 %collective-permute-start.2 = (bf16[256,768]{1,0:T(8,128)(2,1)}, bf16[256,768]{1,0:T(8,128)(2,1)S(1)}, u32[]{:S(2)}, u32[]{:S(2)}) collective-permute-start(bf16[256,768]{1,0:T(8,128)(2,1)} %refs_0_.5), channel_id=1, source_target_pairs={{0,8},{8,16},{16,24},{24,28},{28,20},{20,12},{12,4},{4,0},{1,9},{9... | collective-permute-start | bytes 1179656 | tf_op jit(solution)/shard_map/ppermute | solution.py:205
  3.0 17.6 %collective-permute-start = (bf16[256,768]{1,0:T(8,128)(2,1)}, bf16[256,768]{1,0:T(8,128)(2,1)S(1)}, u32[]{:S(2)}, u32[]{:S(2)}) collective-permute-start(bf16[256,768]{1,0:T(8,128)(2,1)} %refs_0_.5), channel_id=1, source_target_pairs={{0,2},{1,3},{2,0},{3,1},{4,6},{5,7},{6,4},{7,5},{8,10},{9,11},{10,... | collective-permute-start | bytes 1179656 | tf_op jit(solution)/shard_map/ppermute | solution.py:164
  5.0 16.1 %collective-permute-start.14 = (bf16[256,768]{1,0:T(8,128)(2,1)}, bf16[256,768]{1,0:T(8,128)(2,1)S(1)}, u32[]{:S(2)}, u32[]{:S(2)}) collective-permute-start(bf16[256,768]{1,0:T(8,128)(2,1)} %refs_0_.5), channel_id=1, source_target_pairs={{8,0},{16,8},{24,16},{28,24},{20,28},{12,20},{4,12},{0,4},{9,1},{1... | collective-permute-start | bytes 1179656 | tf_op jit(solution)/shard_map/ppermute | solution.py:209
  6.5 16.2 %collective-permute-start.17 = (bf16[256,768]{1,0:T(8,128)(2,1)}, bf16[256,768]{1,0:T(8,128)(2,1)S(1)}, u32[]{:S(2)}, u32[]{:S(2)}) collective-permute-start(bf16[256,768]{1,0:T(8,128)(2,1)} %refs_1_.5), channel_id=1, source_target_pairs={{0,8},{8,16},{16,24},{24,28},{28,20},{20,12},{12,4},{4,0},{1,9},{9... | collective-permute-start | bytes 1179656 | tf_op jit(solution)/shard_map/ppermute | solution.py:208
  7.0 8.3 %copy-start.6 = (s32[8,64]{1,0:T(8,128)S(1)}, s32[8,64]{1,0:T(8,128)}, u32[]{:S(2)}) copy-start(s32[8,64]{1,0:T(8,128)} %mask.1) | copy-start | bytes 6148
  15.2 7.5 %collective-permute-start.4 = (bf16[256,768]{1,0:T(8,128)(2,1)}, bf16[256,768]{1,0:T(8,128)(2,1)S(1)}, u32[]{:S(2)}, u32[]{:S(2)}) collective-permute-start(bf16[256,768]{1,0:T(8,128)(2,1)} %refs_0_.5), channel_id=1, source_target_pairs={{0,1},{1,0},{2,3},{3,2},{4,5},{5,4},{6,7},{7,6},{8,9},{9,8},{10,11... | collective-permute-start | bytes 1179656 | tf_op jit(solution)/shard_map/ppermute | solution.py:170
  15.2 0.7 copy-start.7
  19.0 34.5 %copy-start.4 = (f32[1024]{0:T(1024)S(1)}, f32[1024]{0:T(1024)}, u32[]{:S(2)}) copy-start(f32[1024]{0:T(1024)} %param.10) | copy-start | bytes 12292
  19.0 12.0 %collective-permute-start.11 = (bf16[256,768]{1,0:T(8,128)(2,1)S(1)}, bf16[256,768]{1,0:T(8,128)(2,1)S(1)}, u32[]{:S(2)}, u32[]{:S(2)}) collective-permute-start(bf16[256,768]{1,0:T(8,128)(2,1)S(1)} %collective-permute-done.3.refs_15_), channel_id=1, source_target_pairs={{8,0},{16,8},{24,16},{28,24},{20,28},{12,20},{4,12},{0,4},{9,1},{1... | collective-permute-start | bytes 1179656 | tf_op jit(solution)/shard_map/ppermute | solution.py:206
  20.7 11.2 %collective-permute-start.8 = (bf16[256,768]{1,0:T(8,128)(2,1)S(1)}, bf16[256,768]{1,0:T(8,128)(2,1)S(1)}, u32[]{:S(2)}, u32[]{:S(2)}) collective-permute-start(bf16[256,768]{1,0:T(8,128)(2,1)S(1)} %collective-permute-done.2.refs_9_), channel_id=1, source_target_pairs={{0,8},{8,16},{16,24},{24,28},{28,20},{20,12},{12,4},{4,0},{1,9},{9... | collective-permute-start | bytes 1179656 | tf_op jit(solution)/shard_map/ppermute | solution.py:205
  21.1 11.2 %collective-permute-start.1 = (bf16[256,768]{1,0:T(8,128)(2,1)}, bf16[256,768]{1,0:T(8,128)(2,1)S(1)}, u32[]{:S(2)}, u32[]{:S(2)}) collective-permute-start(bf16[256,768]{1,0:T(8,128)(2,1)} %refs_1_.5), channel_id=1, source_target_pairs={{0,2},{1,3},{2,0},{3,1},{4,6},{5,7},{6,4},{7,5},{8,10},{9,11},{10,... | collective-permute-start | bytes 1179656 | tf_op jit(solution)/shard_map/ppermute | solution.py:165
  22.6 10.5 %collective-permute-start.6 = (bf16[256,768]{1,0:T(8,128)(2,1)S(1)}, bf16[256,768]{1,0:T(8,128)(2,1)S(1)}, u32[]{:S(2)}, u32[]{:S(2)}) collective-permute-start(bf16[256,768]{1,0:T(8,128)(2,1)S(1)} %collective-permute-done.refs_2_), channel_id=1, source_target_pairs={{0,1},{1,0},{2,3},{3,2},{4,5},{5,4},{6,7},{7,6},{8,9},{9,8},{10,11... | collective-permute-start | bytes 1179656 | tf_op jit(solution)/shard_map/ppermute | solution.py:170
  22.6 16.8 %collective-permute-start.15 = (bf16[256,768]{1,0:T(8,128)(2,1)S(1)}, bf16[256,768]{1,0:T(8,128)(2,1)S(1)}, u32[]{:S(2)}, u32[]{:S(2)}) collective-permute-start(bf16[256,768]{1,0:T(8,128)(2,1)S(1)} %collective-permute-done.14.refs_10_), channel_id=1, source_target_pairs={{8,0},{16,8},{24,16},{28,24},{20,28},{12,20},{4,12},{0,4},{9,1},{1... | collective-permute-start | bytes 1179656 | tf_op jit(solution)/shard_map/ppermute | solution.py:209
  31.0 12.1 %collective-permute-start.18 = (bf16[256,768]{1,0:T(8,128)(2,1)S(1)}, bf16[256,768]{1,0:T(8,128)(2,1)S(1)}, u32[]{:S(2)}, u32[]{:S(2)}) collective-permute-start(bf16[256,768]{1,0:T(8,128)(2,1)S(1)} %collective-permute-done.17.refs_14_), channel_id=1, source_target_pairs={{0,8},{8,16},{16,24},{24,28},{28,20},{20,12},{12,4},{4,0},{1,9},{9... | collective-permute-start | bytes 1179656 | tf_op jit(solution)/shard_map/ppermute | solution.py:208
  31.9 12.7 %collective-permute-start.5 = (bf16[256,768]{1,0:T(8,128)(2,1)}, bf16[256,768]{1,0:T(8,128)(2,1)S(1)}, u32[]{:S(2)}, u32[]{:S(2)}) collective-permute-start(bf16[256,768]{1,0:T(8,128)(2,1)} %refs_1_.5), channel_id=1, source_target_pairs={{0,1},{1,0},{2,3},{3,2},{4,5},{5,4},{6,7},{7,6},{8,9},{9,8},{10,11... | collective-permute-start | bytes 1179656 | tf_op jit(solution)/shard_map/ppermute | solution.py:170
  32.3 19.2 %collective-permute-start.9 = (bf16[256,768]{1,0:T(8,128)(2,1)S(1)}, bf16[256,768]{1,0:T(8,128)(2,1)S(1)}, u32[]{:S(2)}, u32[]{:S(2)}) collective-permute-start(bf16[256,768]{1,0:T(8,128)(2,1)S(1)} %collective-permute-done.8.refs_11_), channel_id=1, source_target_pairs={{0,8},{8,16},{16,24},{24,28},{28,20},{20,12},{12,4},{4,0},{1,9},{9... | collective-permute-start | bytes 1179656 | tf_op jit(solution)/shard_map/ppermute | solution.py:205
  33.2 18.4 %collective-permute-start.12 = (bf16[256,768]{1,0:T(8,128)(2,1)S(1)}, bf16[256,768]{1,0:T(8,128)(2,1)S(1)}, u32[]{:S(2)}, u32[]{:S(2)}) collective-permute-start(bf16[256,768]{1,0:T(8,128)(2,1)S(1)} %collective-permute-done.11.refs_17_), channel_id=1, source_target_pairs={{8,0},{16,8},{24,16},{28,24},{20,28},{12,20},{4,12},{0,4},{9,1},{1... | collective-permute-start | bytes 1179656 | tf_op jit(solution)/shard_map/ppermute | solution.py:206
  39.4 14.1 %collective-permute-start.7 = (bf16[256,768]{1,0:T(8,128)(2,1)S(1)}, bf16[256,768]{1,0:T(8,128)(2,1)S(1)}, u32[]{:S(2)}, u32[]{:S(2)}) collective-permute-start(bf16[256,768]{1,0:T(8,128)(2,1)S(1)} %collective-permute-done.1.refs_3_), channel_id=1, source_target_pairs={{0,1},{1,0},{2,3},{3,2},{4,5},{5,4},{6,7},{7,6},{8,9},{9,8},{10,11... | collective-permute-start | bytes 1179656 | tf_op jit(solution)/shard_map/ppermute | solution.py:170
  43.0 16.9 %collective-permute-start.16 = (bf16[256,768]{1,0:T(8,128)(2,1)S(1)}, bf16[256,768]{1,0:T(8,128)(2,1)S(1)}, u32[]{:S(2)}, u32[]{:S(2)}) collective-permute-start(bf16[256,768]{1,0:T(8,128)(2,1)S(1)} %collective-permute-done.15.refs_12_), channel_id=1, source_target_pairs={{8,0},{16,8},{24,16},{28,24},{20,28},{12,20},{4,12},{0,4},{9,1},{1... | collective-permute-start | bytes 1179656 | tf_op jit(solution)/shard_map/ppermute | solution.py:209
  44.6 15.3 %collective-permute-start.19 = (bf16[256,768]{1,0:T(8,128)(2,1)S(1)}, bf16[256,768]{1,0:T(8,128)(2,1)S(1)}, u32[]{:S(2)}, u32[]{:S(2)}) collective-permute-start(bf16[256,768]{1,0:T(8,128)(2,1)S(1)} %collective-permute-done.18.refs_16_), channel_id=1, source_target_pairs={{0,8},{8,16},{16,24},{24,28},{28,20},{20,12},{12,4},{4,0},{1,9},{9... | collective-permute-start | bytes 1179656 | tf_op jit(solution)/shard_map/ppermute | solution.py:208
  51.5 15.2 %collective-permute-start.10 = (bf16[256,768]{1,0:T(8,128)(2,1)S(1)}, bf16[256,768]{1,0:T(8,128)(2,1)S(1)}, u32[]{:S(2)}, u32[]{:S(2)}) collective-permute-start(bf16[256,768]{1,0:T(8,128)(2,1)S(1)} %collective-permute-done.9.refs_8_), channel_id=1, source_target_pairs={{0,8},{8,16},{16,24},{24,28},{28,20},{20,12},{12,4},{4,0},{1,9},{9... | collective-permute-start | bytes 1179656 | tf_op jit(solution)/shard_map/ppermute | solution.py:205
  51.6 15.0 %collective-permute-start.13 = (bf16[256,768]{1,0:T(8,128)(2,1)S(1)}, bf16[256,768]{1,0:T(8,128)(2,1)S(1)}, u32[]{:S(2)}, u32[]{:S(2)}) collective-permute-start(bf16[256,768]{1,0:T(8,128)(2,1)S(1)} %collective-permute-done.12.refs_11_), channel_id=1, source_target_pairs={{8,0},{16,8},{24,16},{28,24},{20,28},{12,20},{4,12},{0,4},{9,1},{1... | collective-permute-start | bytes 1179656 | tf_op jit(solution)/shard_map/ppermute | solution.py:206
  53.5 0.7 copy-start.5
  54.2 1.0 %copy-start = (bf16[256,768]{1,0:T(8,128)(2,1)S(1)}, bf16[256,768]{1,0:T(8,128)(2,1)}, u32[]{:S(2)}) copy-start(bf16[256,768]{1,0:T(8,128)(2,1)} %refs_0_.5) | copy-start | bytes 1179652
  55.2 1.0 %copy-start.2 = (bf16[256,768]{1,0:T(8,128)(2,1)S(1)}, bf16[256,768]{1,0:T(8,128)(2,1)}, u32[]{:S(2)}) copy-start(bf16[256,768]{1,0:T(8,128)(2,1)} %refs_1_.5) | copy-start | bytes 1179652
  56.2 3.8 %copy-start.1 = (bf16[256,768]{1,0:T(8,128)(2,1)S(1)}, bf16[256,768]{1,0:T(8,128)(2,1)}, u32[]{:S(2)}) copy-start(bf16[256,768]{1,0:T(8,128)(2,1)} %refs_0_.5) | copy-start | bytes 1179652
  56.2 3.8 %copy-start.3 = (bf16[256,768]{1,0:T(8,128)(2,1)S(1)}, bf16[256,768]{1,0:T(8,128)(2,1)}, u32[]{:S(2)}) copy-start(bf16[256,768]{1,0:T(8,128)(2,1)} %refs_1_.5) | copy-start | bytes 1179652

commit v7 on v6

--- a/solution.py
+++ b/solution.py
@@ -166,7 +166,7 @@
         else:
             known = len(arrays)
             for n, array in enumerate(list(arrays)):
-                gate = held if n == 0 else arrays[known] if n == 1 else None
+                gate = held if n == 1 else None
                 arrays.append(lax.ppermute(after(array, gate), "col", pairs))
             spots.update({m ^ bit: tuple((n + known, q) for n, q in at) for m, at in spots.items()})
         bit //= 2
@@ -199,7 +199,7 @@
     int_up = int_down = integrals
     waiting, held = [], None
     for s in range(1, far + 1):
-        held = (amp_up, int_down) if s == 2 else held
+        held = (amp_down,) if s == 2 else held
         last = (amp_up, amp_down, int_up, int_down)
         gate = tab if s == 2 else None
         amp_up = lax.ppermute(after(amp_up, gate), "row", ahead)

time: 68.7 us -> 68.8 us (level)
  starting transfers between devices: 18.5 us -> 19.5 us
  waiting for transfers between devices: 35.5 us -> 34.6 us
    ppermute x3, waiting for transfers between devices: 5.1 us -> 9.63 us  [shards(): amp_down = lax.ppermute(amp_down, 'row', behind)]
    ppermute x3, waiting for transfers between devices: 3.63 us -> 0.05 us  [shards(): int_up = lax.ppermute(int_up, 'row', ahead)]
    ppermute x4, waiting for transfers between devices: 13.5 us -> 12.7 us  [shards(): amp_up = lax.ppermute(after(amp_up, gate), 'row', ahead)]
    ppermute x4, starting transfers between devices: 1.54 us -> 2.31 us  [shards(): amp_up = lax.ppermute(after(amp_up, gate), 'row', ahead)]
    ppermute x4, waiting for transfers between devices: 12.9 us -> 12.2 us  [shards(): int_down = lax.ppermute(after(int_down, gate), 'row', behind)]
  transfers between devices with their start and end apart: 20 -> 20, of which waited for: 9 -> 7; matrix products, arithmetic and copies ran while one was open for 0% -> 0% of each run, Pallas kernels for 14% -> 14%
where the time goes in v7:
time: 68.8 us; the launch traced here: 68.6 us
  waiting for transfers between devices  34.6 us (50%)
  starting transfers between devices  19.5 us (28%)
  Pallas kernels  11.1 us (16%)
  local copies, waits for them, and re-layouts  3.24 us (5%)
    ppermute x4, waiting for transfers between devices, shards(): amp_up = lax.ppermute(after(amp_up, gate), 'row', ahead)  12.7 us
    ppermute x4, waiting for transfers between devices, shards(): int_down = lax.ppermute(after(int_down, gate), 'row', behind)  12.2 us
    ppermute x3, waiting for transfers between devices, shards(): amp_down = lax.ppermute(amp_down, 'row', behind)  9.63 us
    pallas_call x3, Pallas kernels, step(): pl.pallas_call(functools.partial(step_kernel, hops, spots, ncol, nrow, sp...  7.91 us
    ppermute x4, starting transfers between devices, shards(): int_down = lax.ppermute(after(int_down, gate), 'row', behind)  6.96 us
    ppermute x3, starting transfers between devices, shards(): amp_down = lax.ppermute(amp_down, 'row', behind)  4.81 us
    unnamed x16, local copies, waits for them, and re-layouts  3.24 us
    pallas_call x1, Pallas kernels, slot_table(): pl.pallas_call(functools.partial(table_kernel, ncol, nrow, split), in_spe...  3.16 us
  transfers between devices with their start and end apart: 20, of which 7 were waited for; matrix products, arithmetic and copies ran while one was open for 0% of the time, Pallas kernels for 14%

profile of v7, /device:TPU:0, one launch (start us, length us, event | category | flops | bytes accessed | tf_op | source)
XLA Modules:
  0.0 68.6 jit_solution(1224783556495100986)
XLA Ops:
  0.0 2.9 %collective-permute-start.11 = (bf16[256,768]{1,0:T(8,128)(2,1)}, bf16[256,768]{1,0:T(8,128)(2,1)S(1)}, u32[]{:S(2)}, u32[]{:S(2)}) collective-permute-start(bf16[256,768]{1,0:T(8,128)(2,1)} %refs_1_.5), channel_id=1, source_target_pairs={{8,0},{16,8},{24,16},{28,24},{20,28},{12,20},{4,12},{0,4},{9,1},{1... | collective-permute-start | bytes 1179656 | tf_op jit(solution)/shard_map/ppermute | solution.py:206
  2.9 0.1 collective-permute-start.7
  3.0 2.0 %collective-permute-start = (bf16[256,768]{1,0:T(8,128)(2,1)}, bf16[256,768]{1,0:T(8,128)(2,1)S(1)}, u32[]{:S(2)}, u32[]{:S(2)}) collective-permute-start(bf16[256,768]{1,0:T(8,128)(2,1)} %refs_0_.5), channel_id=1, source_target_pairs={{0,2},{1,3},{2,0},{3,1},{4,6},{5,7},{6,4},{7,5},{8,10},{9,11},{10,... | collective-permute-start | bytes 1179656 | tf_op jit(solution)/shard_map/ppermute | solution.py:164
  5.0 1.5 %collective-permute-start.3 = (bf16[256,768]{1,0:T(8,128)(2,1)}, bf16[256,768]{1,0:T(8,128)(2,1)S(1)}, u32[]{:S(2)}, u32[]{:S(2)}) collective-permute-start(bf16[256,768]{1,0:T(8,128)(2,1)} %refs_0_.5), channel_id=1, source_target_pairs={{8,0},{16,8},{24,16},{28,24},{20,28},{12,20},{4,12},{0,4},{9,1},{1... | collective-permute-start | bytes 1179656 | tf_op jit(solution)/shard_map/ppermute | solution.py:209
  6.5 0.5 collective-permute-start.17
  7.0 0.0 copy-start.6
  7.0 6.2 %collective-permute-done.11.refs_15_ = bf16[256,768]{1,0:T(8,128)(2,1)S(1)} collective-permute-done((bf16[256,768]{1,0:T(8,128)(2,1)}, bf16[256,768]{1,0:T(8,128)(2,1)S(1)}, u32[]{:S(2)}, u32[]{:S(2)}) %collective-permute-start.11) | collective-permute-done | bytes 393248 | tf_op jit(solution)/shard_map/ppermute | solution.py:206
  13.2 0.0 collective-permute-start.2
  13.2 0.0 copy-start.7
  13.2 0.1 pad_add_fusion.where
  13.3 0.0 copy-done.6
  13.3 0.6 copy-done.7
  13.8 3.2 %slots.1 = (s32[106]{0:T(128)S(1)}, bf16[32,128,128]{2,1,0:T(8,128)(2,1)}) custom-call(s32[2]{0:T(128)S(1)} %pad_add_fusion.where, s32[64]{0:T(128)S(1)} %copy-done.7, s32[8,64]{1,0:T(8,128)S(1)} %copy-done.6), custom_call_target="tpu_custom_call" | custom-call | tf_op jit(solution)/shard_map/slots/pallas_call | solution.py:74
  17.0 0.0 copy-start.4
  17.0 0.0 collective-permute-done.7.refs_9_
  17.0 2.0 %collective-permute-start.12 = (bf16[256,768]{1,0:T(8,128)(2,1)S(1)}, bf16[256,768]{1,0:T(8,128)(2,1)S(1)}, u32[]{:S(2)}, u32[]{:S(2)}) collective-permute-start(bf16[256,768]{1,0:T(8,128)(2,1)S(1)} %collective-permute-done.11.refs_15_), channel_id=1, source_target_pairs={{8,0},{16,8},{24,16},{28,24},{20,28},{12,20},{4,12},{0,4},{9,1},{1... | collective-permute-start | bytes 1179656 | tf_op jit(solution)/shard_map/ppermute | solution.py:206
  19.1 0.0 collective-permute-done.refs_2_
  19.1 0.2 collective-permute-start.8
  19.2 1.8 %collective-permute-done.3.refs_10_ = bf16[256,768]{1,0:T(8,128)(2,1)S(1)} collective-permute-done((bf16[256,768]{1,0:T(8,128)(2,1)}, bf16[256,768]{1,0:T(8,128)(2,1)S(1)}, u32[]{:S(2)}, u32[]{:S(2)}) %collective-permute-start.3) | collective-permute-done | bytes 393248 | tf_op jit(solution)/shard_map/ppermute | solution.py:209
  21.0 1.7 %collective-permute-start.1 = (bf16[256,768]{1,0:T(8,128)(2,1)}, bf16[256,768]{1,0:T(8,128)(2,1)S(1)}, u32[]{:S(2)}, u32[]{:S(2)}) collective-permute-start(bf16[256,768]{1,0:T(8,128)(2,1)} %refs_1_.5), channel_id=1, source_target_pairs={{0,2},{1,3},{2,0},{3,1},{4,6},{5,7},{6,4},{7,5},{8,10},{9,11},{10,... | collective-permute-start | bytes 1179656 | tf_op jit(solution)/shard_map/ppermute | solution.py:165
  22.7 0.0 collective-permute-done.17.refs_14_
  22.7 0.0 collective-permute-start.5
  22.7 0.0 collective-permute-done.2.refs_4_
  22.7 0.5 collective-permute-start.4
  23.2 6.0 %collective-permute-done.12.refs_17_ = bf16[256,768]{1,0:T(8,128)(2,1)S(1)} collective-permute-done((bf16[256,768]{1,0:T(8,128)(2,1)S(1)}, bf16[256,768]{1,0:T(8,128)(2,1)S(1)}, u32[]{:S(2)}, u32[]{:S(2)}) %collective-permute-start.12) | collective-permute-done | bytes 393248 | tf_op jit(solution)/shard_map/ppermute | solution.py:206
  29.2 1.7 %collective-permute-start.15 = (bf16[256,768]{1,0:T(8,128)(2,1)S(1)}, bf16[256,768]{1,0:T(8,128)(2,1)S(1)}, u32[]{:S(2)}, u32[]{:S(2)}) collective-permute-start(bf16[256,768]{1,0:T(8,128)(2,1)S(1)} %collective-permute-done.3.refs_10_), channel_id=1, source_target_pairs={{8,0},{16,8},{24,16},{28,24},{20,28},{12,20},{4,12},{0,4},{9,1},{1... | collective-permute-start | bytes 1179656 | tf_op jit(solution)/shard_map/ppermute | solution.py:209
  30.9 0.0 collective-permute-done.8.refs_11_
  30.9 0.4 collective-permute-start.18
  31.2 0.1 collective-permute-done.1.refs_3_
  31.3 1.7 %collective-permute-start.9 = (bf16[256,768]{1,0:T(8,128)(2,1)S(1)}, bf16[256,768]{1,0:T(8,128)(2,1)S(1)}, u32[]{:S(2)}, u32[]{:S(2)}) collective-permute-start(bf16[256,768]{1,0:T(8,128)(2,1)S(1)} %collective-permute-done.8.refs_11_), channel_id=1, source_target_pairs={{0,8},{8,16},{16,24},{24,28},{28,20},{20,12},{12,4},{4,0},{1,9},{9... | collective-permute-start | bytes 1179656 | tf_op jit(solution)/shard_map/ppermute | solution.py:205
  33.0 0.0 collective-permute-done.5.refs_6_
  33.0 0.3 collective-permute-start.13
  33.3 0.0 collective-permute-done.4.refs_5_
  33.3 0.0 collective-permute-start.6
  33.3 7.9 %collective-permute-done.15.refs_12_ = bf16[256,768]{1,0:T(8,128)(2,1)S(1)} collective-permute-done((bf16[256,768]{1,0:T(8,128)(2,1)S(1)}, bf16[256,768]{1,0:T(8,128)(2,1)S(1)}, u32[]{:S(2)}, u32[]{:S(2)}) %collective-permute-start.15) | collective-permute-done | bytes 393248 | tf_op jit(solution)/shard_map/ppermute | solution.py:209
  41.2 1.7 %collective-permute-start.16 = (bf16[256,768]{1,0:T(8,128)(2,1)S(1)}, bf16[256,768]{1,0:T(8,128)(2,1)S(1)}, u32[]{:S(2)}, u32[]{:S(2)}) collective-permute-start(bf16[256,768]{1,0:T(8,128)(2,1)S(1)} %collective-permute-done.15.refs_12_), channel_id=1, source_target_pairs={{8,0},{16,8},{24,16},{28,24},{20,28},{12,20},{4,12},{0,4},{9,1},{1... | collective-permute-start | bytes 1179656 | tf_op jit(solution)/shard_map/ppermute | solution.py:209
  42.8 0.0 collective-permute-done.18.refs_16_
  42.9 0.4 collective-permute-start.19
  43.3 8.1 %collective-permute-done.9.refs_8_ = bf16[256,768]{1,0:T(8,128)(2,1)S(1)} collective-permute-done((bf16[256,768]{1,0:T(8,128)(2,1)S(1)}, bf16[256,768]{1,0:T(8,128)(2,1)S(1)}, u32[]{:S(2)}, u32[]{:S(2)}) %collective-permute-start.9) | collective-permute-done | bytes 393248 | tf_op jit(solution)/shard_map/ppermute | solution.py:205
  51.3 0.4 collective-permute-start.10
  51.7 0.0 collective-permute-done.13.refs_11_
  51.7 1.7 %collective-permute-start.14 = (bf16[256,768]{1,0:T(8,128)(2,1)S(1)}, bf16[256,768]{1,0:T(8,128)(2,1)S(1)}, u32[]{:S(2)}, u32[]{:S(2)}) collective-permute-start(bf16[256,768]{1,0:T(8,128)(2,1)S(1)} %collective-permute-done.13.refs_11_), channel_id=1, source_target_pairs={{8,0},{16,8},{24,16},{28,24},{20,28},{12,20},{4,12},{0,4},{9,1},{1... | collective-permute-start | bytes 1179656 | tf_op jit(solution)/shard_map/ppermute | solution.py:206
  53.3 0.0 collective-permute-done.6.refs_7_
  53.4 0.0 copy-start.5
  53.4 0.0 copy-done.4
  53.4 0.7 copy-done.5
  54.0 0.0 copy-start
  54.0 1.0 %copy-done = bf16[256,768]{1,0:T(8,128)(2,1)S(1)} copy-done((bf16[256,768]{1,0:T(8,128)(2,1)S(1)}, bf16[256,768]{1,0:T(8,128)(2,1)}, u32[]{:S(2)}) %copy-start) | copy-done | bytes 393240
  55.0 0.0 copy-start.2
  55.0 1.0 %copy-done.2 = bf16[256,768]{1,0:T(8,128)(2,1)S(1)} copy-done((bf16[256,768]{1,0:T(8,128)(2,1)S(1)}, bf16[256,768]{1,0:T(8,128)(2,1)}, u32[]{:S(2)}) %copy-start.2) | copy-done | bytes 393240
  56.0 0.0 copy-start.1
  56.0 0.0 copy-start.3
  56.0 3.8 %blocks.3.refs_12_ = bf16[32,128,128]{2,1,0:T(8,128)(2,1)} custom-call(s32[106]{0:T(128)S(1)} %get-tuple-element.11.tab, f32[8]{0:T(128)S(1)} %copy-done.5, f32[8,128]{1,0:T(8,128)S(1)} %bitcast.4, bf16[256,768]{1,0:T(8,128)(2,1)S(1)} %copy-done, bf16[256,768]{1,0:T(8,128)(2,1)S(1)} %copy-done.2, ...), custom_call_target="tpu_custom_call", output_to_operand_aliasing={{}: (21, {})} | custom-call | flops 1006632960 | bytes 11796480 | tf_op jit(solution)/shard_map/blocks/pallas_call | solution.py:137
  59.8 0.0 collective-permute-done.16.refs_9_
  59.8 0.0 collective-permute-done.19.refs_10_
  59.8 0.0 copy-done.1
  59.8 0.0 copy-done.3
  59.8 2.3 %blocks.4.refs_10_ = bf16[32,128,128]{2,1,0:T(8,128)(2,1)} custom-call(s32[106]{0:T(128)S(1)} %get-tuple-element.11.tab, f32[8]{0:T(128)S(1)} %copy-done.5, f32[8,128]{1,0:T(8,128)S(1)} %bitcast.5, bf16[256,768]{1,0:T(8,128)(2,1)S(1)} %copy-done.1, bf16[256,768]{1,0:T(8,128)(2,1)S(1)} %copy-done.3, ...), custom_call_target="tpu_custom_call", output_to_operand_aliasing={{}: (15, {})} | custom-call | flops 402653184 | bytes 4718592 | tf_op jit(solution)/shard_map/blocks/pallas_call | solution.py:137
  62.2 4.6 %collective-permute-done.10.refs_8_ = bf16[256,768]{1,0:T(8,128)(2,1)S(1)} collective-permute-done((bf16[256,768]{1,0:T(8,128)(2,1)S(1)}, bf16[256,768]{1,0:T(8,128)(2,1)S(1)}, u32[]{:S(2)}, u32[]{:S(2)}) %collective-permute-start.10) | collective-permute-done | bytes 393248 | tf_op jit(solution)/shard_map/ppermute | solution.py:205
  66.8 0.0 collective-permute-done.14.refs_9_
  66.8 1.8 %blocks.5 = bf16[32,128,128]{2,1,0:T(8,128)(2,1)} custom-call(s32[106]{0:T(128)S(1)} %get-tuple-element.11.tab, f32[8]{0:T(128)S(1)} %copy-done.5, f32[8,128]{1,0:T(8,128)S(1)} %bitcast.6, bf16[256,768]{1,0:T(8,128)(2,1)S(1)} %copy-done.1, bf16[256,768]{1,0:T(8,128)(2,1)S(1)} %copy-done.3, ...), custom_call_target="tpu_custom_call", output_to_operand_aliasing={{}: (13, {})} | custom-call | flops 201326592 | bytes 2359296 | tf_op jit(solution)/shard_map/blocks/pallas_call | solution.py:137
Async XLA Ops:
  0.0 13.2 %collective-permute-start.11 = (bf16[256,768]{1,0:T(8,128)(2,1)}, bf16[256,768]{1,0:T(8,128)(2,1)S(1)}, u32[]{:S(2)}, u32[]{:S(2)}) collective-permute-start(bf16[256,768]{1,0:T(8,128)(2,1)} %refs_1_.5), channel_id=1, source_target_pairs={{8,0},{16,8},{24,16},{28,24},{20,28},{12,20},{4,12},{0,4},{9,1},{1... | collective-permute-start | bytes 1179656 | tf_op jit(solution)/shard_map/ppermute | solution.py:206
  2.9 14.1 %collective-permute-start.7 = (bf16[256,768]{1,0:T(8,128)(2,1)}, bf16[256,768]{1,0:T(8,128)(2,1)S(1)}, u32[]{:S(2)}, u32[]{:S(2)}) collective-permute-start(bf16[256,768]{1,0:T(8,128)(2,1)} %refs_0_.5), channel_id=1, source_target_pairs={{0,8},{8,16},{16,24},{24,28},{28,20},{20,12},{12,4},{4,0},{1,9},{9... | collective-permute-start | bytes 1179656 | tf_op jit(solution)/shard_map/ppermute | solution.py:205
  3.0 16.0 %collective-permute-start = (bf16[256,768]{1,0:T(8,128)(2,1)}, bf16[256,768]{1,0:T(8,128)(2,1)S(1)}, u32[]{:S(2)}, u32[]{:S(2)}) collective-permute-start(bf16[256,768]{1,0:T(8,128)(2,1)} %refs_0_.5), channel_id=1, source_target_pairs={{0,2},{1,3},{2,0},{3,1},{4,6},{5,7},{6,4},{7,5},{8,10},{9,11},{10,... | collective-permute-start | bytes 1179656 | tf_op jit(solution)/shard_map/ppermute | solution.py:164
  5.0 16.0 %collective-permute-start.3 = (bf16[256,768]{1,0:T(8,128)(2,1)}, bf16[256,768]{1,0:T(8,128)(2,1)S(1)}, u32[]{:S(2)}, u32[]{:S(2)}) collective-permute-start(bf16[256,768]{1,0:T(8,128)(2,1)} %refs_0_.5), channel_id=1, source_target_pairs={{8,0},{16,8},{24,16},{28,24},{20,28},{12,20},{4,12},{0,4},{9,1},{1... | collective-permute-start | bytes 1179656 | tf_op jit(solution)/shard_map/ppermute | solution.py:209
  6.5 16.2 %collective-permute-start.17 = (bf16[256,768]{1,0:T(8,128)(2,1)}, bf16[256,768]{1,0:T(8,128)(2,1)S(1)}, u32[]{:S(2)}, u32[]{:S(2)}) collective-permute-start(bf16[256,768]{1,0:T(8,128)(2,1)} %refs_1_.5), channel_id=1, source_target_pairs={{0,8},{8,16},{16,24},{24,28},{28,20},{20,12},{12,4},{4,0},{1,9},{9... | collective-permute-start | bytes 1179656 | tf_op jit(solution)/shard_map/ppermute | solution.py:208
  7.0 6.2 %copy-start.6 = (s32[8,64]{1,0:T(8,128)S(1)}, s32[8,64]{1,0:T(8,128)}, u32[]{:S(2)}) copy-start(s32[8,64]{1,0:T(8,128)} %mask.1) | copy-start | bytes 6148
  13.2 9.5 %collective-permute-start.2 = (bf16[256,768]{1,0:T(8,128)(2,1)}, bf16[256,768]{1,0:T(8,128)(2,1)S(1)}, u32[]{:S(2)}, u32[]{:S(2)}) collective-permute-start(bf16[256,768]{1,0:T(8,128)(2,1)} %refs_0_.5), channel_id=1, source_target_pairs={{0,1},{1,0},{2,3},{3,2},{4,5},{5,4},{6,7},{7,6},{8,9},{9,8},{10,11... | collective-permute-start | bytes 1179656 | tf_op jit(solution)/shard_map/ppermute | solution.py:170
  13.2 0.7 copy-start.7
  17.0 36.4 %copy-start.4 = (f32[1024]{0:T(1024)S(1)}, f32[1024]{0:T(1024)}, u32[]{:S(2)}) copy-start(f32[1024]{0:T(1024)} %param.10) | copy-start | bytes 12292
  17.0 12.2 %collective-permute-start.12 = (bf16[256,768]{1,0:T(8,128)(2,1)S(1)}, bf16[256,768]{1,0:T(8,128)(2,1)S(1)}, u32[]{:S(2)}, u32[]{:S(2)}) collective-permute-start(bf16[256,768]{1,0:T(8,128)(2,1)S(1)} %collective-permute-done.11.refs_15_), channel_id=1, source_target_pairs={{8,0},{16,8},{24,16},{28,24},{20,28},{12,20},{4,12},{0,4},{9,1},{1... | collective-permute-start | bytes 1179656 | tf_op jit(solution)/shard_map/ppermute | solution.py:206
  19.1 11.8 %collective-permute-start.8 = (bf16[256,768]{1,0:T(8,128)(2,1)S(1)}, bf16[256,768]{1,0:T(8,128)(2,1)S(1)}, u32[]{:S(2)}, u32[]{:S(2)}) collective-permute-start(bf16[256,768]{1,0:T(8,128)(2,1)S(1)} %collective-permute-done.7.refs_9_), channel_id=1, source_target_pairs={{0,8},{8,16},{16,24},{24,28},{28,20},{20,12},{12,4},{4,0},{1,9},{9... | collective-permute-start | bytes 1179656 | tf_op jit(solution)/shard_map/ppermute | solution.py:205
  21.0 10.3 %collective-permute-start.1 = (bf16[256,768]{1,0:T(8,128)(2,1)}, bf16[256,768]{1,0:T(8,128)(2,1)S(1)}, u32[]{:S(2)}, u32[]{:S(2)}) collective-permute-start(bf16[256,768]{1,0:T(8,128)(2,1)} %refs_1_.5), channel_id=1, source_target_pairs={{0,2},{1,3},{2,0},{3,1},{4,6},{5,7},{6,4},{7,5},{8,10},{9,11},{10,... | collective-permute-start | bytes 1179656 | tf_op jit(solution)/shard_map/ppermute | solution.py:165
  22.7 10.3 %collective-permute-start.5 = (bf16[256,768]{1,0:T(8,128)(2,1)S(1)}, bf16[256,768]{1,0:T(8,128)(2,1)S(1)}, u32[]{:S(2)}, u32[]{:S(2)}) collective-permute-start(bf16[256,768]{1,0:T(8,128)(2,1)S(1)} %collective-permute-done.refs_2_), channel_id=1, source_target_pairs={{0,1},{1,0},{2,3},{3,2},{4,5},{5,4},{6,7},{7,6},{8,9},{9,8},{10,11... | collective-permute-start | bytes 1179656 | tf_op jit(solution)/shard_map/ppermute | solution.py:170
  22.7 10.6 %collective-permute-start.4 = (bf16[256,768]{1,0:T(8,128)(2,1)}, bf16[256,768]{1,0:T(8,128)(2,1)S(1)}, u32[]{:S(2)}, u32[]{:S(2)}) collective-permute-start(bf16[256,768]{1,0:T(8,128)(2,1)} %refs_1_.5), channel_id=1, source_target_pairs={{0,1},{1,0},{2,3},{3,2},{4,5},{5,4},{6,7},{7,6},{8,9},{9,8},{10,11... | collective-permute-start | bytes 1179656 | tf_op jit(solution)/shard_map/ppermute | solution.py:170
  29.2 12.0 %collective-permute-start.15 = (bf16[256,768]{1,0:T(8,128)(2,1)S(1)}, bf16[256,768]{1,0:T(8,128)(2,1)S(1)}, u32[]{:S(2)}, u32[]{:S(2)}) collective-permute-start(bf16[256,768]{1,0:T(8,128)(2,1)S(1)} %collective-permute-done.3.refs_10_), channel_id=1, source_target_pairs={{8,0},{16,8},{24,16},{28,24},{20,28},{12,20},{4,12},{0,4},{9,1},{1... | collective-permute-start | bytes 1179656 | tf_op jit(solution)/shard_map/ppermute | solution.py:209
  30.9 12.0 %collective-permute-start.18 = (bf16[256,768]{1,0:T(8,128)(2,1)S(1)}, bf16[256,768]{1,0:T(8,128)(2,1)S(1)}, u32[]{:S(2)}, u32[]{:S(2)}) collective-permute-start(bf16[256,768]{1,0:T(8,128)(2,1)S(1)} %collective-permute-done.17.refs_14_), channel_id=1, source_target_pairs={{0,8},{8,16},{16,24},{24,28},{28,20},{20,12},{12,4},{4,0},{1,9},{9... | collective-permute-start | bytes 1179656 | tf_op jit(solution)/shard_map/ppermute | solution.py:208
  31.3 20.0 %collective-permute-start.9 = (bf16[256,768]{1,0:T(8,128)(2,1)S(1)}, bf16[256,768]{1,0:T(8,128)(2,1)S(1)}, u32[]{:S(2)}, u32[]{:S(2)}) collective-permute-start(bf16[256,768]{1,0:T(8,128)(2,1)S(1)} %collective-permute-done.8.refs_11_), channel_id=1, source_target_pairs={{0,8},{8,16},{16,24},{24,28},{28,20},{20,12},{12,4},{4,0},{1,9},{9... | collective-permute-start | bytes 1179656 | tf_op jit(solution)/shard_map/ppermute | solution.py:205
  33.0 18.7 %collective-permute-start.13 = (bf16[256,768]{1,0:T(8,128)(2,1)S(1)}, bf16[256,768]{1,0:T(8,128)(2,1)S(1)}, u32[]{:S(2)}, u32[]{:S(2)}) collective-permute-start(bf16[256,768]{1,0:T(8,128)(2,1)S(1)} %collective-permute-done.12.refs_17_), channel_id=1, source_target_pairs={{8,0},{16,8},{24,16},{28,24},{20,28},{12,20},{4,12},{0,4},{9,1},{1... | collective-permute-start | bytes 1179656 | tf_op jit(solution)/shard_map/ppermute | solution.py:206
  33.3 20.0 %collective-permute-start.6 = (bf16[256,768]{1,0:T(8,128)(2,1)S(1)}, bf16[256,768]{1,0:T(8,128)(2,1)S(1)}, u32[]{:S(2)}, u32[]{:S(2)}) collective-permute-start(bf16[256,768]{1,0:T(8,128)(2,1)S(1)} %collective-permute-done.1.refs_3_), channel_id=1, source_target_pairs={{0,1},{1,0},{2,3},{3,2},{4,5},{5,4},{6,7},{7,6},{8,9},{9,8},{10,11... | collective-permute-start | bytes 1179656 | tf_op jit(solution)/shard_map/ppermute | solution.py:170
  41.2 18.6 %collective-permute-start.16 = (bf16[256,768]{1,0:T(8,128)(2,1)S(1)}, bf16[256,768]{1,0:T(8,128)(2,1)S(1)}, u32[]{:S(2)}, u32[]{:S(2)}) collective-permute-start(bf16[256,768]{1,0:T(8,128)(2,1)S(1)} %collective-permute-done.15.refs_12_), channel_id=1, source_target_pairs={{8,0},{16,8},{24,16},{28,24},{20,28},{12,20},{4,12},{0,4},{9,1},{1... | collective-permute-start | bytes 1179656 | tf_op jit(solution)/shard_map/ppermute | solution.py:209
  42.9 16.9 %collective-permute-start.19 = (bf16[256,768]{1,0:T(8,128)(2,1)S(1)}, bf16[256,768]{1,0:T(8,128)(2,1)S(1)}, u32[]{:S(2)}, u32[]{:S(2)}) collective-permute-start(bf16[256,768]{1,0:T(8,128)(2,1)S(1)} %collective-permute-done.18.refs_16_), channel_id=1, source_target_pairs={{0,8},{8,16},{16,24},{24,28},{28,20},{20,12},{12,4},{4,0},{1,9},{9... | collective-permute-start | bytes 1179656 | tf_op jit(solution)/shard_map/ppermute | solution.py:208
  51.3 15.5 %collective-permute-start.10 = (bf16[256,768]{1,0:T(8,128)(2,1)S(1)}, bf16[256,768]{1,0:T(8,128)(2,1)S(1)}, u32[]{:S(2)}, u32[]{:S(2)}) collective-permute-start(bf16[256,768]{1,0:T(8,128)(2,1)S(1)} %collective-permute-done.9.refs_8_), channel_id=1, source_target_pairs={{0,8},{8,16},{16,24},{24,28},{28,20},{20,12},{12,4},{4,0},{1,9},{9... | collective-permute-start | bytes 1179656 | tf_op jit(solution)/shard_map/ppermute | solution.py:205
  51.7 15.1 %collective-permute-start.14 = (bf16[256,768]{1,0:T(8,128)(2,1)S(1)}, bf16[256,768]{1,0:T(8,128)(2,1)S(1)}, u32[]{:S(2)}, u32[]{:S(2)}) collective-permute-start(bf16[256,768]{1,0:T(8,128)(2,1)S(1)} %collective-permute-done.13.refs_11_), channel_id=1, source_target_pairs={{8,0},{16,8},{24,16},{28,24},{20,28},{12,20},{4,12},{0,4},{9,1},{1... | collective-permute-start | bytes 1179656 | tf_op jit(solution)/shard_map/ppermute | solution.py:206
  53.4 0.7 copy-start.5
  54.0 1.0 %copy-start = (bf16[256,768]{1,0:T(8,128)(2,1)S(1)}, bf16[256,768]{1,0:T(8,128)(2,1)}, u32[]{:S(2)}) copy-start(bf16[256,768]{1,0:T(8,128)(2,1)} %refs_0_.5) | copy-start | bytes 1179652
  55.0 1.0 %copy-start.2 = (bf16[256,768]{1,0:T(8,128)(2,1)S(1)}, bf16[256,768]{1,0:T(8,128)(2,1)}, u32[]{:S(2)}) copy-start(bf16[256,768]{1,0:T(8,128)(2,1)} %refs_1_.5) | copy-start | bytes 1179652
  56.0 3.8 %copy-start.1 = (bf16[256,768]{1,0:T(8,128)(2,1)S(1)}, bf16[256,768]{1,0:T(8,128)(2,1)}, u32[]{:S(2)}) copy-start(bf16[256,768]{1,0:T(8,128)(2,1)} %refs_0_.5) | copy-start | bytes 1179652
  56.0 3.8 %copy-start.3 = (bf16[256,768]{1,0:T(8,128)(2,1)S(1)}, bf16[256,768]{1,0:T(8,128)(2,1)}, u32[]{:S(2)}) copy-start(bf16[256,768]{1,0:T(8,128)(2,1)} %refs_1_.5) | copy-start | bytes 1179652

commit v8 on v5

--- a/solution.py
+++ b/solution.py
@@ -199,7 +199,7 @@
     waiting = []
     for s in range(1, far + 1):
         last = (amp_up, amp_down, int_up, int_down)
-        gate = tab if s == 2 else None
+        gate = tab if s == 3 else None
         amp_up = lax.ppermute(after(amp_up, gate), "row", ahead)
         int_down = lax.ppermute(after(int_down, gate), "row", behind)
         if s < nrow - s:

time: 67.3 us -> 68.9 us (1.024)
  waiting for transfers between devices: 26.1 us -> 35.8 us
  starting transfers between devices: 26.5 us -> 17.7 us
    ppermute x1, waiting for transfers between devices: 0.01 us -> 5.27 us  [gather_cols(): arrays.append(lax.ppermute(amplitudes, 'col', pairs))]
    ppermute x3, waiting for transfers between devices: 5.29 us -> 10.5 us  [shards(): amp_down = lax.ppermute(amp_down, 'row', behind)]
    ppermute x4, starting transfers between devices: 5.47 us -> 2.14 us  [shards(): amp_up = lax.ppermute(after(amp_up, gate), 'row', ahead)]
    ppermute x3, starting transfers between devices: 4.66 us -> 1.6 us  [shards(): int_up = lax.ppermute(int_up, 'row', ahead)]
    ppermute x4, waiting for transfers between devices: 3.98 us -> 1.24 us  [shards(): amp_up = lax.ppermute(after(amp_up, gate), 'row', ahead)]
    ppermute x4, starting transfers between devices: 7.67 us -> 6.02 us  [shards(): int_down = lax.ppermute(after(int_down, gate), 'row', behind)]
    ppermute x4, waiting for transfers between devices: 15.1 us -> 16.6 us  [shards(): int_down = lax.ppermute(after(int_down, gate), 'row', behind)]
    ppermute x1, starting transfers between devices: 1.52 us -> 0.51 us  [gather_cols(): arrays.append(lax.ppermute(after(integrals, arrays[2]), 'col', pairs))]
  transfers between devices with their start and end apart: 20 -> 20, of which waited for: 9 -> 10; matrix products, arithmetic and copies ran while one was open for 0% -> 0% of each run, Pallas kernels for 14% -> 14%
where the time goes in v8:
time: 68.9 us; the launch traced here: 68.7 us
  waiting for transfers between devices  35.8 us (52%)
  starting transfers between devices  17.7 us (26%)
  Pallas kernels  11.7 us (17%)
  local copies, waits for them, and re-layouts  3.24 us (5%)
    ppermute x4, waiting for transfers between devices, shards(): int_down = lax.ppermute(after(int_down, gate), 'row', behind)  16.6 us
    ppermute x3, waiting for transfers between devices, shards(): amp_down = lax.ppermute(amp_down, 'row', behind)  10.5 us
    pallas_call x3, Pallas kernels, step(): pl.pallas_call(functools.partial(step_kernel, hops, spots, ncol, nrow, sp...  8.58 us
    ppermute x4, starting transfers between devices, shards(): int_down = lax.ppermute(after(int_down, gate), 'row', behind)  6.02 us
    ppermute x1, waiting for transfers between devices, gather_cols(): arrays.append(lax.ppermute(amplitudes, 'col', pairs))  5.27 us
    ppermute x3, starting transfers between devices, shards(): amp_down = lax.ppermute(amp_down, 'row', behind)  4.47 us
    unnamed x16, local copies, waits for them, and re-layouts  3.24 us
    pallas_call x1, Pallas kernels, slot_table(): pl.pallas_call(functools.partial(table_kernel, ncol, nrow, split), in_spe...  3.16 us
  transfers between devices with their start and end apart: 20, of which 10 were waited for; matrix products, arithmetic and copies ran while one was open for 0% of the time, Pallas kernels for 14%

profile of v8, /device:TPU:0, one launch (start us, length us, event | category | flops | bytes accessed | tf_op | source)
XLA Modules:
  0.0 68.7 jit_solution(7930104853187892094)
XLA Ops:
  0.0 3.0 %collective-permute-start = (bf16[256,768]{1,0:T(8,128)(2,1)}, bf16[256,768]{1,0:T(8,128)(2,1)S(1)}, u32[]{:S(2)}, u32[]{:S(2)}) collective-permute-start(bf16[256,768]{1,0:T(8,128)(2,1)} %refs_0_.5), channel_id=1, source_target_pairs={{0,2},{1,3},{2,0},{3,1},{4,6},{5,7},{6,4},{7,5},{8,10},{9,11},{10,... | collective-permute-start | bytes 1179656 | tf_op jit(solution)/shard_map/ppermute | solution.py:164
  3.0 1.5 %collective-permute-start.10 = (bf16[256,768]{1,0:T(8,128)(2,1)}, bf16[256,768]{1,0:T(8,128)(2,1)S(1)}, u32[]{:S(2)}, u32[]{:S(2)}) collective-permute-start(bf16[256,768]{1,0:T(8,128)(2,1)} %refs_1_.5), channel_id=1, source_target_pairs={{8,0},{16,8},{24,16},{28,24},{20,28},{12,20},{4,12},{0,4},{9,1},{1... | collective-permute-start | bytes 1179656 | tf_op jit(solution)/shard_map/ppermute | solution.py:204
  4.5 0.5 collective-permute-start.6
  5.0 1.5 %collective-permute-start.14 = (bf16[256,768]{1,0:T(8,128)(2,1)}, bf16[256,768]{1,0:T(8,128)(2,1)S(1)}, u32[]{:S(2)}, u32[]{:S(2)}) collective-permute-start(bf16[256,768]{1,0:T(8,128)(2,1)} %refs_0_.5), channel_id=1, source_target_pairs={{8,0},{16,8},{24,16},{28,24},{20,28},{12,20},{4,12},{0,4},{9,1},{1... | collective-permute-start | bytes 1179656 | tf_op jit(solution)/shard_map/ppermute | solution.py:207
  6.5 0.5 collective-permute-start.17
  7.0 5.3 %collective-permute-done.refs_2_ = bf16[256,768]{1,0:T(8,128)(2,1)S(1)} collective-permute-done((bf16[256,768]{1,0:T(8,128)(2,1)}, bf16[256,768]{1,0:T(8,128)(2,1)S(1)}, u32[]{:S(2)}, u32[]{:S(2)}) %collective-permute-start) | collective-permute-done | bytes 393248 | tf_op jit(solution)/shard_map/ppermute | solution.py:164
  12.3 0.0 collective-permute-start.2
  12.3 2.9 %collective-permute-done.10.refs_15_ = bf16[256,768]{1,0:T(8,128)(2,1)S(1)} collective-permute-done((bf16[256,768]{1,0:T(8,128)(2,1)}, bf16[256,768]{1,0:T(8,128)(2,1)S(1)}, u32[]{:S(2)}, u32[]{:S(2)}) %collective-permute-start.10) | collective-permute-done | bytes 393248 | tf_op jit(solution)/shard_map/ppermute | solution.py:204
  15.2 1.5 %collective-permute-start.11 = (bf16[256,768]{1,0:T(8,128)(2,1)S(1)}, bf16[256,768]{1,0:T(8,128)(2,1)}, u32[]{:S(2)}, u32[]{:S(2)}) collective-permute-start(bf16[256,768]{1,0:T(8,128)(2,1)S(1)} %collective-permute-done.10.refs_15_), channel_id=1, source_target_pairs={{8,0},{16,8},{24,16},{28,24},{20,28},{12,20},{4,12},{0,4},{9,1},{1... | collective-permute-start | bytes 1179656 | tf_op jit(solution)/shard_map/ppermute | solution.py:204
  16.7 0.0 collective-permute-done.6.refs_9_
  16.7 0.5 collective-permute-start.7
  17.3 6.4 %collective-permute-done.14.refs_10_ = bf16[256,768]{1,0:T(8,128)(2,1)S(1)} collective-permute-done((bf16[256,768]{1,0:T(8,128)(2,1)}, bf16[256,768]{1,0:T(8,128)(2,1)S(1)}, u32[]{:S(2)}, u32[]{:S(2)}) %collective-permute-start.14) | collective-permute-done | bytes 393248 | tf_op jit(solution)/shard_map/ppermute | solution.py:207
  23.6 0.0 collective-permute-start.3
  23.6 1.5 %collective-permute-done.17.refs_14_ = bf16[256,768]{1,0:T(8,128)(2,1)S(1)} collective-permute-done((bf16[256,768]{1,0:T(8,128)(2,1)}, bf16[256,768]{1,0:T(8,128)(2,1)S(1)}, u32[]{:S(2)}, u32[]{:S(2)}) %collective-permute-start.17) | collective-permute-done | bytes 393248 | tf_op jit(solution)/shard_map/ppermute | solution.py:206
  25.2 0.5 collective-permute-start.1
  25.7 0.0 collective-permute-done.2.refs_4_
  25.7 0.0 collective-permute-start.4
  25.7 0.0 copy-start.6
  25.7 5.0 %collective-permute-done.11.refs_17_ = bf16[256,768]{1,0:T(8,128)(2,1)} collective-permute-done((bf16[256,768]{1,0:T(8,128)(2,1)S(1)}, bf16[256,768]{1,0:T(8,128)(2,1)}, u32[]{:S(2)}, u32[]{:S(2)}) %collective-permute-start.11) | collective-permute-done | bytes 393248 | tf_op jit(solution)/shard_map/ppermute | solution.py:204
  30.7 1.5 %collective-permute-start.15 = (bf16[256,768]{1,0:T(8,128)(2,1)S(1)}, bf16[256,768]{1,0:T(8,128)(2,1)S(1)}, u32[]{:S(2)}, u32[]{:S(2)}) collective-permute-start(bf16[256,768]{1,0:T(8,128)(2,1)S(1)} %collective-permute-done.14.refs_10_), channel_id=1, source_target_pairs={{8,0},{16,8},{24,16},{28,24},{20,28},{12,20},{4,12},{0,4},{9,1},{1... | collective-permute-start | bytes 1179656 | tf_op jit(solution)/shard_map/ppermute | solution.py:207
  32.2 0.0 collective-permute-done.7.refs_11_
  32.2 0.5 collective-permute-start.18
  32.7 0.0 copy-start.7
  32.7 0.1 pad_add_fusion.where
  32.8 0.0 copy-done.6
  32.8 0.6 copy-done.7
  33.4 3.2 %slots.1 = (s32[106]{0:T(128)S(1)}, bf16[32,128,128]{2,1,0:T(8,128)(2,1)}) custom-call(s32[2]{0:T(128)S(1)} %pad_add_fusion.where, s32[64]{0:T(128)S(1)} %copy-done.7, s32[8,64]{1,0:T(8,128)S(1)} %copy-done.6), custom_call_target="tpu_custom_call" | custom-call | tf_op jit(solution)/shard_map/slots/pallas_call | solution.py:74
  36.6 0.0 copy-start.4
  36.6 0.0 collective-permute-done.3.refs_5_
  36.6 1.5 %collective-permute-start.12 = (bf16[256,768]{1,0:T(8,128)(2,1)}, bf16[256,768]{1,0:T(8,128)(2,1)S(1)}, u32[]{:S(2)}, u32[]{:S(2)}) collective-permute-start(bf16[256,768]{1,0:T(8,128)(2,1)} %collective-permute-done.11.refs_17_), channel_id=1, source_target_pairs={{8,0},{16,8},{24,16},{28,24},{20,28},{12,20},{4,12},{0,4},{9,1},{1... | collective-permute-start | bytes 1179656 | tf_op jit(solution)/shard_map/ppermute | solution.py:204
  38.1 0.0 collective-permute-done.1.refs_3_
  38.1 0.5 collective-permute-start.8
  38.7 0.0 collective-permute-done.4.refs_6_
  38.7 0.0 collective-permute-start.5
  38.7 4.1 %collective-permute-done.15.refs_12_ = bf16[256,768]{1,0:T(8,128)(2,1)S(1)} collective-permute-done((bf16[256,768]{1,0:T(8,128)(2,1)S(1)}, bf16[256,768]{1,0:T(8,128)(2,1)S(1)}, u32[]{:S(2)}, u32[]{:S(2)}) %collective-permute-start.15) | collective-permute-done | bytes 393248 | tf_op jit(solution)/shard_map/ppermute | solution.py:207
  42.8 1.5 %collective-permute-start.16 = (bf16[256,768]{1,0:T(8,128)(2,1)S(1)}, bf16[256,768]{1,0:T(8,128)(2,1)S(1)}, u32[]{:S(2)}, u32[]{:S(2)}) collective-permute-start(bf16[256,768]{1,0:T(8,128)(2,1)S(1)} %collective-permute-done.15.refs_12_), channel_id=1, source_target_pairs={{8,0},{16,8},{24,16},{28,24},{20,28},{12,20},{4,12},{0,4},{9,1},{1... | collective-permute-start | bytes 1179656 | tf_op jit(solution)/shard_map/ppermute | solution.py:207
  44.3 0.0 collective-permute-done.18.refs_16_
  44.3 0.5 collective-permute-start.19
  44.8 6.4 %collective-permute-done.12.refs_11_ = bf16[256,768]{1,0:T(8,128)(2,1)S(1)} collective-permute-done((bf16[256,768]{1,0:T(8,128)(2,1)}, bf16[256,768]{1,0:T(8,128)(2,1)S(1)}, u32[]{:S(2)}, u32[]{:S(2)}) %collective-permute-start.12) | collective-permute-done | bytes 393248 | tf_op jit(solution)/shard_map/ppermute | solution.py:204
  51.2 1.5 %collective-permute-start.13 = (bf16[256,768]{1,0:T(8,128)(2,1)S(1)}, bf16[256,768]{1,0:T(8,128)(2,1)S(1)}, u32[]{:S(2)}, u32[]{:S(2)}) collective-permute-start(bf16[256,768]{1,0:T(8,128)(2,1)S(1)} %collective-permute-done.12.refs_11_), channel_id=1, source_target_pairs={{8,0},{16,8},{24,16},{28,24},{20,28},{12,20},{4,12},{0,4},{9,1},{1... | collective-permute-start | bytes 1179656 | tf_op jit(solution)/shard_map/ppermute | solution.py:204
  52.7 0.0 collective-permute-done.8.refs_8_
  52.7 0.5 collective-permute-start.9
  53.2 0.0 collective-permute-done.5.refs_7_
  53.2 0.0 copy-start.5
  53.2 0.0 copy-done.4
  53.2 0.7 copy-done.5
  53.9 0.0 copy-start
  53.9 1.0 %copy-done = bf16[256,768]{1,0:T(8,128)(2,1)S(1)} copy-done((bf16[256,768]{1,0:T(8,128)(2,1)S(1)}, bf16[256,768]{1,0:T(8,128)(2,1)}, u32[]{:S(2)}) %copy-start) | copy-done | bytes 393240
  54.9 0.0 copy-start.2
  54.9 1.0 %copy-done.2 = bf16[256,768]{1,0:T(8,128)(2,1)S(1)} copy-done((bf16[256,768]{1,0:T(8,128)(2,1)S(1)}, bf16[256,768]{1,0:T(8,128)(2,1)}, u32[]{:S(2)}) %copy-start.2) | copy-done | bytes 393240
  55.9 0.0 copy-start.1
  55.9 0.0 copy-start.3
  55.9 4.5 %blocks.3.refs_12_ = bf16[32,128,128]{2,1,0:T(8,128)(2,1)} custom-call(s32[106]{0:T(128)S(1)} %get-tuple-element.10.tab, f32[8]{0:T(128)S(1)} %copy-done.5, f32[8,128]{1,0:T(8,128)S(1)} %bitcast.4, bf16[256,768]{1,0:T(8,128)(2,1)S(1)} %copy-done, bf16[256,768]{1,0:T(8,128)(2,1)S(1)} %copy-done.2, ...), custom_call_target="tpu_custom_call", output_to_operand_aliasing={{}: (21, {})} | custom-call | flops 1006632960 | bytes 11796480 | tf_op jit(solution)/shard_map/blocks/pallas_call | solution.py:137
  60.3 0.0 collective-permute-done.16.refs_9_
  60.3 0.8 %collective-permute-done.19.refs_10_ = bf16[256,768]{1,0:T(8,128)(2,1)S(1)} collective-permute-done((bf16[256,768]{1,0:T(8,128)(2,1)S(1)}, bf16[256,768]{1,0:T(8,128)(2,1)S(1)}, u32[]{:S(2)}, u32[]{:S(2)}) %collective-permute-start.19) | collective-permute-done | bytes 393248 | tf_op jit(solution)/shard_map/ppermute | solution.py:206
  61.1 0.0 copy-done.1
  61.1 0.0 copy-done.3
  61.1 2.3 %blocks.4.refs_10_ = bf16[32,128,128]{2,1,0:T(8,128)(2,1)} custom-call(s32[106]{0:T(128)S(1)} %get-tuple-element.10.tab, f32[8]{0:T(128)S(1)} %copy-done.5, f32[8,128]{1,0:T(8,128)S(1)} %bitcast.5, bf16[256,768]{1,0:T(8,128)(2,1)S(1)} %copy-done.1, bf16[256,768]{1,0:T(8,128)(2,1)S(1)} %copy-done.3, ...), custom_call_target="tpu_custom_call", output_to_operand_aliasing={{}: (15, {})} | custom-call | flops 402653184 | bytes 4718592 | tf_op jit(solution)/shard_map/blocks/pallas_call | solution.py:137
  63.4 2.2 %collective-permute-done.13.refs_9_ = bf16[256,768]{1,0:T(8,128)(2,1)S(1)} collective-permute-done((bf16[256,768]{1,0:T(8,128)(2,1)S(1)}, bf16[256,768]{1,0:T(8,128)(2,1)S(1)}, u32[]{:S(2)}, u32[]{:S(2)}) %collective-permute-start.13) | collective-permute-done | bytes 393248 | tf_op jit(solution)/shard_map/ppermute | solution.py:204
  65.7 1.2 %collective-permute-done.9.refs_8_ = bf16[256,768]{1,0:T(8,128)(2,1)S(1)} collective-permute-done((bf16[256,768]{1,0:T(8,128)(2,1)S(1)}, bf16[256,768]{1,0:T(8,128)(2,1)S(1)}, u32[]{:S(2)}, u32[]{:S(2)}) %collective-permute-start.9) | collective-permute-done | bytes 393248 | tf_op jit(solution)/shard_map/ppermute | solution.py:203
  66.9 1.8 %blocks.5 = bf16[32,128,128]{2,1,0:T(8,128)(2,1)} custom-call(s32[106]{0:T(128)S(1)} %get-tuple-element.10.tab, f32[8]{0:T(128)S(1)} %copy-done.5, f32[8,128]{1,0:T(8,128)S(1)} %bitcast.6, bf16[256,768]{1,0:T(8,128)(2,1)S(1)} %copy-done.1, bf16[256,768]{1,0:T(8,128)(2,1)S(1)} %copy-done.3, ...), custom_call_target="tpu_custom_call", output_to_operand_aliasing={{}: (13, {})} | custom-call | flops 201326592 | bytes 2359296 | tf_op jit(solution)/shard_map/blocks/pallas_call | solution.py:137
Async XLA Ops:
  0.0 12.3 %collective-permute-start = (bf16[256,768]{1,0:T(8,128)(2,1)}, bf16[256,768]{1,0:T(8,128)(2,1)S(1)}, u32[]{:S(2)}, u32[]{:S(2)}) collective-permute-start(bf16[256,768]{1,0:T(8,128)(2,1)} %refs_0_.5), channel_id=1, source_target_pairs={{0,2},{1,3},{2,0},{3,1},{4,6},{5,7},{6,4},{7,5},{8,10},{9,11},{10,... | collective-permute-start | bytes 1179656 | tf_op jit(solution)/shard_map/ppermute | solution.py:164
  3.0 12.2 %collective-permute-start.10 = (bf16[256,768]{1,0:T(8,128)(2,1)}, bf16[256,768]{1,0:T(8,128)(2,1)S(1)}, u32[]{:S(2)}, u32[]{:S(2)}) collective-permute-start(bf16[256,768]{1,0:T(8,128)(2,1)} %refs_1_.5), channel_id=1, source_target_pairs={{8,0},{16,8},{24,16},{28,24},{20,28},{12,20},{4,12},{0,4},{9,1},{1... | collective-permute-start | bytes 1179656 | tf_op jit(solution)/shard_map/ppermute | solution.py:204
  4.5 12.3 %collective-permute-start.6 = (bf16[256,768]{1,0:T(8,128)(2,1)}, bf16[256,768]{1,0:T(8,128)(2,1)S(1)}, u32[]{:S(2)}, u32[]{:S(2)}) collective-permute-start(bf16[256,768]{1,0:T(8,128)(2,1)} %refs_0_.5), channel_id=1, source_target_pairs={{0,8},{8,16},{16,24},{24,28},{28,20},{20,12},{12,4},{4,0},{1,9},{9... | collective-permute-start | bytes 1179656 | tf_op jit(solution)/shard_map/ppermute | solution.py:203
  5.0 18.6 %collective-permute-start.14 = (bf16[256,768]{1,0:T(8,128)(2,1)}, bf16[256,768]{1,0:T(8,128)(2,1)S(1)}, u32[]{:S(2)}, u32[]{:S(2)}) collective-permute-start(bf16[256,768]{1,0:T(8,128)(2,1)} %refs_0_.5), channel_id=1, source_target_pairs={{8,0},{16,8},{24,16},{28,24},{20,28},{12,20},{4,12},{0,4},{9,1},{1... | collective-permute-start | bytes 1179656 | tf_op jit(solution)/shard_map/ppermute | solution.py:207
  6.5 18.7 %collective-permute-start.17 = (bf16[256,768]{1,0:T(8,128)(2,1)}, bf16[256,768]{1,0:T(8,128)(2,1)S(1)}, u32[]{:S(2)}, u32[]{:S(2)}) collective-permute-start(bf16[256,768]{1,0:T(8,128)(2,1)} %refs_1_.5), channel_id=1, source_target_pairs={{0,8},{8,16},{16,24},{24,28},{28,20},{20,12},{12,4},{4,0},{1,9},{9... | collective-permute-start | bytes 1179656 | tf_op jit(solution)/shard_map/ppermute | solution.py:206
  12.3 13.4 %collective-permute-start.2 = (bf16[256,768]{1,0:T(8,128)(2,1)}, bf16[256,768]{1,0:T(8,128)(2,1)S(1)}, u32[]{:S(2)}, u32[]{:S(2)}) collective-permute-start(bf16[256,768]{1,0:T(8,128)(2,1)} %refs_0_.5), channel_id=1, source_target_pairs={{0,1},{1,0},{2,3},{3,2},{4,5},{5,4},{6,7},{7,6},{8,9},{9,8},{10,11... | collective-permute-start | bytes 1179656 | tf_op jit(solution)/shard_map/ppermute | solution.py:168
  15.2 15.5 %collective-permute-start.11 = (bf16[256,768]{1,0:T(8,128)(2,1)S(1)}, bf16[256,768]{1,0:T(8,128)(2,1)}, u32[]{:S(2)}, u32[]{:S(2)}) collective-permute-start(bf16[256,768]{1,0:T(8,128)(2,1)S(1)} %collective-permute-done.10.refs_15_), channel_id=1, source_target_pairs={{8,0},{16,8},{24,16},{28,24},{20,28},{12,20},{4,12},{0,4},{9,1},{1... | collective-permute-start | bytes 1179656 | tf_op jit(solution)/shard_map/ppermute | solution.py:204
  16.7 15.5 %collective-permute-start.7 = (bf16[256,768]{1,0:T(8,128)(2,1)S(1)}, bf16[256,768]{1,0:T(8,128)(2,1)}, u32[]{:S(2)}, u32[]{:S(2)}) collective-permute-start(bf16[256,768]{1,0:T(8,128)(2,1)S(1)} %collective-permute-done.6.refs_9_), channel_id=1, source_target_pairs={{0,8},{8,16},{16,24},{24,28},{28,20},{20,12},{12,4},{4,0},{1,9},{9... | collective-permute-start | bytes 1179656 | tf_op jit(solution)/shard_map/ppermute | solution.py:203
  23.6 12.9 %collective-permute-start.3 = (bf16[256,768]{1,0:T(8,128)(2,1)}, bf16[256,768]{1,0:T(8,128)(2,1)S(1)}, u32[]{:S(2)}, u32[]{:S(2)}) collective-permute-start(bf16[256,768]{1,0:T(8,128)(2,1)} %refs_1_.5), channel_id=1, source_target_pairs={{0,1},{1,0},{2,3},{3,2},{4,5},{5,4},{6,7},{7,6},{8,9},{9,8},{10,11... | collective-permute-start | bytes 1179656 | tf_op jit(solution)/shard_map/ppermute | solution.py:168
  25.2 13.0 %collective-permute-start.1 = (bf16[256,768]{1,0:T(8,128)(2,1)}, bf16[256,768]{1,0:T(8,128)(2,1)S(1)}, u32[]{:S(2)}, u32[]{:S(2)}) collective-permute-start(bf16[256,768]{1,0:T(8,128)(2,1)} %refs_1_.5), channel_id=1, source_target_pairs={{0,2},{1,3},{2,0},{3,1},{4,6},{5,7},{6,4},{7,5},{8,10},{9,11},{10,... | collective-permute-start | bytes 1179656 | tf_op jit(solution)/shard_map/ppermute | solution.py:165
  25.7 13.0 %collective-permute-start.4 = (bf16[256,768]{1,0:T(8,128)(2,1)S(1)}, bf16[256,768]{1,0:T(8,128)(2,1)S(1)}, u32[]{:S(2)}, u32[]{:S(2)}) collective-permute-start(bf16[256,768]{1,0:T(8,128)(2,1)S(1)} %collective-permute-done.refs_2_), channel_id=1, source_target_pairs={{0,1},{1,0},{2,3},{3,2},{4,5},{5,4},{6,7},{7,6},{8,9},{9,8},{10,11... | collective-permute-start | bytes 1179656 | tf_op jit(solution)/shard_map/ppermute | solution.py:168
  25.7 7.2 %copy-start.6 = (s32[8,64]{1,0:T(8,128)S(1)}, s32[8,64]{1,0:T(8,128)}, u32[]{:S(2)}) copy-start(s32[8,64]{1,0:T(8,128)} %mask.1) | copy-start | bytes 6148
  30.7 12.1 %collective-permute-start.15 = (bf16[256,768]{1,0:T(8,128)(2,1)S(1)}, bf16[256,768]{1,0:T(8,128)(2,1)S(1)}, u32[]{:S(2)}, u32[]{:S(2)}) collective-permute-start(bf16[256,768]{1,0:T(8,128)(2,1)S(1)} %collective-permute-done.14.refs_10_), channel_id=1, source_target_pairs={{8,0},{16,8},{24,16},{28,24},{20,28},{12,20},{4,12},{0,4},{9,1},{1... | collective-permute-start | bytes 1179656 | tf_op jit(solution)/shard_map/ppermute | solution.py:207
  32.2 12.1 %collective-permute-start.18 = (bf16[256,768]{1,0:T(8,128)(2,1)S(1)}, bf16[256,768]{1,0:T(8,128)(2,1)S(1)}, u32[]{:S(2)}, u32[]{:S(2)}) collective-permute-start(bf16[256,768]{1,0:T(8,128)(2,1)S(1)} %collective-permute-done.17.refs_14_), channel_id=1, source_target_pairs={{0,8},{8,16},{16,24},{24,28},{28,20},{20,12},{12,4},{4,0},{1,9},{9... | collective-permute-start | bytes 1179656 | tf_op jit(solution)/shard_map/ppermute | solution.py:206
  32.7 0.7 copy-start.7
  36.6 16.7 %copy-start.4 = (f32[1024]{0:T(1024)S(1)}, f32[1024]{0:T(1024)}, u32[]{:S(2)}) copy-start(f32[1024]{0:T(1024)} %param.10) | copy-start | bytes 12292
  36.6 14.6 %collective-permute-start.12 = (bf16[256,768]{1,0:T(8,128)(2,1)}, bf16[256,768]{1,0:T(8,128)(2,1)S(1)}, u32[]{:S(2)}, u32[]{:S(2)}) collective-permute-start(bf16[256,768]{1,0:T(8,128)(2,1)} %collective-permute-done.11.refs_17_), channel_id=1, source_target_pairs={{8,0},{16,8},{24,16},{28,24},{20,28},{12,20},{4,12},{0,4},{9,1},{1... | collective-permute-start | bytes 1179656 | tf_op jit(solution)/shard_map/ppermute | solution.py:204
  38.1 14.5 %collective-permute-start.8 = (bf16[256,768]{1,0:T(8,128)(2,1)}, bf16[256,768]{1,0:T(8,128)(2,1)S(1)}, u32[]{:S(2)}, u32[]{:S(2)}) collective-permute-start(bf16[256,768]{1,0:T(8,128)(2,1)} %collective-permute-done.7.refs_11_), channel_id=1, source_target_pairs={{0,8},{8,16},{16,24},{24,28},{28,20},{20,12},{12,4},{4,0},{1,9},{9... | collective-permute-start | bytes 1179656 | tf_op jit(solution)/shard_map/ppermute | solution.py:203
  38.7 14.5 %collective-permute-start.5 = (bf16[256,768]{1,0:T(8,128)(2,1)S(1)}, bf16[256,768]{1,0:T(8,128)(2,1)S(1)}, u32[]{:S(2)}, u32[]{:S(2)}) collective-permute-start(bf16[256,768]{1,0:T(8,128)(2,1)S(1)} %collective-permute-done.1.refs_3_), channel_id=1, source_target_pairs={{0,1},{1,0},{2,3},{3,2},{4,5},{5,4},{6,7},{7,6},{8,9},{9,8},{10,11... | collective-permute-start | bytes 1179656 | tf_op jit(solution)/shard_map/ppermute | solution.py:168
  42.8 17.6 %collective-permute-start.16 = (bf16[256,768]{1,0:T(8,128)(2,1)S(1)}, bf16[256,768]{1,0:T(8,128)(2,1)S(1)}, u32[]{:S(2)}, u32[]{:S(2)}) collective-permute-start(bf16[256,768]{1,0:T(8,128)(2,1)S(1)} %collective-permute-done.15.refs_12_), channel_id=1, source_target_pairs={{8,0},{16,8},{24,16},{28,24},{20,28},{12,20},{4,12},{0,4},{9,1},{1... | collective-permute-start | bytes 1179656 | tf_op jit(solution)/shard_map/ppermute | solution.py:207
  44.3 16.9 %collective-permute-start.19 = (bf16[256,768]{1,0:T(8,128)(2,1)S(1)}, bf16[256,768]{1,0:T(8,128)(2,1)S(1)}, u32[]{:S(2)}, u32[]{:S(2)}) collective-permute-start(bf16[256,768]{1,0:T(8,128)(2,1)S(1)} %collective-permute-done.18.refs_16_), channel_id=1, source_target_pairs={{0,8},{8,16},{16,24},{24,28},{28,20},{20,12},{12,4},{4,0},{1,9},{9... | collective-permute-start | bytes 1179656 | tf_op jit(solution)/shard_map/ppermute | solution.py:206
  51.2 14.5 %collective-permute-start.13 = (bf16[256,768]{1,0:T(8,128)(2,1)S(1)}, bf16[256,768]{1,0:T(8,128)(2,1)S(1)}, u32[]{:S(2)}, u32[]{:S(2)}) collective-permute-start(bf16[256,768]{1,0:T(8,128)(2,1)S(1)} %collective-permute-done.12.refs_11_), channel_id=1, source_target_pairs={{8,0},{16,8},{24,16},{28,24},{20,28},{12,20},{4,12},{0,4},{9,1},{1... | collective-permute-start | bytes 1179656 | tf_op jit(solution)/shard_map/ppermute | solution.py:204
  52.7 14.2 %collective-permute-start.9 = (bf16[256,768]{1,0:T(8,128)(2,1)S(1)}, bf16[256,768]{1,0:T(8,128)(2,1)S(1)}, u32[]{:S(2)}, u32[]{:S(2)}) collective-permute-start(bf16[256,768]{1,0:T(8,128)(2,1)S(1)} %collective-permute-done.8.refs_8_), channel_id=1, source_target_pairs={{0,8},{8,16},{16,24},{24,28},{28,20},{20,12},{12,4},{4,0},{1,9},{9... | collective-permute-start | bytes 1179656 | tf_op jit(solution)/shard_map/ppermute | solution.py:203
  53.2 0.7 copy-start.5
  53.9 1.0 %copy-start = (bf16[256,768]{1,0:T(8,128)(2,1)S(1)}, bf16[256,768]{1,0:T(8,128)(2,1)}, u32[]{:S(2)}) copy-start(bf16[256,768]{1,0:T(8,128)(2,1)} %refs_0_.5) | copy-start | bytes 1179652
  54.9 1.0 %copy-start.2 = (bf16[256,768]{1,0:T(8,128)(2,1)S(1)}, bf16[256,768]{1,0:T(8,128)(2,1)}, u32[]{:S(2)}) copy-start(bf16[256,768]{1,0:T(8,128)(2,1)} %refs_1_.5) | copy-start | bytes 1179652
  55.9 5.2 %copy-start.1 = (bf16[256,768]{1,0:T(8,128)(2,1)S(1)}, bf16[256,768]{1,0:T(8,128)(2,1)}, u32[]{:S(2)}) copy-start(bf16[256,768]{1,0:T(8,128)(2,1)} %refs_0_.5) | copy-start | bytes 1179652
  55.9 5.2 %copy-start.3 = (bf16[256,768]{1,0:T(8,128)(2,1)S(1)}, bf16[256,768]{1,0:T(8,128)(2,1)}, u32[]{:S(2)}) copy-start(bf16[256,768]{1,0:T(8,128)(2,1)} %refs_1_.5) | copy-start | bytes 1179652
